TPU v7x, 128 devices: a whole 4x4x4 slice. The times are simulated.
128 devices in a mesh: branch: 16 (over z_hi, x, core), head: 8 (over z_lo, y).
Axes of the slice: x: 4, y: 4, z: 4 (z_hi: 2, z_lo: 2; z = z_hi * 2 + z_lo), core: 2. Of those that a mesh axis runs over, the one named last changes fastest.
Arguments:
- queries: bfloat16 [4, 16, 256, 8192], P(None, 'branch', None, 'head'), may hold values from -96 to 96
- key_rows: bfloat16 [4, 16, 256, 1024], P(None, 'branch', None, 'head'), may hold values from -4 to 4
- value_rows: bfloat16 [4, 16, 256, 1024], P(None, 'branch', None, 'head'), may hold values from -5 to 5
- cotangent: bfloat16 [4, 16, 256, 8192], P(None, 'branch', None, 'head'), may hold values from -6 to 6
- out_weight: bfloat16 [8192, 8192], P('head'), may hold values from -0.0625 to 0.0625
- parents: int32 [3, 16], replicated, may hold values from 0 to 15
- seg_len: int32 [4, 16], replicated, may hold values from 128 to 256, as said below
Outputs:
- query_grad: bfloat16 [4, 16, 256, 8192], P(None, 'branch', None, 'head')
- key_grad: bfloat16 [4, 16, 256, 1024], P(None, 'branch', None, 'head')
- value_grad: bfloat16 [4, 16, 256, 1024], P(None, 'branch', None, 'head')
Inputs may be any that keep to these rules, and one draw needn't show every extreme that they name: parents[m, j] is the node of level m that node j of level m + 1 continues; a node may have many children or none. `seg_len`: some node uses all 256 slots in every draw.
All inputs are finite; a program needn't handle non-finite values.
Results may differ from a plain program's by a relative error of at most 0.015.
Values may be sent and summed in bfloat16 or wider, within the bound.
No kernel may reach another device: no remote copies, remote signals or barrier semaphores. Data moves between devices by JAX's collectives and lax.ppermute only.
A program may use at most 192 MiB of HBM per device.

v0:
```python
import functools

import jax
import jax.numpy as jnp
from jax import lax
from jax.experimental import pallas as pl
from jax.experimental.pallas import tpu as pltpu
from jax.sharding import Mesh, PartitionSpec as P

HD = 128
SEG = 256
GROUP = 8
BATCH = 4
LEVELS = 4
NODES = 16
FEATURES = 1024
HALF = 4096
PIECE = 128
ROWS = 256
SCALE = 1.0 / HD**0.5
EXP2_SCALE = SCALE * 1.4426950408889634
MASKED = -1e30
NT = (((1,), (1,)), ((), ()))
PARAMS = pltpu.CompilerParams(vmem_limit_bytes=56 * 2**20)
SMALL = pltpu.CompilerParams(vmem_limit_bytes=16 * 2**20)
ANY = pl.BlockSpec(memory_space=pl.ANY)
AXES = ("zh", "x", "c")
ALT = [(0, 3), (1, 2), (2, 1), (3, 0)]
SWAP = [(0, 1), (1, 0)]
UP = [(i, (i + 1) % 4) for i in range(4)]
DOWN = [(i, (i + 3) % 4) for i in range(4)]
ACROSS = [(i, (i + 2) % 4) for i in range(4)]


def cost(flops, size, exps=0):
    return pl.CostEstimate(flops=flops, bytes_accessed=size, transcendentals=exps)


def node_id(meta):
    return (meta[0] * 4 + meta[1]) * 2 + meta[2]


def ancestor(parents, node, level, target):
    for m in reversed(range(target, level)):
        node = parents[m * NODES + node]
    return node


def relative(meta, node):
    zh = lax.rem(node // 8 + meta[0], 2)
    x = lax.rem(node // 2, 4)
    c = lax.rem(lax.rem(node, 2) + meta[2], 2)
    return c, x, zh


def prepare_kernel(meta, weight, keys, values, cot, *refs):
    pieces, (rows, upper, lower), refs = refs[:4], refs[4:7], refs[7:]
    held, kept, passed, in_sems, out_sems = refs

    def piece(step):
        row = pl.multiple_of((meta[2] * 4 + step) * PIECE, PIECE)
        column = pl.multiple_of((1 - meta[3]) * HALF, HALF)
        return weight.at[pl.ds(row, PIECE), pl.ds(column, HALF)]

    moves = [
        (keys.at[0 : LEVELS - 1, 0], kept.at[0], rows.at[0]),
        (values.at[0 : LEVELS - 1, 0], kept.at[1], rows.at[1]),
        (cot.at[2:4, 0], passed.at[0], upper),
        (cot.at[0:2, 0], passed.at[1], lower),
    ] + [(piece(i), held.at[i], pieces[i]) for i in range(4)]
    reads = [
        pltpu.make_async_copy(source, middle, in_sems.at[i])
        for i, (source, middle, _) in enumerate(moves)
    ]
    writes = [
        pltpu.make_async_copy(middle, target, out_sems.at[i])
        for i, (_, middle, target) in enumerate(moves)
    ]
    for read in reads:
        read.start()
    for read, write in zip(reads, writes):
        read.wait()
        write.start()
    for write in writes:
        write.wait()


def prepare(meta, weight, keys, values, cot):
    return pl.pallas_call(
        prepare_kernel,
        grid_spec=pltpu.PrefetchScalarGridSpec(
            num_scalar_prefetch=1,
            grid=(),
            in_specs=[ANY] * 4,
            out_specs=[ANY] * 7,
            scratch_shapes=[
                pltpu.VMEM((4, PIECE, HALF), jnp.bfloat16),
                pltpu.VMEM((2, LEVELS - 1, SEG, HD), jnp.bfloat16),
                pltpu.VMEM((2, 2, SEG, FEATURES), jnp.bfloat16),
                pltpu.SemaphoreType.DMA((8,)),
                pltpu.SemaphoreType.DMA((8,)),
            ],
        ),
        out_shape=[
            *[jax.ShapeDtypeStruct((PIECE, HALF), jnp.bfloat16)] * 4,
            jax.ShapeDtypeStruct((2, LEVELS - 1, SEG, HD), jnp.bfloat16),
            jax.ShapeDtypeStruct((2, SEG, FEATURES), jnp.bfloat16),
            jax.ShapeDtypeStruct((2, SEG, FEATURES), jnp.bfloat16),
        ],
        compiler_params=PARAMS,
        cost_estimate=cost(0, 12 * 2**20),
        name="prepare",
    )(meta, weight, keys, values, cot)


def tie_kernel(*refs):
    pass


def tie(*arrays):
    return pl.pallas_call(
        tie_kernel,
        in_specs=[ANY] * len(arrays),
        out_specs=[ANY] * len(arrays),
        out_shape=[jax.ShapeDtypeStruct(a.shape, a.dtype) for a in arrays],
        input_output_aliases={i: i for i in range(len(arrays))},
        name="tie",
    )(*arrays)


def early_kernel(meta, own, above, below, w0, w1, w2, out):
    total = sum(
        lax.dot_general(
            cot[...].reshape(2 * SEG, FEATURES), w[...], NT, preferred_element_type=jnp.float32
        )
        for cot, w in ((own, w0), (above, w1), (below, w2))
    )
    out[...] = total.reshape(out.shape)


def late_kernel(meta, across, weight, early, token, *outs):
    total = lax.dot_general(
        across[...].reshape(2 * SEG, FEATURES),
        weight[...],
        NT,
        preferred_element_type=jnp.float32,
    )
    for i in range(2):
        outs[i][...] = early[i] + total[i * SEG : (i + 1) * SEG]


def feature_spec(step):
    def index(n, meta):
        return n, meta[3] * 4 + lax.rem(meta[4] + step, 4)

    return pl.BlockSpec((ROWS, FEATURES), index)


def early_product(meta, own, above, below, weight):
    whole = pl.BlockSpec((2, SEG, FEATURES), lambda n, *_: (0, 0, 0))
    return pl.pallas_call(
        early_kernel,
        grid_spec=pltpu.PrefetchScalarGridSpec(
            num_scalar_prefetch=1,
            grid=(4,),
            in_specs=[whole] * 3 + [feature_spec(step) for step in (0, 1, 3)],
            out_specs=pl.BlockSpec((2, SEG, ROWS), lambda n, *_: (0, 0, n)),
        ),
        out_shape=jax.ShapeDtypeStruct((2, SEG, FEATURES), jnp.float32),
        compiler_params=PARAMS,
        cost_estimate=cost(3 * SEG * 1024 * HALF, 2 * 1024 * HALF),
        name="early_product",
    )(meta, own, above, below, weight, weight, weight)


def late_product(meta, across, weight, early, token):
    whole = pl.BlockSpec((2, SEG, FEATURES), lambda n, *_: (0, 0, 0))
    return pl.pallas_call(
        late_kernel,
        grid_spec=pltpu.PrefetchScalarGridSpec(
            num_scalar_prefetch=1,
            grid=(4,),
            in_specs=[
                whole,
                feature_spec(2),
                pl.BlockSpec((2, SEG, ROWS), lambda n, *_: (0, 0, n)),
                ANY,
            ],
            out_specs=[pl.BlockSpec((SEG, ROWS), lambda n, *_: (0, n))] * 2,
        ),
        out_shape=[jax.ShapeDtypeStruct((SEG, FEATURES), jnp.float32)] * 2,
        compiler_params=PARAMS,
        cost_estimate=cost(SEG * 1024 * HALF, 2 * 1024 * 1024),
        name="late_product",
    )(meta, across, weight, early, token)


def product_kernel(partner, meta, own, above, below, across, *refs):
    count = 8 if partner else 1
    weights, refs = refs[:count], refs[count:]
    outs, (cots, held, cot_sems, sems) = refs[1:3], refs[3:]
    step = pl.program_id(0)

    def place(source, offset, sem, rows):
        column = pl.multiple_of(lax.rem(meta[4] + offset, 4) * FEATURES, FEATURES)
        target = cots.at[rows, pl.ds(column, FEATURES)]
        return pltpu.make_async_copy(source, target, cot_sems.at[sem])

    def block(q):
        if partner:
            return [
                pltpu.make_async_copy(
                    weights[2 * q + i], held.at[q, pl.ds(i * PIECE, PIECE)], sems.at[q, i]
                )
                for i in range(2)
            ]
        column = pl.multiple_of(meta[3] * HALF, HALF)
        source = weights[0].at[q * ROWS : (q + 1) * ROWS, pl.ds(column, HALF)]
        return [pltpu.make_async_copy(source, held.at[q], sems.at[q, 0])]

    upper, lower = pl.ds(0, SEG), pl.ds(SEG, SEG)
    moves = [
        place(part.at[i], offset, 2 * k + i, rows)
        for k, (part, offset) in enumerate(((own, 0), (above, 1), (below, 3), (across, 2)))
        for i, rows in enumerate((upper, lower))
    ]
    blocks = [block(q) for q in range(4)]

    @pl.when(step == 0)
    def _():
        for move in moves + blocks[0]:
            move.start()
        for move in moves + blocks[0]:
            move.wait()
        for move in blocks[1] + blocks[2] + blocks[3]:
            move.start()

    for q in range(1, 4):

        @pl.when(step == q)
        def _(q=q):
            for move in blocks[q]:
                move.wait()

    total = lax.dot_general(cots[...], held[step], NT, preferred_element_type=jnp.float32)
    for i in range(2):
        part = total[i * SEG : (i + 1) * SEG]
        if partner:
            outs[i][0] = part[:, :PIECE].astype(jnp.bfloat16)
            outs[i][1] = part[:, PIECE:].astype(jnp.bfloat16)
        else:
            outs[i][...] = part


def product(partner, meta, cots, weights, token):
    if partner:
        out_shape = [jax.ShapeDtypeStruct((8, SEG, PIECE), jnp.bfloat16)] * 2
        out_specs = [pl.BlockSpec((2, SEG, PIECE), lambda q, *_: (q, 0, 0))] * 2
    else:
        out_shape = [jax.ShapeDtypeStruct((SEG, FEATURES), jnp.float32)] * 2
        out_specs = [pl.BlockSpec((SEG, ROWS), lambda q, *_: (0, q))] * 2
    return pl.pallas_call(
        functools.partial(product_kernel, partner),
        grid_spec=pltpu.PrefetchScalarGridSpec(
            num_scalar_prefetch=1,
            grid=(4,),
            in_specs=[ANY] * (5 + len(weights)),
            out_specs=out_specs,
            scratch_shapes=[
                pltpu.VMEM((2 * SEG, HALF), jnp.bfloat16),
                pltpu.VMEM((4, ROWS, HALF), jnp.bfloat16),
                pltpu.SemaphoreType.DMA((8,)),
                pltpu.SemaphoreType.DMA((4, 2)),
            ],
        ),
        out_shape=out_shape,
        compiler_params=PARAMS,
        cost_estimate=cost(4 * SEG * 1024 * HALF, 2 * 1024 * HALF + 8 * SEG * 1024),
        name="partner_product" if partner else "own_product",
    )(meta, *cots, *weights, token)


def pair_index(level, target):
    return level * (level - 1) // 2 + target


PAIRS = [(level, m) for level in range(LEVELS) for m in range(level)]


def probs_kernel(meta, parents, lengths, query, own_key, mine, other, *refs):
    outs, picked, sems = refs[1:5], refs[5], refs[6]
    me = node_id(meta)

    @pl.when(pl.program_id(0) == 0)
    def _():
        copies = []
        for i, (level, m) in enumerate(PAIRS):
            c, x, zh = relative(meta, ancestor(parents, me, level, m))
            for part in range(2):
                pair = [
                    pltpu.make_async_copy(
                        source.at[x, zh, part, m], picked.at[i, part], sems.at[i, part]
                    )
                    for source in (mine, other)
                ]
                pl.when(c == 0)(pair[0].start)
                pl.when(c == 1)(pair[1].start)
                copies.append(pair[0])
        for copy in copies:
            copy.wait()

    for level in reversed(range(LEVELS)):
        q = jnp.concatenate(
            [query[level, 0, :, i * HD : (i + 1) * HD] for i in range(BATCH)], axis=0
        )
        blocks = []
        for m in range(level + 1):
            key = picked[pair_index(level, m), 0] if m < level else own_key[level, 0]
            s = lax.dot_general(key, q, NT, preferred_element_type=jnp.float32)
            length = lengths[m * NODES + ancestor(parents, me, level, m)]
            position = lax.broadcasted_iota(jnp.int32, s.shape, 0)
            allowed = position < length
            if m == level:
                asked = lax.broadcasted_iota(jnp.int32, s.shape, 1) & (SEG - 1)
                allowed = allowed & (position <= asked)
            blocks.append(jnp.where(allowed, s, MASKED))
        top = functools.reduce(
            jnp.maximum, [jnp.max(s, axis=0, keepdims=True) for s in blocks]
        )
        exps = [jnp.exp2((s - top) * EXP2_SCALE) for s in blocks]
        inverse = 1.0 / sum(jnp.sum(e, axis=0, keepdims=True) for e in exps)
        for m in range(level + 1):
            outs[level][0, m * SEG : (m + 1) * SEG] = (exps[m] * inverse).astype(jnp.bfloat16)


def probs(meta, parents, lengths, queries, key_rows, mine, other, token):
    width = BATCH * HD
    counts = [(level + 1) * SEG for level in range(LEVELS)]
    total = sum(counts)
    return pl.pallas_call(
        probs_kernel,
        grid_spec=pltpu.PrefetchScalarGridSpec(
            num_scalar_prefetch=3,
            grid=(GROUP // BATCH,),
            in_specs=[
                pl.BlockSpec((LEVELS, 1, SEG, width), lambda h, *_: (0, 0, 0, h)),
                pl.BlockSpec((LEVELS, 1, SEG, HD), lambda h, *_: (0, 0, 0, 0)),
                ANY,
                ANY,
                ANY,
            ],
            out_specs=[
                pl.BlockSpec((1, count, BATCH * SEG), lambda h, *_: (h, 0, 0))
                for count in counts
            ]
            + [pl.BlockSpec((len(PAIRS), 2, SEG, HD), lambda h, *_: (0, 0, 0, 0))],
            scratch_shapes=[pltpu.SemaphoreType.DMA((len(PAIRS), 2))],
        ),
        out_shape=[
            jax.ShapeDtypeStruct((GROUP // BATCH, count, BATCH * SEG), jnp.bfloat16)
            for count in counts
        ]
        + [jax.ShapeDtypeStruct((len(PAIRS), 2, SEG, HD), jnp.bfloat16)],
        compiler_params=PARAMS,
        cost_estimate=cost(
            2 * GROUP * total * SEG * HD, 2 * GROUP * total * SEG, GROUP * total * SEG
        ),
        name="probs",
    )(meta, parents, lengths, queries, key_rows, mine, other, token)


def backward_kernel(
    level, meta, parents, lengths, probs_ref, query, own, partner, own_key, own_value, *refs
):
    if level:
        picked, refs = refs[0], refs[1:]
    refs = refs[2:]
    if level:
        query_out, own_out, ancestor_out, flipped, key_total, value_total = refs
    else:
        query_out, own_out, flipped, key_total, value_total = refs
    first = pair_index(level, 0)
    step = pl.program_id(0)
    blocks = [slice(m * SEG, (m + 1) * SEG) for m in range(level + 1)]

    @pl.when(step == 0)
    def _():
        key_total[...] = jnp.zeros_like(key_total)
        value_total[...] = jnp.zeros_like(value_total)
        for m in range(level + 1):
            key = picked[first + m, 0] if m < level else own_key[0, 0]
            flipped[:, blocks[m]] = key.astype(jnp.float32).T.astype(jnp.bfloat16)

    length = lengths[level * NODES + node_id(meta)]
    valid = lax.broadcasted_iota(jnp.int32, (SEG, HD), 0) < length
    heads = []
    for i in range(BATCH):
        head = step * BATCH + i
        piece = lax.rem(step + meta[2], 2) * 4 + i
        total = own[:, i * HD : (i + 1) * HD] + partner[piece].astype(jnp.float32)
        heads.append(jnp.where(valid, total, 0.0).astype(jnp.bfloat16))
    dout = jnp.concatenate(heads, axis=0)
    q = jnp.concatenate([query[0, 0, :, i * HD : (i + 1) * HD] for i in range(BATCH)], axis=0)
    value = jnp.concatenate(
        [picked[first + m, 1] for m in range(level)] + [own_value[0, 0]], axis=0
    )
    narrow = probs_ref[0]
    wide = narrow.astype(jnp.float32)
    grads = lax.dot_general(value, dout, NT, preferred_element_type=jnp.float32)
    delta = jnp.sum(wide * grads, axis=0, keepdims=True)
    scores = (wide * (grads - delta)).astype(jnp.bfloat16)
    key_total[...] += jnp.dot(scores, q, preferred_element_type=jnp.float32)
    value_total[...] += jnp.dot(narrow, dout, preferred_element_type=jnp.float32)
    query_total = jnp.dot(flipped[...], scores, preferred_element_type=jnp.float32) * SCALE
    for i in range(BATCH):
        part = query_total[:, i * SEG : (i + 1) * SEG]
        query_out[0, 0, :, i * HD : (i + 1) * HD] = part.T.astype(jnp.bfloat16)

    @pl.when(step == GROUP // BATCH - 1)
    def _():
        for m in range(level):
            ancestor_out[m, 0] = (key_total[blocks[m]] * SCALE).astype(jnp.bfloat16)
            ancestor_out[m, 1] = value_total[blocks[m]].astype(jnp.bfloat16)
        own_out[0] = key_total[blocks[level]] * SCALE
        own_out[1] = value_total[blocks[level]]


def backward(
    level, meta, parents, lengths, probabilities, queries, own, partner, key_rows, value_rows,
    picked, query_grad, token,
):
    count = (level + 1) * SEG
    width = BATCH * HD
    out_specs = [
        pl.BlockSpec((1, 1, SEG, width), lambda h, *_: (level, 0, 0, h)),
        pl.BlockSpec((2, SEG, HD), lambda h, *_: (0, 0, 0)),
    ]
    out_shape = [
        jax.ShapeDtypeStruct(queries.shape, jnp.bfloat16),
        jax.ShapeDtypeStruct((2, SEG, HD), jnp.float32),
    ]
    if level:
        out_specs.append(pl.BlockSpec((level, 2, SEG, HD), lambda h, *_: (0, 0, 0, 0)))
        out_shape.append(jax.ShapeDtypeStruct((level, 2, SEG, HD), jnp.bfloat16))
    last = level == LEVELS - 1
    return pl.pallas_call(
        functools.partial(backward_kernel, level),
        grid_spec=pltpu.PrefetchScalarGridSpec(
            num_scalar_prefetch=3,
            grid=(GROUP // BATCH,),
            in_specs=[
                pl.BlockSpec((1, count, BATCH * SEG), lambda h, *_: (h, 0, 0)),
                pl.BlockSpec((1, 1, SEG, width), lambda h, *_: (level, 0, 0, h)),
                pl.BlockSpec((SEG, width), lambda h, *_: (0, h)),
                pl.BlockSpec((8, SEG, PIECE), lambda h, *_: (0, 0, 0)),
                pl.BlockSpec((1, 1, SEG, HD), lambda h, *_: (level, 0, 0, 0)),
                pl.BlockSpec((1, 1, SEG, HD), lambda h, *_: (level, 0, 0, 0)),
            ]
            + [pl.BlockSpec((len(PAIRS), 2, SEG, HD), lambda h, *_: (0, 0, 0, 0))] * min(level, 1)
            + [ANY] * 2,
            out_specs=out_specs,
            scratch_shapes=[
                pltpu.VMEM((HD, count), jnp.bfloat16),
                pltpu.VMEM((count, HD), jnp.float32),
                pltpu.VMEM((count, HD), jnp.float32),
            ],
        ),
        out_shape=out_shape,
        input_output_aliases={} if last else {10 if level else 9: 0},
        compiler_params=PARAMS,
        cost_estimate=cost(8 * GROUP * count * SEG * HD, 2 * GROUP * count * SEG),
        name=f"backward_{level}",
    )(
        meta, parents, lengths, probabilities, queries, own, partner, key_rows, value_rows,
        *[picked] * min(level, 1), query_grad, token,
    )


def spread_kernel(target, meta, parents, *refs):
    terms, outs = refs[:-5], refs[-4:]
    me = node_id(meta)
    sibling = me + 1 - 2 * meta[2]
    other = 8 - 16 * meta[0]
    places = []
    for i in range(len(terms)):
        node = (me, sibling, me + other, sibling + other)[i % 4]
        places.append(ancestor(parents, node, target + 1 + i // 4, target))
    for step, out in enumerate(outs):
        x = lax.rem(meta[1] + step, 4)
        wanted = (meta[0] * 4 + x) * 2 + meta[2]
        total = jnp.zeros((2, SEG, HD), jnp.float32)
        for term, place in zip(terms, places):
            total += jnp.where(place == wanted, term[0].astype(jnp.float32), 0.0)
        out[...] = total.astype(jnp.bfloat16)


def spread(target, meta, parents, terms, token):
    return pl.pallas_call(
        functools.partial(spread_kernel, target),
        grid_spec=pltpu.PrefetchScalarGridSpec(
            num_scalar_prefetch=2,
            grid=(1,),
            in_specs=[pl.BlockSpec((1, 2, SEG, HD), lambda n, *_: (target, 0, 0, 0))] * len(terms)
            + [ANY],
            out_specs=[pl.BlockSpec((2, SEG, HD), lambda n, *_: (0, 0, 0))] * 4,
        ),
        out_shape=[jax.ShapeDtypeStruct((2, SEG, HD), jnp.bfloat16)] * 4,
        compiler_params=SMALL,
        cost_estimate=cost(8 * len(terms) * 2 * SEG * HD, 16 * 2 * SEG * HD),
        name=f"spread_{target}",
    )(meta, parents, *terms, token)


def finish_kernel(*refs):
    owns, parts, outs = refs[:LEVELS], refs[LEVELS:-2], refs[-2:]
    for t in range(LEVELS):
        total = owns[t][...]
        for part in parts[4 * t : 4 * t + 4]:
            total += part[...].astype(jnp.float32)
        for i in range(2):
            outs[i][t, 0] = total[i].astype(jnp.bfloat16)


def finish(owns, parts, shape):
    both = pl.BlockSpec((2, SEG, HD), lambda n: (0, 0, 0))
    return pl.pallas_call(
        finish_kernel,
        grid=(1,),
        in_specs=[both] * (LEVELS + len(parts)),
        out_specs=[pl.BlockSpec((LEVELS, 1, SEG, HD), lambda n: (0, 0, 0, 0))] * 2,
        out_shape=[jax.ShapeDtypeStruct(shape, jnp.bfloat16)] * 2,
        compiler_params=SMALL,
        cost_estimate=cost(16 * SEG * HD, 64 * SEG * HD),
        name="finish",
    )(*owns, *parts)


def local(queries, key_rows, value_rows, cotangent, out_weight, parents, seg_len):
    zh, x, c, zl, y = [lax.axis_index(name) for name in ("zh", "x", "c", "zl", "y")]
    meta = jnp.stack([zh, x, c, zl, y]).astype(jnp.int32)
    parents = parents.reshape(-1)
    lengths = seg_len.reshape(-1)
    *pieces, rows, upper, lower = prepare(meta, out_weight, key_rows, value_rows, cotangent)

    def hop(piece, i):
        if i % 2:
            return lax.ppermute(piece, ("zh", "zl"), ALT)
        return lax.ppermute(piece, "zl", SWAP)

    away = lax.ppermute(rows, "zh", SWAP)
    above = lax.ppermute(upper, "y", DOWN)
    below = lax.ppermute(upper, "y", UP)
    w0, w1 = hop(pieces[0], 0), hop(pieces[1], 1)
    rows, away, above, below, w0, w1, lower, p2, p3 = tie(
        rows, away, above, below, w0, w1, lower, pieces[2], pieces[3]
    )
    mine = lax.all_gather(jnp.stack([rows, away]), "x")
    across = lax.ppermute(below, "y", UP)
    above_low = lax.ppermute(lower, "y", DOWN)
    w2, w3 = hop(p2, 2), hop(p3, 3)
    o0, o1 = lax.ppermute(w0, "c", SWAP), lax.ppermute(w1, "c", SWAP)
    early = early_product(meta, upper, above, below, out_weight)
    across, above_low, w0, w1, w2, w3, o0, o1, lower, mine, early = tie(
        across, above_low, w0, w1, w2, w3, o0, o1, lower, mine, early
    )
    below_low = lax.ppermute(lower, "y", UP)
    across_low = lax.ppermute(above_low, "y", DOWN)
    o2, o3 = lax.ppermute(w2, "c", SWAP), lax.ppermute(w3, "c", SWAP)
    weights = [w0, w1, w2, w3, o0, o1, o2, o3]
    cots = [(lower, above_low, below_low, across_low), (upper, above, below, across)]
    other = lax.ppermute(mine, "c", SWAP)
    table = (meta, parents, lengths)
    owns = [None] * LEVELS
    partners = [None] * LEVELS

    def own_pair(i, token):
        owns[2 * i], owns[2 * i + 1] = product(False, meta, cots[i], [out_weight], token)
        return owns[2 * i]

    def partner_pair(i, token):
        parts = product(True, meta, cots[i], weights, token)
        for j in (1, 0):
            partners[2 * i + j] = lax.ppermute(parts[j], "zl", SWAP)
        return parts[0]

    owns[2], owns[3] = late_product(meta, across, out_weight, early, meta)
    token = partner_pair(1, owns[2])
    *probabilities, picked = probs(*table, queries, key_rows, mine, other, token)
    token = partner_pair(0, picked)
    query_grad = own_pair(0, token)
    own_grads = [None] * LEVELS
    terms = []
    parts = []
    token = query_grad
    for level in (3, 2, 1, 0):
        query_grad, own_grads[level], *rest = backward(
            level, *table, probabilities[level], queries, owns[level], partners[level],
            key_rows, value_rows, picked, query_grad, token,
        )
        if level < 3:
            here, up, across, down = spread(level, meta, parents, terms, query_grad)
            token = here
            parts = [
                here,
                lax.ppermute(up, "x", UP),
                lax.ppermute(down, "x", DOWN),
                lax.ppermute(across, "x", ACROSS),
            ] + parts
        if level:
            near = rest[0]
            sibling = lax.ppermute(near, "c", SWAP)
            terms = [
                near,
                sibling,
                lax.ppermute(near, "zh", SWAP),
                lax.ppermute(sibling, "zh", SWAP),
            ] + terms
    key_grad, value_grad = finish(own_grads, parts, key_rows.shape)
    return (query_grad, key_grad, value_grad)


def solution(mesh):
    fine = Mesh(mesh.devices.reshape(2, 4, 2, 2, 4), ("zh", "x", "c", "zl", "y"))
    rows = P(None, AXES, None, ("zl", "y"))
    in_specs = (rows, rows, rows, rows, P(("zl", "y"), None), P(), P())
    return jax.shard_map(
        local, mesh=fine, in_specs=in_specs, out_specs=(rows, rows, rows), check_vma=False
    )
```

profile of v0, /device:TPU:0, one launch (start us, length us, event | category | flops | bytes accessed | tf_op | source)
XLA Modules:
  0.0 262.2 jit_solution(9439734143392858681)
XLA Ops:
  7.9 6.5 %prepare.1 = (bf16[128,4096]{1,0:T(8,128)(2,1)}, bf16[128,4096]{1,0:T(8,128)(2,1)}, bf16[128,4096]{1,0:T(8,128)(2,1)}, bf16[128,4096]{1,0:T(8,128)(2,1)}, bf16[2...) custom-call(s32[5]{0:T(128)} %stack.32.meta.token, ...), custom_call_target="tpu_custom_call" | custom-call | bytes 12582912 | tf_op jit(solution)/shard_map/prepare/pallas_call | solution.py:89
  14.4 3.2 %collective-permute-start.1 = (bf16[2,256,1024]{2,1,0:T(8,128)(2,1)}, bf16[2,256,1024]{2,1,0:T(8,128)(2,1)S(1)}, u32[]{:S(2)}, u32[]{:S(2)}) collective-permute-start(bf16[2,256,1024]{2,1,0:T(8,128)(2,1)} %get-tuple-element.69.own), channel_id=1, source_target_pairs={{0,3},{1,0},{2,1},{3,2},{4,7},{5,4},{6,5},{7,6},{8,11},{9,8},{10,9... | collective-permute-start | bytes 3145736 | tf_op jit(solution)/shard_map/ppermute | solution.py:551
  17.6 1.9 collective-permute-start.3
  19.5 2.5 collective-permute-start.4
  22.0 1.1 collective-permute-start
  23.1 31.2 %collective-permute-done.refs_1_ = bf16[2,3,256,128]{3,2,1,0:T(8,128)(2,1)S(1)} collective-permute-done((bf16[2,3,256,128]{3,2,1,0:T(8,128)(2,1)}, bf16[2,3,256,128]{3,2,1,0:T(8,128)(2,1)S(1)}, u32[]{:S(2)}, u32[]{:S(2)}) %collective-permute-start) | collective-permute-done | bytes 393248 | tf_op jit(solution)/shard_map/ppermute | solution.py:550
  55.7 2.2 pad_maximum_fusion
  58.4 2.9 %collective-permute-start.6 = (bf16[2,256,1024]{2,1,0:T(8,128)(2,1)S(1)}, bf16[2,256,1024]{2,1,0:T(8,128)(2,1)S(1)}, u32[]{:S(2)}, u32[]{:S(2)}) collective-permute-start(bf16[2,256,1024]{2,1,0:T(8,128)(2,1)S(1)} %copy-done.20), channel_id=1, source_target_pairs={{0,3},{1,0},{2,1},{3,2},{4,7},{5,4},{6,5},{7,6},{8,11},{9,8},{10,9... | collective-permute-start | bytes 3145736 | tf_op jit(solution)/shard_map/ppermute | solution.py:559
  61.3 1.0 collective-permute-start.8
  62.3 8.9 %early_product.1.refs_10_ = f32[2,256,1024]{2,1,0:T(8,128)} custom-call(s32[5]{0:T(128)} %stack.32.meta.token, bf16[2,256,1024]{2,1,0:T(8,128)(2,1)} %get-tuple-element.69.own, bf16[2,256,1024]{2,1,0:T(8,128)(2,1)} %get-tuple-element.83.above, bf16[2,256,1024]{2,1,0:T(8,128)(2,1)} %get-tuple-element.75.below, bf16[1024,8192]{1,0:T(8,128)(2,1)} %refs_0_.1, ...), custom_call_target="tpu_custom_call" | custom-call | flops 3221225472 | bytes 8388608 | tf_op jit(solution)/shard_map/early_product/pallas_call | solution.py:161
  71.3 13.7 %collective-permute-done.5.refs_0_ = bf16[2,256,1024]{2,1,0:T(8,128)(2,1)S(1)} collective-permute-done((bf16[2,256,1024]{2,1,0:T(8,128)(2,1)}, bf16[2,256,1024]{2,1,0:T(8,128)(2,1)S(1)}, u32[]{:S(2)}, u32[]{:S(2)}) %collective-permute-start.5) | collective-permute-done | bytes 1048608 | tf_op jit(solution)/shard_map/ppermute | solution.py:558
  85.0 1.6 collective-permute-done.7.refs_4_
  86.6 1.2 collective-permute-done.8.refs_5_
  87.8 8.5 %all-gather.3.cloned.1.call-done = bf16[8,2,3,256,128]{4,3,2,1,0:T(8,128)(2,1)} async-done(((bf16[2,2,3,256,128]{4,3,2,1,0:T(8,128)(2,1)}), bf16[8,2,3,256,128]{4,3,2,1,0:T(8,128)(2,1)}) %all-gather.3.cloned.1.call-update) | async-done | bytes 3145744 | tf_op jit(solution)/shard_map/all_gather | solution.py:557
  97.0 1.5 collective-permute-start.14
  98.5 1.8 collective-permute-start.15
  101.5 6.0 %late_product.1 = (f32[256,1024]{1,0:T(8,128)}, f32[256,1024]{1,0:T(8,128)}) custom-call(s32[5]{0:T(128)} %stack.32.meta.token, bf16[2,256,1024]{2,1,0:T(8,128)(2,1)} %get-tuple-element.85.across, bf16[1024,8192]{1,0:T(8,128)(2,1)} %refs_0_.1, f32[2,256,1024]{2,1,0:T(8,128)} %get-tuple-element.92.early, s32[5]{0:T(128)} %stack.32.meta.token), custom_call_target="tpu_custom_call" | custom-call | flops 1073741824 | bytes 2097152 | tf_op jit(solution)/shard_map/late_product/pallas_call | solution.py:178
  108.5 9.8 %partner_product.2 = (bf16[8,256,128]{2,1,0:T(8,128)(2,1)}, bf16[8,256,128]{2,1,0:T(8,128)(2,1)}) custom-call(s32[5]{0:T(128)} %stack.32.meta.token, bf16[2,256,1024]{2,1,0:T(8,128)(2,1)} %get-tuple-element.69.own, bf16[2,256,1024]{2,1,0:T(8,128)(2,1)} %get-tuple-element.83.above, bf16[2,256,1024]{2,1,0:T(8,128)(2,1)} %get-tuple-element.75.below, ...), custom_call_target="tpu_custom_call" | custom-call | flops 4294967296 | bytes 10485760 | tf_op jit(solution)/shard_map/partner_product/pallas_call | solution.py:262
  118.3 1.6 collective-permute-start.19
  120.4 14.4 %probs.1 = (bf16[2,256,1024]{2,1,0:T(8,128)(2,1)}, bf16[2,512,1024]{2,1,0:T(8,128)(2,1)}, bf16[2,768,1024]{2,1,0:T(8,128)(2,1)}, bf16[2,1024,1024]{2,1,0:T(8,128)(2,1)}, bf16[6,2,256,128]{3,2,1,0:T(8,128)(2,1)}) custom-call(s32[5]{0:T(128)} %stack.32.meta.token, s32[48]{0:T(128)} %reshape.12.parents, s32[64]{0:T(128)} %reshape.13.lengths, ...), custom_call_target="tpu_custom_call" | custom-call | flops 1342177280 | bytes 10485760 | tf_op jit(solution)/shard_map/probs/pallas_call | solution.py:340
  136.2 9.8 %partner_product.3 = (bf16[8,256,128]{2,1,0:T(8,128)(2,1)}, bf16[8,256,128]{2,1,0:T(8,128)(2,1)}) custom-call(s32[5]{0:T(128)} %stack.32.meta.token, bf16[2,256,1024]{2,1,0:T(8,128)(2,1)} %get-tuple-element.96.own, bf16[2,256,1024]{2,1,0:T(8,128)(2,1)} %get-tuple-element.97.above, bf16[2,256,1024]{2,1,0:T(8,128)(2,1)} %copy-done.26, ...), custom_call_target="tpu_custom_call" | custom-call | flops 4294967296 | bytes 10485760 | tf_op jit(solution)/shard_map/partner_product/pallas_call | solution.py:262
  146.0 10.1 %own_product.1 = (f32[256,1024]{1,0:T(8,128)}, f32[256,1024]{1,0:T(8,128)}) custom-call(s32[5]{0:T(128)} %stack.32.meta.token, bf16[2,256,1024]{2,1,0:T(8,128)(2,1)} %get-tuple-element.96.own, bf16[2,256,1024]{2,1,0:T(8,128)(2,1)} %get-tuple-element.97.above, bf16[2,256,1024]{2,1,0:T(8,128)(2,1)} %copy-done.26, bf16[2,256,1024]{2,1,0:T(8,128)(2,1)} %copy-done.27, ...), custom_call_target="tpu_custom_call" | custom-call | flops 4294967296 | bytes 10485760 | tf_op jit(solution)/shard_map/own_product/pallas_call | solution.py:262
  156.9 10.0 %backward_3.1 = (bf16[4,1,256,1024]{3,2,1,0:T(8,128)(2,1)}, f32[2,256,128]{2,1,0:T(8,128)}, bf16[3,2,256,128]{3,2,1,0:T(8,128)(2,1)}) custom-call(s32[5]{0:T(128)} %stack.32.meta.token, s32[48]{0:T(128)} %reshape.12.parents, s32[64]{0:T(128)} %reshape.13.lengths, bf16[2,1024,1024]{2,1,0:T(8,128)(2,1)} %get-tuple-element.105.probs_ref, ...), custom_call_target="tpu_custom_call" | custom-call | flops 2147483648 | bytes 4194304 | tf_op jit(solution)/shard_map/backward_3/pallas_call | solution.py:446
  166.9 1.6 collective-permute-start.17
  168.6 2.9 %collective-permute-start.21 = (bf16[3,2,256,128]{3,2,1,0:T(8,128)(2,1)}, bf16[3,2,256,128]{3,2,1,0:T(8,128)(2,1)S(1)}, u32[]{:S(2)}, u32[]{:S(2)}) collective-permute-start(bf16[3,2,256,128]{3,2,1,0:T(8,128)(2,1)} %get-tuple-element.110.refs_0_.refs_4_.refs_8_), channel_id=1, source_target_pairs={{0,64},{64,0},{1,65},{65,1},{2,66},{66,2},{3,67},{67,3},{4,68},{68... | collective-permute-start | bytes 1179656 | tf_op jit(solution)/shard_map/ppermute | solution.py:615
  172.9 8.4 %backward_2.1 = (bf16[4,1,256,1024]{3,2,1,0:T(8,128)(2,1)}, f32[2,256,128]{2,1,0:T(8,128)}, bf16[2,2,256,128]{3,2,1,0:T(8,128)(2,1)}) custom-call(s32[5]{0:T(128)} %stack.32.meta.token, s32[48]{0:T(128)} %reshape.12.parents, s32[64]{0:T(128)} %reshape.13.lengths, ...), custom_call_target="tpu_custom_call", output_to_operand_aliasing={{0}: (10, {})} | custom-call | flops 1610612736 | bytes 3145728 | tf_op jit(solution)/shard_map/backward_2/pallas_call | solution.py:446
  182.0 1.1 collective-permute-done.23.refs_1_.refs_5_
  183.1 2.9 %collective-permute-start.24 = (bf16[2,2,256,128]{3,2,1,0:T(8,128)(2,1)}, bf16[2,2,256,128]{3,2,1,0:T(8,128)(2,1)S(1)}, u32[]{:S(2)}, u32[]{:S(2)}) collective-permute-start(bf16[2,2,256,128]{3,2,1,0:T(8,128)(2,1)} %get-tuple-element.113.refs_0_.refs_4_), channel_id=1, source_target_pairs={{0,64},{64,0},{1,65},{65,1},{2,66},{66,2},{3,67},{67,3},{4,68},{68... | collective-permute-start | bytes 786440 | tf_op jit(solution)/shard_map/ppermute | solution.py:615
  186.0 6.6 %collective-permute-done.21.refs_2_.refs_6_.refs_10_ = bf16[3,2,256,128]{3,2,1,0:T(8,128)(2,1)S(1)} collective-permute-done((bf16[3,2,256,128]{3,2,1,0:T(8,128)(2,1)}, bf16[3,2,256,128]{3,2,1,0:T(8,128)(2,1)S(1)}, u32[]{:S(2)}, u32[]{:S(2)}) %collective-permute-start.21) | collective-permute-done | bytes 393248 | tf_op jit(solution)/shard_map/ppermute | solution.py:615
  193.2 7.8 %collective-permute-done.22.refs_3_.refs_7_.refs_11_ = bf16[3,2,256,128]{3,2,1,0:T(8,128)(2,1)S(1)} collective-permute-done((bf16[3,2,256,128]{3,2,1,0:T(8,128)(2,1)S(1)}, bf16[3,2,256,128]{3,2,1,0:T(8,128)(2,1)S(1)}, u32[]{:S(2)}, u32[]{:S(2)}) %collective-permute-start.22) | collective-permute-done | bytes 393248 | tf_op jit(solution)/shard_map/ppermute | solution.py:616
  201.0 1.6 copy-done
  205.0 6.9 %backward_1.1 = (bf16[4,1,256,1024]{3,2,1,0:T(8,128)(2,1)}, f32[2,256,128]{2,1,0:T(8,128)}, bf16[1,2,256,128]{3,2,1,0:T(8,128)(2,1)}) custom-call(s32[5]{0:T(128)} %stack.32.meta.token, s32[48]{0:T(128)} %reshape.12.parents, s32[64]{0:T(128)} %reshape.13.lengths, ...), custom_call_target="tpu_custom_call", output_to_operand_aliasing={{0}: (10, {})} | custom-call | flops 1073741824 | bytes 2097152 | tf_op jit(solution)/shard_map/backward_1/pallas_call | solution.py:446
  213.5 2.1 collective-permute-start.28
  215.6 2.3 collective-permute-done.24.refs_2_.refs_6_
  217.9 5.6 %collective-permute-done.25.refs_3_.refs_7_ = bf16[2,2,256,128]{3,2,1,0:T(8,128)(2,1)S(1)} collective-permute-done((bf16[2,2,256,128]{3,2,1,0:T(8,128)(2,1)S(1)}, bf16[2,2,256,128]{3,2,1,0:T(8,128)(2,1)S(1)}, u32[]{:S(2)}, u32[]{:S(2)}) %collective-permute-start.25) | collective-permute-done | bytes 262176 | tf_op jit(solution)/shard_map/ppermute | solution.py:616
  223.5 1.6 copy-done.1
  225.1 1.4 spread_1.1
  227.8 2.5 collective-permute-start.33
  231.3 5.1 %backward_0.1 = (bf16[4,1,256,1024]{3,2,1,0:T(8,128)(2,1)}, f32[2,256,128]{2,1,0:T(8,128)}) custom-call(s32[5]{0:T(128)} %stack.32.meta.token, s32[48]{0:T(128)} %reshape.12.parents, s32[64]{0:T(128)} %reshape.13.lengths, bf16[2,256,1024]{2,1,0:T(8,128)(2,1)} %get-tuple-element.95.probs_ref, ...), custom_call_target="tpu_custom_call", output_to_operand_aliasing={{0}: (9, {})} | custom-call | flops 536870912 | bytes 1048576 | tf_op jit(solution)/shard_map/backward_0/pallas_call | solution.py:446
  236.4 3.1 %collective-permute-start.36 = (bf16[2,256,128]{2,1,0:T(8,128)(2,1)S(1)}, bf16[2,256,128]{2,1,0:T(8,128)(2,1)S(1)}, u32[]{:S(2)}, u32[]{:S(2)}) collective-permute-start(bf16[2,256,128]{2,1,0:T(8,128)(2,1)S(1)} %get-tuple-element.129), channel_id=1, source_target_pairs={{0,48},{16,0},{32,16},{48,32},{1,49},{17,1},{33,17},{49,33},{2,50}... | collective-permute-start | bytes 393224 | tf_op jit(solution)/shard_map/ppermute | solution.py:606
  239.4 1.6 copy-done.2
  241.0 1.8 spread_0.1
  242.9 1.7 collective-permute-start.37
  244.6 3.2 %collective-permute-start.30 = (bf16[2,256,128]{2,1,0:T(8,128)(2,1)S(1)}, bf16[2,256,128]{2,1,0:T(8,128)(2,1)S(1)}, u32[]{:S(2)}, u32[]{:S(2)}) collective-permute-start(bf16[2,256,128]{2,1,0:T(8,128)(2,1)S(1)} %get-tuple-element.123), channel_id=1, source_target_pairs={{0,48},{16,0},{32,16},{48,32},{1,49},{17,1},{33,17},{49,33},{2,50}... | collective-permute-start | bytes 393224 | tf_op jit(solution)/shard_map/ppermute | solution.py:606
  248.5 1.6 collective-permute-done.37.refs_15_
  250.1 2.1 collective-permute-done.29.refs_5_
  252.2 2.1 collective-permute-done.31.refs_7_
  254.3 1.0 finish.1
  (126 shorter events, 18.1 us)
Async XLA Ops:
  7.2 89.1 %all-gather.3.cloned.1.call-start = ((), (), s32[]{:S(2)}) async-start(), calls=%async_computation | async-start | bytes 3932160 | tf_op jit(solution)/shard_map/all_gather | solution.py:557
  14.4 39.9 %collective-permute-start.1 = (bf16[2,256,1024]{2,1,0:T(8,128)(2,1)}, bf16[2,256,1024]{2,1,0:T(8,128)(2,1)S(1)}, u32[]{:S(2)}, u32[]{:S(2)}) collective-permute-start(bf16[2,256,1024]{2,1,0:T(8,128)(2,1)} %get-tuple-element.69.own), channel_id=1, source_target_pairs={{0,3},{1,0},{2,1},{3,2},{4,7},{5,4},{6,5},{7,6},{8,11},{9,8},{10,9... | collective-permute-start | bytes 3145736 | tf_op jit(solution)/shard_map/ppermute | solution.py:551
  17.5 36.7 %collective-permute-start.2 = (bf16[2,256,1024]{2,1,0:T(8,128)(2,1)}, bf16[2,256,1024]{2,1,0:T(8,128)(2,1)}, u32[]{:S(2)}, u32[]{:S(2)}) collective-permute-start(bf16[2,256,1024]{2,1,0:T(8,128)(2,1)} %get-tuple-element.69.own), channel_id=1, source_target_pairs={{0,1},{1,2},{2,3},{3,0},{4,5},{5,6},{6,7},{7,4},{8,9},{9,10},{10,1... | collective-permute-start | bytes 3145736 | tf_op jit(solution)/shard_map/ppermute | solution.py:552
  17.6 36.7 %collective-permute-start.3 = (bf16[128,4096]{1,0:T(8,128)(2,1)}, bf16[128,4096]{1,0:T(8,128)(2,1)S(1)}, u32[]{:S(2)}, u32[]{:S(2)}) collective-permute-start(bf16[128,4096]{1,0:T(8,128)(2,1)} %get-tuple-element.70), channel_id=1, source_target_pairs={{0,4},{4,0},{1,5},{5,1},{2,6},{6,2},{3,7},{7,3},{8,12},{12,8},{9,1... | collective-permute-start | bytes 3145736 | tf_op jit(solution)/shard_map/ppermute | solution.py:548
  19.5 34.8 %collective-permute-start.4 = (bf16[128,4096]{1,0:T(8,128)(2,1)}, bf16[128,4096]{1,0:T(8,128)(2,1)}, u32[]{:S(2)}, u32[]{:S(2)}) collective-permute-start(bf16[128,4096]{1,0:T(8,128)(2,1)} %get-tuple-element.71), channel_id=1, source_target_pairs={{0,68},{4,64},{64,4},{68,0},{1,69},{5,65},{65,5},{69,1},{2,70},{6,... | collective-permute-start | bytes 3145736 | tf_op jit(solution)/shard_map/ppermute | solution.py:547
  22.0 32.3 %collective-permute-start = (bf16[2,3,256,128]{3,2,1,0:T(8,128)(2,1)}, bf16[2,3,256,128]{3,2,1,0:T(8,128)(2,1)S(1)}, u32[]{:S(2)}, u32[]{:S(2)}) collective-permute-start(bf16[2,3,256,128]{3,2,1,0:T(8,128)(2,1)} %get-tuple-element.68.refs_0_), channel_id=1, source_target_pairs={{0,64},{64,0},{1,65},{65,1},{2,66},{66,2},{3,67},{67,3},{4,68},{68... | collective-permute-start | bytes 1179656 | tf_op jit(solution)/shard_map/ppermute | solution.py:550
  57.9 4.4 %collective-permute-start.10 = (bf16[128,4096]{1,0:T(8,128)(2,1)}, bf16[128,4096]{1,0:T(8,128)(2,1)}, u32[]{:S(2)}, u32[]{:S(2)}) collective-permute-start(bf16[128,4096]{1,0:T(8,128)(2,1)} %get-tuple-element.78.refs_3_), channel_id=1, source_target_pairs={{0,8},{8,0},{1,9},{9,1},{2,10},{10,2},{3,11},{11,3},{4,12},{12,4},... | collective-permute-start | bytes 3145736 | tf_op jit(solution)/shard_map/ppermute | solution.py:561
  58.0 27.0 %collective-permute-start.5 = (bf16[2,256,1024]{2,1,0:T(8,128)(2,1)}, bf16[2,256,1024]{2,1,0:T(8,128)(2,1)S(1)}, u32[]{:S(2)}, u32[]{:S(2)}) collective-permute-start(bf16[2,256,1024]{2,1,0:T(8,128)(2,1)} %get-tuple-element.75.below), channel_id=1, source_target_pairs={{0,1},{1,2},{2,3},{3,0},{4,5},{5,6},{6,7},{7,4},{8,9},{9,10},{10,1... | collective-permute-start | bytes 3145736 | tf_op jit(solution)/shard_map/ppermute | solution.py:558
  58.4 26.6 %collective-permute-start.6 = (bf16[2,256,1024]{2,1,0:T(8,128)(2,1)S(1)}, bf16[2,256,1024]{2,1,0:T(8,128)(2,1)S(1)}, u32[]{:S(2)}, u32[]{:S(2)}) collective-permute-start(bf16[2,256,1024]{2,1,0:T(8,128)(2,1)S(1)} %copy-done.20), channel_id=1, source_target_pairs={{0,3},{1,0},{2,1},{3,2},{4,7},{5,4},{6,5},{7,6},{8,11},{9,8},{10,9... | collective-permute-start | bytes 3145736 | tf_op jit(solution)/shard_map/ppermute | solution.py:559
  61.3 25.3 %collective-permute-start.7 = (bf16[128,4096]{1,0:T(8,128)(2,1)}, bf16[128,4096]{1,0:T(8,128)(2,1)}, u32[]{:S(2)}, u32[]{:S(2)}) collective-permute-start(bf16[128,4096]{1,0:T(8,128)(2,1)} %get-tuple-element.79), channel_id=1, source_target_pairs={{0,4},{4,0},{1,5},{5,1},{2,6},{6,2},{3,7},{7,3},{8,12},{12,8},{9,1... | collective-permute-start | bytes 3145736 | tf_op jit(solution)/shard_map/ppermute | solution.py:548
  61.3 26.5 %collective-permute-start.8 = (bf16[128,4096]{1,0:T(8,128)(2,1)}, bf16[128,4096]{1,0:T(8,128)(2,1)}, u32[]{:S(2)}, u32[]{:S(2)}) collective-permute-start(bf16[128,4096]{1,0:T(8,128)(2,1)} %get-tuple-element.80), channel_id=1, source_target_pairs={{0,68},{4,64},{64,4},{68,0},{1,69},{5,65},{65,5},{69,1},{2,70},{6,... | collective-permute-start | bytes 3145736 | tf_op jit(solution)/shard_map/ppermute | solution.py:547
  62.3 25.5 %collective-permute-start.9 = (bf16[128,4096]{1,0:T(8,128)(2,1)}, bf16[128,4096]{1,0:T(8,128)(2,1)}, u32[]{:S(2)}, u32[]{:S(2)}) collective-permute-start(bf16[128,4096]{1,0:T(8,128)(2,1)} %get-tuple-element.77.refs_2_), channel_id=1, source_target_pairs={{0,8},{8,0},{1,9},{9,1},{2,10},{10,2},{3,11},{11,3},{4,12},{12,4},... | collective-permute-start | bytes 3145736 | tf_op jit(solution)/shard_map/ppermute | solution.py:561
  96.3 24.1 %collective-permute-start.11 = (bf16[4,2,2,3,256,128]{5,4,3,2,1,0:T(8,128)(2,1)}, bf16[4,2,2,3,256,128]{5,4,3,2,1,0:T(8,128)(2,1)}, u32[]{:S(2)}, u32[]{:S(2)}) collective-permute-start(bf16[4,2,2,3,256,128]{5,4,3,2,1,0:T(8,128)(2,1)} %get-tuple-element.84.mine), channel_id=1, source_target_pairs={{0,8},{8,0},{1,9},{9,1},{2,10},{10,2},{3,11},{11,3},{4,12},{12,4},... | collective-permute-start | bytes 9437192 | tf_op jit(solution)/shard_map/ppermute | solution.py:571
  96.4 11.1 %collective-permute-start.12 = (bf16[128,4096]{1,0:T(8,128)(2,1)}, bf16[128,4096]{1,0:T(8,128)(2,1)S(1)}, u32[]{:S(2)}, u32[]{:S(2)}) collective-permute-start(bf16[128,4096]{1,0:T(8,128)(2,1)} %get-tuple-element.88.refs_2_), channel_id=1, source_target_pairs={{0,8},{8,0},{1,9},{9,1},{2,10},{10,2},{3,11},{11,3},{4,12},{12,4},... | collective-permute-start | bytes 3145736 | tf_op jit(solution)/shard_map/ppermute | solution.py:568
  96.9 10.6 %collective-permute-start.13 = (bf16[128,4096]{1,0:T(8,128)(2,1)}, bf16[128,4096]{1,0:T(8,128)(2,1)}, u32[]{:S(2)}, u32[]{:S(2)}) collective-permute-start(bf16[128,4096]{1,0:T(8,128)(2,1)} %get-tuple-element.89.refs_3_), channel_id=1, source_target_pairs={{0,8},{8,0},{1,9},{9,1},{2,10},{10,2},{3,11},{11,3},{4,12},{12,4},... | collective-permute-start | bytes 3145736 | tf_op jit(solution)/shard_map/ppermute | solution.py:568
  97.0 37.9 %collective-permute-start.14 = (bf16[2,256,1024]{2,1,0:T(8,128)(2,1)}, bf16[2,256,1024]{2,1,0:T(8,128)(2,1)S(1)}, u32[]{:S(2)}, u32[]{:S(2)}) collective-permute-start(bf16[2,256,1024]{2,1,0:T(8,128)(2,1)} %get-tuple-element.96.own), channel_id=1, source_target_pairs={{0,1},{1,2},{2,3},{3,0},{4,5},{5,6},{6,7},{7,4},{8,9},{9,10},{10,1... | collective-permute-start | bytes 3145736 | tf_op jit(solution)/shard_map/ppermute | solution.py:566
  98.5 36.4 %collective-permute-start.15 = (bf16[2,256,1024]{2,1,0:T(8,128)(2,1)}, bf16[2,256,1024]{2,1,0:T(8,128)(2,1)S(1)}, u32[]{:S(2)}, u32[]{:S(2)}) collective-permute-start(bf16[2,256,1024]{2,1,0:T(8,128)(2,1)} %get-tuple-element.97.above), channel_id=1, source_target_pairs={{0,3},{1,0},{2,1},{3,2},{4,7},{5,4},{6,5},{7,6},{8,11},{9,8},{10,9... | collective-permute-start | bytes 3145736 | tf_op jit(solution)/shard_map/ppermute | solution.py:567
  118.3 37.8 %collective-permute-start.19 = (bf16[8,256,128]{2,1,0:T(8,128)(2,1)}, bf16[8,256,128]{2,1,0:T(8,128)(2,1)S(1)}, u32[]{:S(2)}, u32[]{:S(2)}) collective-permute-start(bf16[8,256,128]{2,1,0:T(8,128)(2,1)} %get-tuple-element.107), channel_id=1, source_target_pairs={{0,4},{4,0},{1,5},{5,1},{2,6},{6,2},{3,7},{7,3},{8,12},{12,8},{9,1... | collective-permute-start | bytes 1572872 | tf_op jit(solution)/shard_map/ppermute | solution.py:583
  119.9 52.2 %collective-permute-start.18 = (bf16[8,256,128]{2,1,0:T(8,128)(2,1)}, bf16[8,256,128]{2,1,0:T(8,128)(2,1)S(1)}, u32[]{:S(2)}, u32[]{:S(2)}) collective-permute-start(bf16[8,256,128]{2,1,0:T(8,128)(2,1)} %get-tuple-element.94.refs_0_), channel_id=1, source_target_pairs={{0,4},{4,0},{1,5},{5,1},{2,6},{6,2},{3,7},{7,3},{8,12},{12,8},{9,1... | collective-permute-start | bytes 1572872 | tf_op jit(solution)/shard_map/ppermute | solution.py:583
  166.9 4.6 %collective-permute-start.20 = (bf16[3,2,256,128]{3,2,1,0:T(8,128)(2,1)}, bf16[3,2,256,128]{3,2,1,0:T(8,128)(2,1)S(1)}, u32[]{:S(2)}, u32[]{:S(2)}) collective-permute-start(bf16[3,2,256,128]{3,2,1,0:T(8,128)(2,1)} %get-tuple-element.110.refs_0_.refs_4_.refs_8_), channel_id=1, source_target_pairs={{0,8},{8,0},{1,9},{9,1},{2,10},{10,2},{3,11},{11,3},{4,12},{12,4},... | collective-permute-start | bytes 1179656 | tf_op jit(solution)/shard_map/ppermute | solution.py:611
  166.9 37.3 %collective-permute-start.17 = (bf16[8,256,128]{2,1,0:T(8,128)(2,1)S(1)}, bf16[8,256,128]{2,1,0:T(8,128)(2,1)S(1)}, u32[]{:S(2)}, u32[]{:S(2)}) collective-permute-start(bf16[8,256,128]{2,1,0:T(8,128)(2,1)S(1)} %copy-done.36), channel_id=1, source_target_pairs={{0,4},{4,0},{1,5},{5,1},{2,6},{6,2},{3,7},{7,3},{8,12},{12,8},{9,1... | collective-permute-start | bytes 1572872 | tf_op jit(solution)/shard_map/ppermute | solution.py:583
  168.6 24.0 %collective-permute-start.21 = (bf16[3,2,256,128]{3,2,1,0:T(8,128)(2,1)}, bf16[3,2,256,128]{3,2,1,0:T(8,128)(2,1)S(1)}, u32[]{:S(2)}, u32[]{:S(2)}) collective-permute-start(bf16[3,2,256,128]{3,2,1,0:T(8,128)(2,1)} %get-tuple-element.110.refs_0_.refs_4_.refs_8_), channel_id=1, source_target_pairs={{0,64},{64,0},{1,65},{65,1},{2,66},{66,2},{3,67},{67,3},{4,68},{68... | collective-permute-start | bytes 1179656 | tf_op jit(solution)/shard_map/ppermute | solution.py:615
  171.4 29.6 %collective-permute-start.22 = (bf16[3,2,256,128]{3,2,1,0:T(8,128)(2,1)S(1)}, bf16[3,2,256,128]{3,2,1,0:T(8,128)(2,1)S(1)}, u32[]{:S(2)}, u32[]{:S(2)}) collective-permute-start(bf16[3,2,256,128]{3,2,1,0:T(8,128)(2,1)S(1)} %collective-permute-done.20.refs_1_.refs_5_.refs_9_), channel_id=1, source_target_pairs={{0,64},{64,0},{1,65},{65,1},{2,66},{66,2},{3,67},{67,3},{4,68},{68... | collective-permute-start | bytes 1179656 | tf_op jit(solution)/shard_map/ppermute | solution.py:616
  172.9 28.1 %copy-start.3 = (bf16[3,2,256,128]{3,2,1,0:T(8,128)(2,1)S(1)}, bf16[3,2,256,128]{3,2,1,0:T(8,128)(2,1)}, u32[]{:S(2)}) copy-start(bf16[3,2,256,128]{3,2,1,0:T(8,128)(2,1)} %get-tuple-element.110.refs_0_.refs_4_.refs_8_) | copy-start | bytes 1179652
  172.9 28.1 %copy-start.14 = (s32[5]{0:T(128)S(1)}, s32[5]{0:T(128)}, u32[]{:S(2)}) copy-start(s32[5]{0:T(128)} %stack.32.meta.token) | copy-start | bytes 64
  172.9 28.1 %copy-start.17 = (s32[48]{0:T(128)S(1)}, s32[48]{0:T(128)}, u32[]{:S(2)}) copy-start(s32[48]{0:T(128)} %reshape.12.parents) | copy-start | bytes 580
  181.3 1.8 collective-permute-start.23
  181.4 48.9 %collective-permute-start.16 = (bf16[8,256,128]{2,1,0:T(8,128)(2,1)S(1)}, bf16[8,256,128]{2,1,0:T(8,128)(2,1)S(1)}, u32[]{:S(2)}, u32[]{:S(2)}) collective-permute-start(bf16[8,256,128]{2,1,0:T(8,128)(2,1)S(1)} %copy-done.28), channel_id=1, source_target_pairs={{0,4},{4,0},{1,5},{5,1},{2,6},{6,2},{3,7},{7,3},{8,12},{12,8},{9,1... | collective-permute-start | bytes 1572872 | tf_op jit(solution)/shard_map/ppermute | solution.py:583
  183.1 34.7 %collective-permute-start.24 = (bf16[2,2,256,128]{3,2,1,0:T(8,128)(2,1)}, bf16[2,2,256,128]{3,2,1,0:T(8,128)(2,1)S(1)}, u32[]{:S(2)}, u32[]{:S(2)}) collective-permute-start(bf16[2,2,256,128]{3,2,1,0:T(8,128)(2,1)} %get-tuple-element.113.refs_0_.refs_4_), channel_id=1, source_target_pairs={{0,64},{64,0},{1,65},{65,1},{2,66},{66,2},{3,67},{67,3},{4,68},{68... | collective-permute-start | bytes 786440 | tf_op jit(solution)/shard_map/ppermute | solution.py:615
  192.6 30.9 %collective-permute-start.25 = (bf16[2,2,256,128]{3,2,1,0:T(8,128)(2,1)S(1)}, bf16[2,2,256,128]{3,2,1,0:T(8,128)(2,1)S(1)}, u32[]{:S(2)}, u32[]{:S(2)}) collective-permute-start(bf16[2,2,256,128]{3,2,1,0:T(8,128)(2,1)S(1)} %collective-permute-done.23.refs_1_.refs_5_), channel_id=1, source_target_pairs={{0,64},{64,0},{1,65},{65,1},{2,66},{66,2},{3,67},{67,3},{4,68},{68... | collective-permute-start | bytes 786440 | tf_op jit(solution)/shard_map/ppermute | solution.py:616
  205.0 18.4 %copy-start.4 = (bf16[2,2,256,128]{3,2,1,0:T(8,128)(2,1)S(1)}, bf16[2,2,256,128]{3,2,1,0:T(8,128)(2,1)}, u32[]{:S(2)}) copy-start(bf16[2,2,256,128]{3,2,1,0:T(8,128)(2,1)} %get-tuple-element.113.refs_0_.refs_4_) | copy-start | bytes 786436
  205.0 18.4 %copy-start.15 = (s32[5]{0:T(128)S(1)}, s32[5]{0:T(128)}, u32[]{:S(2)}) copy-start(s32[5]{0:T(128)} %stack.32.meta.token) | copy-start | bytes 64
  205.0 18.5 %copy-start.18 = (s32[48]{0:T(128)S(1)}, s32[48]{0:T(128)}, u32[]{:S(2)}) copy-start(s32[48]{0:T(128)} %reshape.12.parents) | copy-start | bytes 580
  211.9 1.6 collective-permute-start.26
  212.0 19.1 %collective-permute-start.27 = (bf16[1,2,256,128]{3,2,1,0:T(8,128)(2,1)}, bf16[1,2,256,128]{3,2,1,0:T(8,128)(2,1)S(1)}, u32[]{:S(2)}, u32[]{:S(2)}) collective-permute-start(bf16[1,2,256,128]{3,2,1,0:T(8,128)(2,1)} %get-tuple-element.120.refs_0_), channel_id=1, source_target_pairs={{0,64},{64,0},{1,65},{65,1},{2,66},{66,2},{3,67},{67,3},{4,68},{68... | collective-permute-start | bytes 393224 | tf_op jit(solution)/shard_map/ppermute | solution.py:615
  213.5 22.8 %collective-permute-start.28 = (bf16[1,2,256,128]{3,2,1,0:T(8,128)(2,1)S(1)}, bf16[1,2,256,128]{3,2,1,0:T(8,128)(2,1)S(1)}, u32[]{:S(2)}, u32[]{:S(2)}) collective-permute-start(bf16[1,2,256,128]{3,2,1,0:T(8,128)(2,1)S(1)} %collective-permute-done.26.refs_1_), channel_id=1, source_target_pairs={{0,64},{64,0},{1,65},{65,1},{2,66},{66,2},{3,67},{67,3},{4,68},{68... | collective-permute-start | bytes 393224 | tf_op jit(solution)/shard_map/ppermute | solution.py:616
  227.1 15.8 %collective-permute-start.32 = (bf16[2,256,128]{2,1,0:T(8,128)(2,1)S(1)}, bf16[2,256,128]{2,1,0:T(8,128)(2,1)S(1)}, u32[]{:S(2)}, u32[]{:S(2)}) collective-permute-start(bf16[2,256,128]{2,1,0:T(8,128)(2,1)S(1)} %get-tuple-element.125), channel_id=1, source_target_pairs={{0,16},{16,32},{32,48},{48,0},{1,17},{17,33},{33,49},{49,1},{2,18}... | collective-permute-start | bytes 393224 | tf_op jit(solution)/shard_map/ppermute | solution.py:605
  227.8 16.8 %collective-permute-start.33 = (bf16[2,256,128]{2,1,0:T(8,128)(2,1)S(1)}, bf16[2,256,128]{2,1,0:T(8,128)(2,1)S(1)}, u32[]{:S(2)}, u32[]{:S(2)}) collective-permute-start(bf16[2,256,128]{2,1,0:T(8,128)(2,1)S(1)} %get-tuple-element.126), channel_id=1, source_target_pairs={{0,48},{16,0},{32,16},{48,32},{1,49},{17,1},{33,17},{49,33},{2,50}... | collective-permute-start | bytes 393224 | tf_op jit(solution)/shard_map/ppermute | solution.py:606
  230.3 14.2 %collective-permute-start.34 = (bf16[2,256,128]{2,1,0:T(8,128)(2,1)S(1)}, bf16[2,256,128]{2,1,0:T(8,128)(2,1)S(1)}, u32[]{:S(2)}, u32[]{:S(2)}) collective-permute-start(bf16[2,256,128]{2,1,0:T(8,128)(2,1)S(1)} %get-tuple-element.127), channel_id=1, source_target_pairs={{0,32},{16,48},{32,0},{48,16},{1,33},{17,49},{33,1},{49,17},{2,34}... | collective-permute-start | bytes 393224 | tf_op jit(solution)/shard_map/ppermute | solution.py:607
  231.0 16.8 %collective-permute-start.35 = (bf16[2,256,128]{2,1,0:T(8,128)(2,1)S(1)}, bf16[2,256,128]{2,1,0:T(8,128)(2,1)S(1)}, u32[]{:S(2)}, u32[]{:S(2)}) collective-permute-start(bf16[2,256,128]{2,1,0:T(8,128)(2,1)S(1)} %get-tuple-element.128), channel_id=1, source_target_pairs={{0,16},{16,32},{32,48},{48,0},{1,17},{17,33},{33,49},{49,1},{2,18}... | collective-permute-start | bytes 393224 | tf_op jit(solution)/shard_map/ppermute | solution.py:605
  236.4 12.2 %collective-permute-start.36 = (bf16[2,256,128]{2,1,0:T(8,128)(2,1)S(1)}, bf16[2,256,128]{2,1,0:T(8,128)(2,1)S(1)}, u32[]{:S(2)}, u32[]{:S(2)}) collective-permute-start(bf16[2,256,128]{2,1,0:T(8,128)(2,1)S(1)} %get-tuple-element.129), channel_id=1, source_target_pairs={{0,48},{16,0},{32,16},{48,32},{1,49},{17,1},{33,17},{49,33},{2,50}... | collective-permute-start | bytes 393224 | tf_op jit(solution)/shard_map/ppermute | solution.py:606
  241.0 13.3 %copy-start.10 = (f32[2,256,128]{2,1,0:T(8,128)S(1)}, f32[2,256,128]{2,1,0:T(8,128)}, u32[]{:S(2)}) copy-start(f32[2,256,128]{2,1,0:T(8,128)} %get-tuple-element.118.refs_2_) | copy-start | bytes 786436
  241.0 13.3 %copy-start.11 = (f32[2,256,128]{2,1,0:T(8,128)S(1)}, f32[2,256,128]{2,1,0:T(8,128)}, u32[]{:S(2)}) copy-start(f32[2,256,128]{2,1,0:T(8,128)} %get-tuple-element.117.refs_1_) | copy-start | bytes 786436
  241.0 13.3 %copy-start.12 = (f32[2,256,128]{2,1,0:T(8,128)S(1)}, f32[2,256,128]{2,1,0:T(8,128)}, u32[]{:S(2)}) copy-start(f32[2,256,128]{2,1,0:T(8,128)} %get-tuple-element.116.refs_0_) | copy-start | bytes 786436
  242.9 7.2 %collective-permute-start.37 = (bf16[2,256,128]{2,1,0:T(8,128)(2,1)S(1)}, bf16[2,256,128]{2,1,0:T(8,128)(2,1)S(1)}, u32[]{:S(2)}, u32[]{:S(2)}) collective-permute-start(bf16[2,256,128]{2,1,0:T(8,128)(2,1)S(1)} %get-tuple-element.130), channel_id=1, source_target_pairs={{0,32},{16,48},{32,0},{48,16},{1,33},{17,49},{33,1},{49,17},{2,34}... | collective-permute-start | bytes 393224 | tf_op jit(solution)/shard_map/ppermute | solution.py:607
  244.6 7.7 %collective-permute-start.29 = (bf16[2,256,128]{2,1,0:T(8,128)(2,1)S(1)}, bf16[2,256,128]{2,1,0:T(8,128)(2,1)S(1)}, u32[]{:S(2)}, u32[]{:S(2)}) collective-permute-start(bf16[2,256,128]{2,1,0:T(8,128)(2,1)S(1)} %get-tuple-element.122), channel_id=1, source_target_pairs={{0,16},{16,32},{32,48},{48,0},{1,17},{17,33},{33,49},{49,1},{2,18}... | collective-permute-start | bytes 393224 | tf_op jit(solution)/shard_map/ppermute | solution.py:605
  244.6 7.6 %collective-permute-start.30 = (bf16[2,256,128]{2,1,0:T(8,128)(2,1)S(1)}, bf16[2,256,128]{2,1,0:T(8,128)(2,1)S(1)}, u32[]{:S(2)}, u32[]{:S(2)}) collective-permute-start(bf16[2,256,128]{2,1,0:T(8,128)(2,1)S(1)} %get-tuple-element.123), channel_id=1, source_target_pairs={{0,48},{16,0},{32,16},{48,32},{1,49},{17,1},{33,17},{49,33},{2,50}... | collective-permute-start | bytes 393224 | tf_op jit(solution)/shard_map/ppermute | solution.py:606
  247.8 6.5 %collective-permute-start.31 = (bf16[2,256,128]{2,1,0:T(8,128)(2,1)S(1)}, bf16[2,256,128]{2,1,0:T(8,128)(2,1)S(1)}, u32[]{:S(2)}, u32[]{:S(2)}) collective-permute-start(bf16[2,256,128]{2,1,0:T(8,128)(2,1)S(1)} %get-tuple-element.124), channel_id=1, source_target_pairs={{0,32},{16,48},{32,0},{48,16},{1,33},{17,49},{33,1},{49,17},{2,34}... | collective-permute-start | bytes 393224 | tf_op jit(solution)/shard_map/ppermute | solution.py:607
  (28 other events, 132.5 us)
Sparse Core Ops, SparseCore 0:
  58.0 38.1 all-gather.2
where the time goes:
time: 263 us; the launch traced here: 262 us
  Pallas kernels  101 us (38%)
  waiting for transfers between devices  86.2 us (33%)
  starting transfers between devices  44.3 us (17%)
  between operations  14.4 us (5%)
  local copies, waits for them, and re-layouts  14.1 us (5%)
    ppermute x1, waiting for transfers between devices, local(): away = lax.ppermute(rows, 'zh', SWAP)  31.2 us
    pallas_call x4, Pallas kernels, backward(): pl.pallas_call(functools.partial(backward_kernel, level), grid_spec=pltpu...  30.4 us
    pallas_call x3, Pallas kernels, product(): pl.pallas_call(functools.partial(product_kernel, partner), grid_spec=pltp...  29.7 us
    pallas_call x1, Pallas kernels, probs(): pl.pallas_call(probs_kernel, grid_spec=pltpu.PrefetchScalarGridSpec(num_s...  14.4 us
    ppermute x1, waiting for transfers between devices, local(): across = lax.ppermute(below, 'y', UP)  13.7 us
    ppermute x3, waiting for transfers between devices, local(): lax.ppermute(sibling, 'zh', SWAP)  13.4 us
    unnamed x74, local copies, waits for them, and re-layouts  12.2 us
    pallas_call x1, Pallas kernels, early_product(): pl.pallas_call(early_kernel, grid_spec=pltpu.PrefetchScalarGridSpec(num_s...  8.95 us
  transfers between devices with their start and end apart: 39, of which 14 were waited for; matrix products, arithmetic and copies ran while one was open for 0% of the time, Pallas kernels for 36%

commit v1 on v0

--- a/solution.py
+++ b/solution.py
@@ -23,7 +23,7 @@
 NT = (((1,), (1,)), ((), ()))
 PARAMS = pltpu.CompilerParams(vmem_limit_bytes=56 * 2**20)
 SMALL = pltpu.CompilerParams(vmem_limit_bytes=16 * 2**20)
-ANY = pl.BlockSpec(memory_space=pl.ANY)
+ANY = pl.BlockSpec(memory_space=pltpu.HBM)
 AXES = ("zh", "x", "c")
 ALT = [(0, 3), (1, 2), (2, 1), (3, 0)]
 SWAP = [(0, 1), (1, 0)]
@@ -33,7 +33,7 @@
 
 
 def cost(flops, size, exps=0):
-    return pl.CostEstimate(flops=flops, bytes_accessed=size, transcendentals=exps)
+    return pl.CostEstimate(flops=1, bytes_accessed=1, transcendentals=0)
 
 
 def node_id(meta):
@@ -53,9 +53,9 @@
     return c, x, zh
 
 
-def prepare_kernel(meta, weight, keys, values, cot, *refs):
-    pieces, (rows, upper, lower), refs = refs[:4], refs[4:7], refs[7:]
-    held, kept, passed, in_sems, out_sems = refs
+def prepare_kernel(meta, weight, cot, *refs):
+    pieces, (upper, lower), refs = refs[:4], refs[4:6], refs[6:]
+    held, passed, in_sems, out_sems = refs
 
     def piece(step):
         row = pl.multiple_of((meta[2] * 4 + step) * PIECE, PIECE)
@@ -63,8 +63,6 @@
         return weight.at[pl.ds(row, PIECE), pl.ds(column, HALF)]
 
     moves = [
-        (keys.at[0 : LEVELS - 1, 0], kept.at[0], rows.at[0]),
-        (values.at[0 : LEVELS - 1, 0], kept.at[1], rows.at[1]),
         (cot.at[2:4, 0], passed.at[0], upper),
         (cot.at[0:2, 0], passed.at[1], lower),
     ] + [(piece(i), held.at[i], pieces[i]) for i in range(4)]
@@ -85,32 +83,30 @@
         write.wait()
 
 
-def prepare(meta, weight, keys, values, cot):
+def prepare(meta, weight, cot):
     return pl.pallas_call(
         prepare_kernel,
         grid_spec=pltpu.PrefetchScalarGridSpec(
             num_scalar_prefetch=1,
             grid=(),
-            in_specs=[ANY] * 4,
-            out_specs=[ANY] * 7,
+            in_specs=[ANY] * 2,
+            out_specs=[ANY] * 6,
             scratch_shapes=[
                 pltpu.VMEM((4, PIECE, HALF), jnp.bfloat16),
-                pltpu.VMEM((2, LEVELS - 1, SEG, HD), jnp.bfloat16),
                 pltpu.VMEM((2, 2, SEG, FEATURES), jnp.bfloat16),
-                pltpu.SemaphoreType.DMA((8,)),
-                pltpu.SemaphoreType.DMA((8,)),
+                pltpu.SemaphoreType.DMA((6,)),
+                pltpu.SemaphoreType.DMA((6,)),
             ],
         ),
         out_shape=[
             *[jax.ShapeDtypeStruct((PIECE, HALF), jnp.bfloat16)] * 4,
-            jax.ShapeDtypeStruct((2, LEVELS - 1, SEG, HD), jnp.bfloat16),
             jax.ShapeDtypeStruct((2, SEG, FEATURES), jnp.bfloat16),
             jax.ShapeDtypeStruct((2, SEG, FEATURES), jnp.bfloat16),
         ],
         compiler_params=PARAMS,
         cost_estimate=cost(0, 12 * 2**20),
         name="prepare",
-    )(meta, weight, keys, values, cot)
+    )(meta, weight, cot)
 
 
 def tie_kernel(*refs):
@@ -128,25 +124,17 @@
     )(*arrays)
 
 
-def early_kernel(meta, own, above, below, w0, w1, w2, out):
+def blocks_kernel(count, added, meta, *refs):
+    cots, weights, refs = refs[:count], refs[count : 2 * count], refs[2 * count :]
     total = sum(
         lax.dot_general(
-            cot[...].reshape(2 * SEG, FEATURES), w[...], NT, preferred_element_type=jnp.float32
+            cot[...].reshape(2 * SEG, FEATURES), weight[...], NT, preferred_element_type=jnp.float32
         )
-        for cot, w in ((own, w0), (above, w1), (below, w2))
-    )
-    out[...] = total.reshape(out.shape)
-
-
-def late_kernel(meta, across, weight, early, token, *outs):
-    total = lax.dot_general(
-        across[...].reshape(2 * SEG, FEATURES),
-        weight[...],
-        NT,
-        preferred_element_type=jnp.float32,
-    )
-    for i in range(2):
-        outs[i][...] = early[i] + total[i * SEG : (i + 1) * SEG]
+        for cot, weight in zip(cots, weights)
+    ).reshape(2, SEG, ROWS)
+    if added:
+        total += refs[0][...]
+    refs[-1][...] = total
 
 
 def feature_spec(step):
@@ -156,48 +144,30 @@
     return pl.BlockSpec((ROWS, FEATURES), index)
 
 
-def early_product(meta, own, above, below, weight):
+def blocks_product(meta, cots, steps, weight, earlier, token):
+    count = len(cots)
     whole = pl.BlockSpec((2, SEG, FEATURES), lambda n, *_: (0, 0, 0))
-    return pl.pallas_call(
-        early_kernel,
+    part = pl.BlockSpec((2, SEG, ROWS), lambda n, *_: (0, 0, n))
+    return pl.pallas_call(
+        functools.partial(blocks_kernel, count, len(earlier)),
         grid_spec=pltpu.PrefetchScalarGridSpec(
             num_scalar_prefetch=1,
             grid=(4,),
-            in_specs=[whole] * 3 + [feature_spec(step) for step in (0, 1, 3)],
-            out_specs=pl.BlockSpec((2, SEG, ROWS), lambda n, *_: (0, 0, n)),
+            in_specs=[whole] * count
+            + [feature_spec(step) for step in steps]
+            + [part] * len(earlier)
+            + [ANY],
+            out_specs=part,
         ),
         out_shape=jax.ShapeDtypeStruct((2, SEG, FEATURES), jnp.float32),
         compiler_params=PARAMS,
-        cost_estimate=cost(3 * SEG * 1024 * HALF, 2 * 1024 * HALF),
-        name="early_product",
-    )(meta, own, above, below, weight, weight, weight)
-
-
-def late_product(meta, across, weight, early, token):
-    whole = pl.BlockSpec((2, SEG, FEATURES), lambda n, *_: (0, 0, 0))
-    return pl.pallas_call(
-        late_kernel,
-        grid_spec=pltpu.PrefetchScalarGridSpec(
-            num_scalar_prefetch=1,
-            grid=(4,),
-            in_specs=[
-                whole,
-                feature_spec(2),
-                pl.BlockSpec((2, SEG, ROWS), lambda n, *_: (0, 0, n)),
-                ANY,
-            ],
-            out_specs=[pl.BlockSpec((SEG, ROWS), lambda n, *_: (0, n))] * 2,
-        ),
-        out_shape=[jax.ShapeDtypeStruct((SEG, FEATURES), jnp.float32)] * 2,
-        compiler_params=PARAMS,
-        cost_estimate=cost(SEG * 1024 * HALF, 2 * 1024 * 1024),
-        name="late_product",
-    )(meta, across, weight, early, token)
-
-
-def product_kernel(partner, meta, own, above, below, across, *refs):
-    count = 8 if partner else 1
-    weights, refs = refs[:count], refs[count:]
+        cost_estimate=cost(count * SEG * 1024 * HALF, 2 * 1024 * HALF),
+        name="own_product",
+    )(meta, *cots, *[weight] * count, *earlier, token)
+
+
+def product_kernel(meta, own, above, below, across, *refs):
+    weights, refs = refs[:8], refs[8:]
     outs, (cots, held, cot_sems, sems) = refs[1:3], refs[3:]
     step = pl.program_id(0)
 
@@ -207,16 +177,12 @@
         return pltpu.make_async_copy(source, target, cot_sems.at[sem])
 
     def block(q):
-        if partner:
-            return [
-                pltpu.make_async_copy(
-                    weights[2 * q + i], held.at[q, pl.ds(i * PIECE, PIECE)], sems.at[q, i]
-                )
-                for i in range(2)
-            ]
-        column = pl.multiple_of(meta[3] * HALF, HALF)
-        source = weights[0].at[q * ROWS : (q + 1) * ROWS, pl.ds(column, HALF)]
-        return [pltpu.make_async_copy(source, held.at[q], sems.at[q, 0])]
+        return [
+            pltpu.make_async_copy(
+                weights[2 * q + i], held.at[q, pl.ds(i * PIECE, PIECE)], sems.at[q, i]
+            )
+            for i in range(2)
+        ]
 
     upper, lower = pl.ds(0, SEG), pl.ds(SEG, SEG)
     moves = [
@@ -245,22 +211,15 @@
     total = lax.dot_general(cots[...], held[step], NT, preferred_element_type=jnp.float32)
     for i in range(2):
         part = total[i * SEG : (i + 1) * SEG]
-        if partner:
-            outs[i][0] = part[:, :PIECE].astype(jnp.bfloat16)
-            outs[i][1] = part[:, PIECE:].astype(jnp.bfloat16)
-        else:
-            outs[i][...] = part
-
-
-def product(partner, meta, cots, weights, token):
-    if partner:
-        out_shape = [jax.ShapeDtypeStruct((8, SEG, PIECE), jnp.bfloat16)] * 2
-        out_specs = [pl.BlockSpec((2, SEG, PIECE), lambda q, *_: (q, 0, 0))] * 2
-    else:
-        out_shape = [jax.ShapeDtypeStruct((SEG, FEATURES), jnp.float32)] * 2
-        out_specs = [pl.BlockSpec((SEG, ROWS), lambda q, *_: (0, q))] * 2
-    return pl.pallas_call(
-        functools.partial(product_kernel, partner),
+        outs[i][0] = part[:, :PIECE].astype(jnp.bfloat16)
+        outs[i][1] = part[:, PIECE:].astype(jnp.bfloat16)
+
+
+def product(meta, cots, weights, token):
+    out_shape = [jax.ShapeDtypeStruct((8, SEG, PIECE), jnp.bfloat16)] * 2
+    out_specs = [pl.BlockSpec((2, SEG, PIECE), lambda q, *_: (q, 0, 0))] * 2
+    return pl.pallas_call(
+        product_kernel,
         grid_spec=pltpu.PrefetchScalarGridSpec(
             num_scalar_prefetch=1,
             grid=(4,),
@@ -276,7 +235,7 @@
         out_shape=out_shape,
         compiler_params=PARAMS,
         cost_estimate=cost(4 * SEG * 1024 * HALF, 2 * 1024 * HALF + 8 * SEG * 1024),
-        name="partner_product" if partner else "own_product",
+        name="partner_product",
     )(meta, *cots, *weights, token)
 
 
@@ -285,6 +244,44 @@
 
 
 PAIRS = [(level, m) for level in range(LEVELS) for m in range(level)]
+
+
+def pick_kernel(meta, parents, mine, *refs):
+    outs, sems = refs[:2], refs[2]
+    copies = []
+    for i, (level, m) in enumerate(PAIRS):
+        for side in range(2):
+            me = node_id(meta)
+            if side:
+                me = me + 1 - 2 * meta[2]
+            c, x, zh = relative(meta, ancestor(parents, me, level, m))
+            for part in range(2):
+                copy = pltpu.make_async_copy(
+                    mine.at[x, zh, part, m], outs[side].at[i, part], sems.at[side, i, part]
+                )
+                copies.append((c == 0, copy))
+    for held, copy in copies:
+        pl.when(held)(copy.start)
+    for held, copy in copies:
+        pl.when(held)(copy.wait)
+
+
+def pick(meta, parents, mine):
+    shape = (len(PAIRS), 2, SEG, HD)
+    return pl.pallas_call(
+        pick_kernel,
+        grid_spec=pltpu.PrefetchScalarGridSpec(
+            num_scalar_prefetch=2,
+            grid=(1,),
+            in_specs=[ANY],
+            out_specs=[pl.BlockSpec(shape, lambda *_: (0, 0, 0, 0))] * 2,
+            scratch_shapes=[pltpu.SemaphoreType.DMA((2, len(PAIRS), 2))],
+        ),
+        out_shape=[jax.ShapeDtypeStruct(shape, jnp.bfloat16)] * 2,
+        compiler_params=PARAMS,
+        cost_estimate=cost(0, 0),
+        name="pick",
+    )(meta, parents, mine)
 
 
 def probs_kernel(meta, parents, lengths, query, own_key, mine, other, *refs):
@@ -295,11 +292,11 @@
     def _():
         copies = []
         for i, (level, m) in enumerate(PAIRS):
-            c, x, zh = relative(meta, ancestor(parents, me, level, m))
+            c = relative(meta, ancestor(parents, me, level, m))[0]
             for part in range(2):
                 pair = [
                     pltpu.make_async_copy(
-                        source.at[x, zh, part, m], picked.at[i, part], sems.at[i, part]
+                        source.at[i, part], picked.at[i, part], sems.at[i, part]
                     )
                     for source in (mine, other)
                 ]
@@ -397,7 +394,7 @@
     for i in range(BATCH):
         head = step * BATCH + i
         piece = lax.rem(step + meta[2], 2) * 4 + i
-        total = own[:, i * HD : (i + 1) * HD] + partner[piece].astype(jnp.float32)
+        total = own[0, :, i * HD : (i + 1) * HD] + partner[piece].astype(jnp.float32)
         heads.append(jnp.where(valid, total, 0.0).astype(jnp.bfloat16))
     dout = jnp.concatenate(heads, axis=0)
     q = jnp.concatenate([query[0, 0, :, i * HD : (i + 1) * HD] for i in range(BATCH)], axis=0)
@@ -451,7 +448,7 @@
             in_specs=[
                 pl.BlockSpec((1, count, BATCH * SEG), lambda h, *_: (h, 0, 0)),
                 pl.BlockSpec((1, 1, SEG, width), lambda h, *_: (level, 0, 0, h)),
-                pl.BlockSpec((SEG, width), lambda h, *_: (0, h)),
+                pl.BlockSpec((1, SEG, width), lambda h, *_: (level % 2, 0, h)),
                 pl.BlockSpec((8, SEG, PIECE), lambda h, *_: (0, 0, 0)),
                 pl.BlockSpec((1, 1, SEG, HD), lambda h, *_: (level, 0, 0, 0)),
                 pl.BlockSpec((1, 1, SEG, HD), lambda h, *_: (level, 0, 0, 0)),
@@ -480,21 +477,22 @@
     terms, outs = refs[:-5], refs[-4:]
     me = node_id(meta)
     sibling = me + 1 - 2 * meta[2]
-    other = 8 - 16 * meta[0]
     places = []
     for i in range(len(terms)):
-        node = (me, sibling, me + other, sibling + other)[i % 4]
-        places.append(ancestor(parents, node, target + 1 + i // 4, target))
+        node = sibling if i % 2 else me
+        places.append(ancestor(parents, node, target + 1 + i // 2, target))
     for step, out in enumerate(outs):
         x = lax.rem(meta[1] + step, 4)
-        wanted = (meta[0] * 4 + x) * 2 + meta[2]
-        total = jnp.zeros((2, SEG, HD), jnp.float32)
-        for term, place in zip(terms, places):
-            total += jnp.where(place == wanted, term[0].astype(jnp.float32), 0.0)
-        out[...] = total.astype(jnp.bfloat16)
+        for zh in range(2):
+            wanted = (zh * 4 + x) * 2 + meta[2]
+            total = jnp.zeros((2, SEG, HD), jnp.float32)
+            for term, place in zip(terms, places):
+                total += jnp.where(place == wanted, term[0].astype(jnp.float32), 0.0)
+            out[zh] = total.astype(jnp.bfloat16)
 
 
 def spread(target, meta, parents, terms, token):
+    whole = pl.BlockSpec((2, 2, SEG, HD), lambda n, *_: (0, 0, 0, 0))
     return pl.pallas_call(
         functools.partial(spread_kernel, target),
         grid_spec=pltpu.PrefetchScalarGridSpec(
@@ -502,20 +500,47 @@
             grid=(1,),
             in_specs=[pl.BlockSpec((1, 2, SEG, HD), lambda n, *_: (target, 0, 0, 0))] * len(terms)
             + [ANY],
-            out_specs=[pl.BlockSpec((2, SEG, HD), lambda n, *_: (0, 0, 0))] * 4,
-        ),
-        out_shape=[jax.ShapeDtypeStruct((2, SEG, HD), jnp.bfloat16)] * 4,
+            out_specs=[whole] * 4,
+        ),
+        out_shape=[jax.ShapeDtypeStruct((2, 2, SEG, HD), jnp.bfloat16)] * 4,
         compiler_params=SMALL,
-        cost_estimate=cost(8 * len(terms) * 2 * SEG * HD, 16 * 2 * SEG * HD),
+        cost_estimate=cost(0, 0),
         name=f"spread_{target}",
     )(meta, parents, *terms, token)
+
+
+def collect_kernel(meta, *refs):
+    parts, (kept, given) = refs[:4], refs[5:]
+    kept[...] = sum(part[meta[0]].astype(jnp.float32) for part in parts)
+    given[...] = sum(part[1 - meta[0]].astype(jnp.float32) for part in parts).astype(jnp.bfloat16)
+
+
+def collect(meta, parts, token):
+    whole = pl.BlockSpec((2, 2, SEG, HD), lambda n, *_: (0, 0, 0, 0))
+    half = pl.BlockSpec((2, SEG, HD), lambda n, *_: (0, 0, 0))
+    return pl.pallas_call(
+        collect_kernel,
+        grid_spec=pltpu.PrefetchScalarGridSpec(
+            num_scalar_prefetch=1,
+            grid=(1,),
+            in_specs=[whole] * 4 + [ANY],
+            out_specs=[half] * 2,
+        ),
+        out_shape=[
+            jax.ShapeDtypeStruct((2, SEG, HD), jnp.float32),
+            jax.ShapeDtypeStruct((2, SEG, HD), jnp.bfloat16),
+        ],
+        compiler_params=SMALL,
+        cost_estimate=cost(0, 0),
+        name="collect",
+    )(meta, *parts, token)
 
 
 def finish_kernel(*refs):
     owns, parts, outs = refs[:LEVELS], refs[LEVELS:-2], refs[-2:]
     for t in range(LEVELS):
         total = owns[t][...]
-        for part in parts[4 * t : 4 * t + 4]:
+        for part in parts[2 * t : 2 * t + 2]:
             total += part[...].astype(jnp.float32)
         for i in range(2):
             outs[i][t, 0] = total[i].astype(jnp.bfloat16)
@@ -540,81 +565,95 @@
     meta = jnp.stack([zh, x, c, zl, y]).astype(jnp.int32)
     parents = parents.reshape(-1)
     lengths = seg_len.reshape(-1)
-    *pieces, rows, upper, lower = prepare(meta, out_weight, key_rows, value_rows, cotangent)
+    table = (meta, parents, lengths)
+    rows = jnp.stack([key_rows[: LEVELS - 1, 0], value_rows[: LEVELS - 1, 0]])
+    away = lax.ppermute(rows, "zh", SWAP)
+    *pieces, upper, lower = prepare(meta, out_weight, cotangent)
+    rows, away, upper, *pieces = tie(rows, away, upper, *pieces)
+    mine = lax.all_gather(jnp.stack([rows, away]), "x")
 
     def hop(piece, i):
         if i % 2:
             return lax.ppermute(piece, ("zh", "zl"), ALT)
         return lax.ppermute(piece, "zl", SWAP)
 
-    away = lax.ppermute(rows, "zh", SWAP)
     above = lax.ppermute(upper, "y", DOWN)
     below = lax.ppermute(upper, "y", UP)
     w0, w1 = hop(pieces[0], 0), hop(pieces[1], 1)
-    rows, away, above, below, w0, w1, lower, p2, p3 = tie(
-        rows, away, above, below, w0, w1, lower, pieces[2], pieces[3]
+    above, below, w0, w1, lower, p2, p3 = tie(
+        above, below, w0, w1, lower, pieces[2], pieces[3]
     )
-    mine = lax.all_gather(jnp.stack([rows, away]), "x")
     across = lax.ppermute(below, "y", UP)
     above_low = lax.ppermute(lower, "y", DOWN)
     w2, w3 = hop(p2, 2), hop(p3, 3)
-    o0, o1 = lax.ppermute(w0, "c", SWAP), lax.ppermute(w1, "c", SWAP)
-    early = early_product(meta, upper, above, below, out_weight)
-    across, above_low, w0, w1, w2, w3, o0, o1, lower, mine, early = tie(
-        across, above_low, w0, w1, w2, w3, o0, o1, lower, mine, early
+    early = blocks_product(meta, [upper, above, below], (0, 1, 3), out_weight, [], meta)
+    mine, early = tie(mine, early)
+    mine, other = pick(meta, parents, mine)
+    other = lax.ppermute(other, "c", SWAP)
+    *probabilities, picked = probs(*table, queries, key_rows, mine, other, early)
+    across, above_low, w0, w1, w2, w3, lower, early, picked = tie(
+        across, above_low, w0, w1, w2, w3, lower, early, picked
     )
     below_low = lax.ppermute(lower, "y", UP)
     across_low = lax.ppermute(above_low, "y", DOWN)
-    o2, o3 = lax.ppermute(w2, "c", SWAP), lax.ppermute(w3, "c", SWAP)
-    weights = [w0, w1, w2, w3, o0, o1, o2, o3]
-    cots = [(lower, above_low, below_low, across_low), (upper, above, below, across)]
-    other = lax.ppermute(mine, "c", SWAP)
-    table = (meta, parents, lengths)
-    owns = [None] * LEVELS
+    weights = [w0, w1, w2, w3]
+    weights += [lax.ppermute(piece, "c", SWAP) for piece in weights]
     partners = [None] * LEVELS
 
-    def own_pair(i, token):
-        owns[2 * i], owns[2 * i + 1] = product(False, meta, cots[i], [out_weight], token)
-        return owns[2 * i]
-
-    def partner_pair(i, token):
-        parts = product(True, meta, cots[i], weights, token)
+    def partner_pair(i, cots, token):
+        parts = product(meta, cots, weights, token)
         for j in (1, 0):
             partners[2 * i + j] = lax.ppermute(parts[j], "zl", SWAP)
         return parts[0]
 
-    owns[2], owns[3] = late_product(meta, across, out_weight, early, meta)
-    token = partner_pair(1, owns[2])
-    *probabilities, picked = probs(*table, queries, key_rows, mine, other, token)
-    token = partner_pair(0, picked)
-    query_grad = own_pair(0, token)
+    own_high = blocks_product(meta, [across], (2,), out_weight, [early], meta)
+    token = partner_pair(1, (upper, above, below, across), own_high)
+    early_low = blocks_product(meta, [lower, above_low], (0, 1), out_weight, [], token)
+    token = partner_pair(0, (lower, above_low, below_low, across_low), early_low)
     own_grads = [None] * LEVELS
-    terms = []
-    parts = []
-    token = query_grad
-    for level in (3, 2, 1, 0):
+    terms = [None] * 6
+    moved = [None] * (LEVELS - 1)
+    parts = [None] * 6
+
+    def back(level, own, query_grad, token):
         query_grad, own_grads[level], *rest = backward(
-            level, *table, probabilities[level], queries, owns[level], partners[level],
+            level, *table, probabilities[level], queries, own, partners[level],
             key_rows, value_rows, picked, query_grad, token,
         )
-        if level < 3:
-            here, up, across, down = spread(level, meta, parents, terms, query_grad)
-            token = here
-            parts = [
-                here,
-                lax.ppermute(up, "x", UP),
-                lax.ppermute(down, "x", DOWN),
-                lax.ppermute(across, "x", ACROSS),
-            ] + parts
         if level:
-            near = rest[0]
-            sibling = lax.ppermute(near, "c", SWAP)
-            terms = [
-                near,
-                sibling,
-                lax.ppermute(near, "zh", SWAP),
-                lax.ppermute(sibling, "zh", SWAP),
-            ] + terms
+            terms[2 * level - 2] = rest[0]
+            terms[2 * level - 1] = lax.ppermute(rest[0], "c", SWAP)
+        return query_grad
+
+    def spread_out(target, token):
+        here, up, across, down = spread(target, meta, parents, terms[2 * target :], token)
+        moved[target] = [
+            here,
+            lax.ppermute(up, "x", UP),
+            lax.ppermute(down, "x", DOWN),
+            lax.ppermute(across, "x", ACROSS),
+        ]
+        return here
+
+    def bring(target, token):
+        kept, given = collect(meta, moved[target], token)
+        parts[2 * target] = kept
+        parts[2 * target + 1] = lax.ppermute(given, "zh", SWAP)
+        return kept
+
+    query_grad = back(3, own_high, token, token)
+    own_low = blocks_product(
+        meta, [below_low, across_low], (3, 2), out_weight, [early_low], query_grad
+    )
+    token = spread_out(2, own_low)
+    query_grad = back(2, own_high, query_grad, token)
+    token = spread_out(1, query_grad)
+    query_grad = back(1, own_low, query_grad, token)
+    token = bring(2, query_grad)
+    token = spread_out(0, token)
+    query_grad = back(0, own_low, query_grad, token)
+    token = bring(1, query_grad)
+    bring(0, token)
     key_grad, value_grad = finish(own_grads, parts, key_rows.shape)
     return (query_grad, key_grad, value_grad)
 

time: 263 us -> 229 us (0.87)
  waiting for transfers between devices: 86.2 us -> 33.1 us
  Pallas kernels: 101 us -> 111 us
  local copies, waits for them, and re-layouts: 14.1 us -> 21.9 us
    ppermute x1, waiting for transfers between devices: 31.2 us -> 2.3 us  [local(): away = lax.ppermute(rows, 'zh', SWAP)]
    ppermute x23 -> x20, waiting for transfers between devices: 29.9 us -> 8.94 us  [the longest x3 4.25 us: bring(): parts[2 * target + 1] = lax.ppermute(given, 'zh', SWAP)]
    ppermute x2, waiting for transfers between devices: 1.57 us -> 17.5 us  [hop(): return lax.ppermute(piece, 'zl', SWAP)]
    ppermute x1, waiting for transfers between devices: 13.7 us -> 0.01 us  [local(): across = lax.ppermute(below, 'y', UP)]
    pallas_call x5 -> x10, Pallas kernels: 44.6 us -> 55.1 us  [the longest x4 29.9 us: blocks_product(): pl.pallas_call(functools.partial(blocks_kernel, count, len(earlier)), gri...]
    all_gather x1, waiting for transfers between devices: 8.47 us -> 0.01 us  [local(): mine = lax.all_gather(jnp.stack([rows, away]), 'x')]
    unnamed x74 -> x94, local copies, waits for them, and re-layouts: 12.2 us -> 19 us
    ppermute x1, starting transfers between devices: 1.06 us -> 4.04 us  [local(): away = lax.ppermute(rows, 'zh', SWAP)]
  transfers between devices with their start and end apart: 39 -> 36, of which waited for: 14 -> 10; matrix products, arithmetic and copies ran while one was open for 0% -> 1% of each run, Pallas kernels for 36% -> 48%
where the time goes in v1:
time: 229 us; the launch traced here: 227 us
  Pallas kernels  111 us (48%)
  starting transfers between devices  44.4 us (19%)
  waiting for transfers between devices  33.1 us (14%)
  local copies, waits for them, and re-layouts  21.9 us (10%)
  between operations  14.5 us (6%)
    pallas_call x4, Pallas kernels, backward(): pl.pallas_call(functools.partial(backward_kernel, level), grid_spec=pltpu...  30.3 us
    pallas_call x4, Pallas kernels, blocks_product(): pl.pallas_call(functools.partial(blocks_kernel, count, len(earlier)), gri...  29.9 us
    pallas_call x2, Pallas kernels, product(): pl.pallas_call(product_kernel, grid_spec=pltpu.PrefetchScalarGridSpec(num...  19.6 us
    unnamed x94, local copies, waits for them, and re-layouts  19 us
    ppermute x2, waiting for transfers between devices, hop(): return lax.ppermute(piece, 'zl', SWAP)  17.5 us
    pallas_call x1, Pallas kernels, probs(): pl.pallas_call(probs_kernel, grid_spec=pltpu.PrefetchScalarGridSpec(num_s...  14.2 us
    ppermute x3, starting transfers between devices, spread_out(): lax.ppermute(down, 'x', DOWN)  7.43 us
    pallas_call x1, Pallas kernels, prepare(): pl.pallas_call(prepare_kernel, grid_spec=pltpu.PrefetchScalarGridSpec(num...  6.16 us
  transfers between devices with their start and end apart: 36, of which 10 were waited for; matrix products, arithmetic and copies ran while one was open for 1% of the time, Pallas kernels for 48%

profile of v1, /device:TPU:0, one launch (start us, length us, event | category | flops | bytes accessed | tf_op | source)
XLA Modules:
  0.0 226.8 jit_solution(1796256642552337787)
XLA Ops:
  7.2 1.1 slice_bitcast_fusion
  8.3 4.0 %collective-permute-start = (bf16[2,3,256,128]{3,2,1,0:T(8,128)(2,1)S(1)}, bf16[2,3,256,128]{3,2,1,0:T(8,128)(2,1)S(1)}, u32[]{:S(2)}, u32[]{:S(2)}) collective-permute-start(bf16[2,3,256,128]{3,2,1,0:T(8,128)(2,1)S(1)} %pad_maximum_fusion.1.refs_0_), channel_id=1, source_target_pairs={{0,64},{64,0},{1,65},{65,1},{2,66},{66,2},{3,67},{67,3},{4,68},{68... | collective-permute-start | bytes 1179656 | tf_op jit(solution)/shard_map/ppermute | solution.py:570
  13.0 6.2 %prepare.1 = (bf16[128,4096]{1,0:T(8,128)(2,1)}, bf16[128,4096]{1,0:T(8,128)(2,1)}, bf16[128,4096]{1,0:T(8,128)(2,1)}, bf16[128,4096]{1,0:T(8,128)(2,1)}, bf16[2...) custom-call(s32[5]{0:T(128)} %stack.35.meta.refs_6_.refs_3_, bf16[1024,8192]{1,0:T(8,128)(2,1)} %refs_3_.5, ...), custom_call_target="tpu_custom_call" | custom-call | flops 1 | bytes 1 | tf_op jit(solution)/shard_map/prepare/pallas_call | solution.py:87
  19.2 2.3 %collective-permute-done.refs_1_ = bf16[2,3,256,128]{3,2,1,0:T(8,128)(2,1)S(1)} collective-permute-done((bf16[2,3,256,128]{3,2,1,0:T(8,128)(2,1)S(1)}, bf16[2,3,256,128]{3,2,1,0:T(8,128)(2,1)S(1)}, u32[]{:S(2)}, u32[]{:S(2)}) %collective-permute-start) | collective-permute-done | bytes 393248 | tf_op jit(solution)/shard_map/ppermute | solution.py:570
  22.2 2.1 pad_maximum_fusion
  24.4 1.4 collective-permute-start.3
  25.7 2.5 %collective-permute-start.4 = (bf16[128,4096]{1,0:T(8,128)(2,1)}, bf16[128,4096]{1,0:T(8,128)(2,1)S(1)}, u32[]{:S(2)}, u32[]{:S(2)}) collective-permute-start(bf16[128,4096]{1,0:T(8,128)(2,1)} %get-tuple-element.85), channel_id=1, source_target_pairs={{0,68},{4,64},{64,4},{68,0},{1,69},{5,65},{65,5},{69,1},{2,70},{6,... | collective-permute-start | bytes 3145736 | tf_op jit(solution)/shard_map/ppermute | solution.py:577
  28.2 1.6 collective-permute-start.2
  29.8 1.7 collective-permute-start.1
  31.5 17.5 %collective-permute-done.3.refs_2_ = bf16[128,4096]{1,0:T(8,128)(2,1)S(1)} collective-permute-done((bf16[128,4096]{1,0:T(8,128)(2,1)}, bf16[128,4096]{1,0:T(8,128)(2,1)S(1)}, u32[]{:S(2)}, u32[]{:S(2)}) %collective-permute-start.3) | collective-permute-done | bytes 1048608 | tf_op jit(solution)/shard_map/ppermute | solution.py:578
  49.0 1.9 collective-permute-done.4.refs_3_
  50.9 2.3 %collective-permute-done.2.refs_1_ = bf16[2,256,1024]{2,1,0:T(8,128)(2,1)S(1)} collective-permute-done((bf16[2,256,1024]{2,1,0:T(8,128)(2,1)}, bf16[2,256,1024]{2,1,0:T(8,128)(2,1)S(1)}, u32[]{:S(2)}, u32[]{:S(2)}) %collective-permute-start.2) | collective-permute-done | bytes 1048608 | tf_op jit(solution)/shard_map/ppermute | solution.py:581
  56.1 2.2 collective-permute-start.7
  58.9 8.8 %own_product.4.refs_1_ = f32[2,256,1024]{2,1,0:T(8,128)} custom-call(s32[5]{0:T(128)} %stack.35.meta.refs_6_.refs_3_, bf16[2,256,1024]{2,1,0:T(8,128)(2,1)} %get-tuple-element.83.refs_0_.own, bf16[2,256,1024]{2,1,0:T(8,128)(2,1)} %get-tuple-element.89.refs_1_.above, bf16[2,256,1024]{2,1,0:T(8,128)(2,1)} %get-tuple-element.90.refs_2_.below, ...), custom_call_target="tpu_custom_call" | custom-call | flops 1 | bytes 1 | tf_op jit(solution)/shard_map/own_product/pallas_call | solution.py:151
  67.7 3.6 %pick.1 = (bf16[6,2,256,128]{3,2,1,0:T(8,128)(2,1)}, bf16[6,2,256,128]{3,2,1,0:T(8,128)(2,1)}) custom-call(s32[5]{0:T(128)} %stack.35.meta.refs_6_.refs_3_, s32[48]{0:T(128)} %reshape.12.parents, bf16[4,2,2,3,256,128]{5,4,3,2,1,0:T(8,128)(2,1)} %get-tuple-element.91.mine), custom_call_target="tpu_custom_call" | custom-call | flops 1 | bytes 1 | tf_op jit(solution)/shard_map/pick/pallas_call | solution.py:271
  72.0 2.0 collective-permute-done.5.other
  74.0 14.2 %probs.1 = (bf16[2,256,1024]{2,1,0:T(8,128)(2,1)}, bf16[2,512,1024]{2,1,0:T(8,128)(2,1)}, bf16[2,768,1024]{2,1,0:T(8,128)(2,1)}, bf16[2,1024,1024]{2,1,0:T(8,128)(2,1)}, bf16[6,2,256,128]{3,2,1,0:T(8,128)(2,1)}) custom-call(s32[5]{0:T(128)} %stack.35.meta.refs_6_.refs_3_, s32[48]{0:T(128)} %reshape.12.parents, s32[64]{0:T(128)} %reshape.13.lengths, ...), custom_call_target="tpu_custom_call" | custom-call | flops 1 | bytes 1 | tf_op jit(solution)/shard_map/probs/pallas_call | solution.py:337
  91.6 1.2 collective-permute-done.12.refs_4_
  92.8 3.2 %collective-permute-start.11 = (bf16[2,256,1024]{2,1,0:T(8,128)(2,1)}, bf16[2,256,1024]{2,1,0:T(8,128)(2,1)S(1)}, u32[]{:S(2)}, u32[]{:S(2)}) collective-permute-start(bf16[2,256,1024]{2,1,0:T(8,128)(2,1)} %get-tuple-element.103.refs_1_.above), channel_id=1, source_target_pairs={{0,3},{1,0},{2,1},{3,2},{4,7},{5,4},{6,5},{7,6},{8,11},{9,8},{10,9... | collective-permute-start | bytes 3145736 | tf_op jit(solution)/shard_map/ppermute | solution.py:598
  96.0 6.1 %own_product.5.refs_8_.own = f32[2,256,1024]{2,1,0:T(8,128)} custom-call(s32[5]{0:T(128)} %stack.35.meta.refs_6_.refs_3_, bf16[2,256,1024]{2,1,0:T(8,128)(2,1)} %get-tuple-element.104.refs_0_.across, bf16[1024,8192]{1,0:T(8,128)(2,1)} %refs_3_.5, f32[2,256,1024]{2,1,0:T(8,128)} %get-tuple-element.109.refs_2_, s32[5]{0:T(128)} %stack.35.meta.refs_6_.refs_3_), custom_call_target="tpu_custom_call" | custom-call | flops 1 | bytes 1 | tf_op jit(solution)/shard_map/own_product/pallas_call | solution.py:151
  103.5 1.0 copy-done.36
  104.5 9.8 %partner_product.2 = (bf16[8,256,128]{2,1,0:T(8,128)(2,1)}, bf16[8,256,128]{2,1,0:T(8,128)(2,1)}) custom-call(s32[5]{0:T(128)} %stack.35.meta.refs_6_.refs_3_, bf16[2,256,1024]{2,1,0:T(8,128)(2,1)} %get-tuple-element.83.refs_0_.own, bf16[2,256,1024]{2,1,0:T(8,128)(2,1)} %get-tuple-element.89.refs_1_.above, ...), custom_call_target="tpu_custom_call" | custom-call | flops 1 | bytes 1 | tf_op jit(solution)/shard_map/partner_product/pallas_call | solution.py:221
  115.3 1.1 collective-permute-start.19
  116.4 7.2 %own_product.6.refs_8_.refs_4_ = f32[2,256,1024]{2,1,0:T(8,128)} custom-call(s32[5]{0:T(128)} %stack.35.meta.refs_6_.refs_3_, bf16[2,256,1024]{2,1,0:T(8,128)(2,1)} %get-tuple-element.102.refs_0_.own, bf16[2,256,1024]{2,1,0:T(8,128)(2,1)} %get-tuple-element.103.refs_1_.above, bf16[1024,8192]{1,0:T(8,128)(2,1)} %refs_3_.5, bf16[1024,8192]{1,0:T(8,128)(2,1)} %refs_3_.5, ...), custom_call_target="tpu_custom_call" | custom-call | flops 1 | bytes 1 | tf_op jit(solution)/shard_map/own_product/pallas_call | solution.py:151
  125.6 9.8 %partner_product.3 = (bf16[8,256,128]{2,1,0:T(8,128)(2,1)}, bf16[8,256,128]{2,1,0:T(8,128)(2,1)}) custom-call(s32[5]{0:T(128)} %stack.35.meta.refs_6_.refs_3_, bf16[2,256,1024]{2,1,0:T(8,128)(2,1)} %get-tuple-element.102.refs_0_.own, bf16[2,256,1024]{2,1,0:T(8,128)(2,1)} %get-tuple-element.103.refs_1_.above, bf16[2,256,1024]{2,1,0:T(8,128)(2,1)} %copy-done.31, ...), custom_call_target="tpu_custom_call" | custom-call | flops 1 | bytes 1 | tf_op jit(solution)/shard_map/partner_product/pallas_call | solution.py:221
  136.2 10.0 %backward_3.1 = (bf16[4,1,256,1024]{3,2,1,0:T(8,128)(2,1)}, f32[2,256,128]{2,1,0:T(8,128)}, bf16[3,2,256,128]{3,2,1,0:T(8,128)(2,1)}) custom-call(s32[5]{0:T(128)} %stack.35.meta.refs_6_.refs_3_, s32[48]{0:T(128)} %reshape.12.parents, s32[64]{0:T(128)} %reshape.13.lengths, bf16[2,1024,1024]{2,1,0:T(8,128)(2,1)} %get-tuple-element.111.probs_ref, ...), custom_call_target="tpu_custom_call" | custom-call | flops 1 | bytes 1 | tf_op jit(solution)/shard_map/backward_3/pallas_call | solution.py:443
  147.3 7.9 %own_product.7.refs_2_.own = f32[2,256,1024]{2,1,0:T(8,128)} custom-call(s32[5]{0:T(128)} %stack.35.meta.refs_6_.refs_3_, bf16[2,256,1024]{2,1,0:T(8,128)(2,1)} %copy-done.31, bf16[2,256,1024]{2,1,0:T(8,128)(2,1)} %copy-done.32, bf16[1024,8192]{1,0:T(8,128)(2,1)} %refs_3_.5, bf16[1024,8192]{1,0:T(8,128)(2,1)} %refs_3_.5, ...), custom_call_target="tpu_custom_call" | custom-call | flops 1 | bytes 1 | tf_op jit(solution)/shard_map/own_product/pallas_call | solution.py:151
  155.2 1.6 copy-done.3
  159.2 8.4 %backward_2.1 = (bf16[4,1,256,1024]{3,2,1,0:T(8,128)(2,1)}, f32[2,256,128]{2,1,0:T(8,128)}, bf16[2,2,256,128]{3,2,1,0:T(8,128)(2,1)}) custom-call(s32[5]{0:T(128)} %stack.35.meta.refs_6_.refs_3_, s32[48]{0:T(128)} %reshape.12.parents, s32[64]{0:T(128)} %reshape.13.lengths, ...), custom_call_target="tpu_custom_call", output_to_operand_aliasing={{0}: (10, {})} | custom-call | flops 1 | bytes 1 | tf_op jit(solution)/shard_map/backward_2/pallas_call | solution.py:443
  167.8 1.1 collective-permute-start.17
  169.0 1.3 collective-permute-start.23
  170.3 1.9 collective-permute-start.24
  172.2 1.7 collective-permute-start.25
  173.9 1.6 copy-done
  176.4 1.3 spread_1.1
  179.2 6.9 %backward_1.1 = (bf16[4,1,256,1024]{3,2,1,0:T(8,128)(2,1)}, f32[2,256,128]{2,1,0:T(8,128)}, bf16[1,2,256,128]{3,2,1,0:T(8,128)(2,1)}) custom-call(s32[5]{0:T(128)} %stack.35.meta.refs_6_.refs_3_, s32[48]{0:T(128)} %reshape.12.parents, s32[64]{0:T(128)} %reshape.13.lengths, ...), custom_call_target="tpu_custom_call", output_to_operand_aliasing={{0}: (10, {})} | custom-call | flops 1 | bytes 1 | tf_op jit(solution)/shard_map/backward_1/pallas_call | solution.py:443
  186.2 2.5 %collective-permute-start.30 = (bf16[2,2,256,128]{3,2,1,0:T(8,128)(2,1)S(1)}, bf16[2,2,256,128]{3,2,1,0:T(8,128)(2,1)S(1)}, u32[]{:S(2)}, u32[]{:S(2)}) collective-permute-start(bf16[2,2,256,128]{3,2,1,0:T(8,128)(2,1)S(1)} %get-tuple-element.140), channel_id=1, source_target_pairs={{0,48},{16,0},{32,16},{48,32},{1,49},{17,1},{33,17},{49,33},{2,50}... | collective-permute-start | bytes 786440 | tf_op jit(solution)/shard_map/ppermute | solution.py:633
  189.4 1.6 copy-done.1
  191.9 1.7 spread_0.1
  194.7 2.9 %collective-permute-start.27 = (bf16[2,2,256,128]{3,2,1,0:T(8,128)(2,1)S(1)}, bf16[2,2,256,128]{3,2,1,0:T(8,128)(2,1)S(1)}, u32[]{:S(2)}, u32[]{:S(2)}) collective-permute-start(bf16[2,2,256,128]{3,2,1,0:T(8,128)(2,1)S(1)} %get-tuple-element.137), channel_id=1, source_target_pairs={{0,48},{16,0},{32,16},{48,32},{1,49},{17,1},{33,17},{49,33},{2,50}... | collective-permute-start | bytes 786440 | tf_op jit(solution)/shard_map/ppermute | solution.py:633
  197.6 1.7 collective-permute-start.28
  199.3 5.0 %backward_0.1 = (bf16[4,1,256,1024]{3,2,1,0:T(8,128)(2,1)}, f32[2,256,128]{2,1,0:T(8,128)}) custom-call(s32[5]{0:T(128)} %stack.35.meta.refs_6_.refs_3_, s32[48]{0:T(128)} %reshape.12.parents, s32[64]{0:T(128)} %reshape.13.lengths, bf16[2,256,1024]{2,1,0:T(8,128)(2,1)} %get-tuple-element.95.probs_ref, ...), custom_call_target="tpu_custom_call", output_to_operand_aliasing={{0}: (9, {})} | custom-call | flops 1 | bytes 1 | tf_op jit(solution)/shard_map/backward_0/pallas_call | solution.py:443
  204.4 2.3 %collective-permute-start.34 = (bf16[2,256,128]{2,1,0:T(8,128)(2,1)S(1)}, bf16[2,256,128]{2,1,0:T(8,128)(2,1)S(1)}, u32[]{:S(2)}, u32[]{:S(2)}) collective-permute-start(bf16[2,256,128]{2,1,0:T(8,128)(2,1)S(1)} %get-tuple-element.146), channel_id=1, source_target_pairs={{0,64},{64,0},{1,65},{65,1},{2,66},{66,2},{3,67},{67,3},{4,68},{68... | collective-permute-start | bytes 393224 | tf_op jit(solution)/shard_map/ppermute | solution.py:641
  206.7 1.6 copy-done.2
  209.0 1.4 collective-permute-start.33
  210.3 1.5 collective-permute-done.27.refs_2_
  212.5 2.3 %collective-permute-start.32 = (bf16[2,256,128]{2,1,0:T(8,128)(2,1)S(1)}, bf16[2,256,128]{2,1,0:T(8,128)(2,1)S(1)}, u32[]{:S(2)}, u32[]{:S(2)}) collective-permute-start(bf16[2,256,128]{2,1,0:T(8,128)(2,1)S(1)} %get-tuple-element.144), channel_id=1, source_target_pairs={{0,64},{64,0},{1,65},{65,1},{2,66},{66,2},{3,67},{67,3},{4,68},{68... | collective-permute-start | bytes 393224 | tf_op jit(solution)/shard_map/ppermute | solution.py:641
  215.5 3.6 %collective-permute-done.32.refs_5_ = bf16[2,256,128]{2,1,0:T(8,128)(2,1)S(1)} collective-permute-done((bf16[2,256,128]{2,1,0:T(8,128)(2,1)S(1)}, bf16[2,256,128]{2,1,0:T(8,128)(2,1)S(1)}, u32[]{:S(2)}, u32[]{:S(2)}) %collective-permute-start.32) | collective-permute-done | bytes 131104 | tf_op jit(solution)/shard_map/ppermute | solution.py:641
  (149 shorter events, 25.8 us)
Async XLA Ops:
  7.2 60.5 %all-gather.3.cloned.1.call-start = ((), (), s32[]{:S(2)}) async-start(), calls=%async_computation | async-start | bytes 3932160 | tf_op jit(solution)/shard_map/all_gather | solution.py:573
  8.3 10.9 %copy-start.37 = (bf16[2,3,256,128]{3,2,1,0:T(8,128)(2,1)}, bf16[2,3,256,128]{3,2,1,0:T(8,128)(2,1)S(1)}, u32[]{:S(2)}) copy-start(bf16[2,3,256,128]{3,2,1,0:T(8,128)(2,1)S(1)} %pad_maximum_fusion.1.refs_0_) | copy-start | bytes 1179652
  8.3 13.2 %collective-permute-start = (bf16[2,3,256,128]{3,2,1,0:T(8,128)(2,1)S(1)}, bf16[2,3,256,128]{3,2,1,0:T(8,128)(2,1)S(1)}, u32[]{:S(2)}, u32[]{:S(2)}) collective-permute-start(bf16[2,3,256,128]{3,2,1,0:T(8,128)(2,1)S(1)} %pad_maximum_fusion.1.refs_0_), channel_id=1, source_target_pairs={{0,64},{64,0},{1,65},{65,1},{2,66},{66,2},{3,67},{67,3},{4,68},{68... | collective-permute-start | bytes 1179656 | tf_op jit(solution)/shard_map/ppermute | solution.py:570
  24.4 24.6 %collective-permute-start.3 = (bf16[128,4096]{1,0:T(8,128)(2,1)}, bf16[128,4096]{1,0:T(8,128)(2,1)S(1)}, u32[]{:S(2)}, u32[]{:S(2)}) collective-permute-start(bf16[128,4096]{1,0:T(8,128)(2,1)} %get-tuple-element.84), channel_id=1, source_target_pairs={{0,4},{4,0},{1,5},{5,1},{2,6},{6,2},{3,7},{7,3},{8,12},{12,8},{9,1... | collective-permute-start | bytes 3145736 | tf_op jit(solution)/shard_map/ppermute | solution.py:578
  25.7 25.2 %collective-permute-start.4 = (bf16[128,4096]{1,0:T(8,128)(2,1)}, bf16[128,4096]{1,0:T(8,128)(2,1)S(1)}, u32[]{:S(2)}, u32[]{:S(2)}) collective-permute-start(bf16[128,4096]{1,0:T(8,128)(2,1)} %get-tuple-element.85), channel_id=1, source_target_pairs={{0,68},{4,64},{64,4},{68,0},{1,69},{5,65},{65,5},{69,1},{2,70},{6,... | collective-permute-start | bytes 3145736 | tf_op jit(solution)/shard_map/ppermute | solution.py:577
  28.2 24.9 %collective-permute-start.2 = (bf16[2,256,1024]{2,1,0:T(8,128)(2,1)}, bf16[2,256,1024]{2,1,0:T(8,128)(2,1)S(1)}, u32[]{:S(2)}, u32[]{:S(2)}) collective-permute-start(bf16[2,256,1024]{2,1,0:T(8,128)(2,1)} %get-tuple-element.83.refs_0_.own), channel_id=1, source_target_pairs={{0,1},{1,2},{2,3},{3,0},{4,5},{5,6},{6,7},{7,4},{8,9},{9,10},{10,1... | collective-permute-start | bytes 3145736 | tf_op jit(solution)/shard_map/ppermute | solution.py:581
  29.8 23.5 %collective-permute-start.1 = (bf16[2,256,1024]{2,1,0:T(8,128)(2,1)}, bf16[2,256,1024]{2,1,0:T(8,128)(2,1)}, u32[]{:S(2)}, u32[]{:S(2)}) collective-permute-start(bf16[2,256,1024]{2,1,0:T(8,128)(2,1)} %get-tuple-element.83.refs_0_.own), channel_id=1, source_target_pairs={{0,3},{1,0},{2,1},{3,2},{4,7},{5,4},{6,5},{7,6},{8,11},{9,8},{10,9... | collective-permute-start | bytes 3145736 | tf_op jit(solution)/shard_map/ppermute | solution.py:580
  54.2 34.0 %collective-permute-start.8 = (bf16[128,4096]{1,0:T(8,128)(2,1)}, bf16[128,4096]{1,0:T(8,128)(2,1)S(1)}, u32[]{:S(2)}, u32[]{:S(2)}) collective-permute-start(bf16[128,4096]{1,0:T(8,128)(2,1)} %get-tuple-element.99), channel_id=1, source_target_pairs={{0,4},{4,0},{1,5},{5,1},{2,6},{6,2},{3,7},{7,3},{8,12},{12,8},{9,1... | collective-permute-start | bytes 3145736 | tf_op jit(solution)/shard_map/ppermute | solution.py:578
  55.2 33.0 %collective-permute-start.9 = (bf16[128,4096]{1,0:T(8,128)(2,1)}, bf16[128,4096]{1,0:T(8,128)(2,1)S(1)}, u32[]{:S(2)}, u32[]{:S(2)}) collective-permute-start(bf16[128,4096]{1,0:T(8,128)(2,1)} %get-tuple-element.100), channel_id=1, source_target_pairs={{0,68},{4,64},{64,4},{68,0},{1,69},{5,65},{65,5},{69,1},{2,70},{6,... | collective-permute-start | bytes 3145736 | tf_op jit(solution)/shard_map/ppermute | solution.py:577
  56.1 32.2 %collective-permute-start.7 = (bf16[2,256,1024]{2,1,0:T(8,128)(2,1)}, bf16[2,256,1024]{2,1,0:T(8,128)(2,1)S(1)}, u32[]{:S(2)}, u32[]{:S(2)}) collective-permute-start(bf16[2,256,1024]{2,1,0:T(8,128)(2,1)} %get-tuple-element.96.refs_6_), channel_id=1, source_target_pairs={{0,3},{1,0},{2,1},{3,2},{4,7},{5,4},{6,5},{7,6},{8,11},{9,8},{10,9... | collective-permute-start | bytes 3145736 | tf_op jit(solution)/shard_map/ppermute | solution.py:587
  58.3 30.0 %collective-permute-start.6 = (bf16[2,256,1024]{2,1,0:T(8,128)(2,1)}, bf16[2,256,1024]{2,1,0:T(8,128)(2,1)}, u32[]{:S(2)}, u32[]{:S(2)}) collective-permute-start(bf16[2,256,1024]{2,1,0:T(8,128)(2,1)} %get-tuple-element.90.refs_2_.below), channel_id=1, source_target_pairs={{0,1},{1,2},{2,3},{3,0},{4,5},{5,6},{6,7},{7,4},{8,9},{9,10},{10,1... | collective-permute-start | bytes 3145736 | tf_op jit(solution)/shard_map/ppermute | solution.py:586
  71.3 2.7 %collective-permute-start.5 = (bf16[6,2,256,128]{3,2,1,0:T(8,128)(2,1)}, bf16[6,2,256,128]{3,2,1,0:T(8,128)(2,1)}, u32[]{:S(2)}, u32[]{:S(2)}) collective-permute-start(bf16[6,2,256,128]{3,2,1,0:T(8,128)(2,1)} %get-tuple-element.93), channel_id=1, source_target_pairs={{0,8},{8,0},{1,9},{9,1},{2,10},{10,2},{3,11},{11,3},{4,12},{12,4},... | collective-permute-start | bytes 2359304 | tf_op jit(solution)/shard_map/ppermute | solution.py:592
  89.9 2.9 %collective-permute-start.12 = (bf16[128,4096]{1,0:T(8,128)(2,1)}, bf16[128,4096]{1,0:T(8,128)(2,1)S(1)}, u32[]{:S(2)}, u32[]{:S(2)}) collective-permute-start(bf16[128,4096]{1,0:T(8,128)(2,1)} %get-tuple-element.105.refs_0_), channel_id=1, source_target_pairs={{0,8},{8,0},{1,9},{9,1},{2,10},{10,2},{3,11},{11,3},{4,12},{12,4},... | collective-permute-start | bytes 3145736 | tf_op jit(solution)/shard_map/ppermute | solution.py:600
  90.0 12.1 %collective-permute-start.13 = (bf16[128,4096]{1,0:T(8,128)(2,1)}, bf16[128,4096]{1,0:T(8,128)(2,1)S(1)}, u32[]{:S(2)}, u32[]{:S(2)}) collective-permute-start(bf16[128,4096]{1,0:T(8,128)(2,1)} %get-tuple-element.106.refs_1_), channel_id=1, source_target_pairs={{0,8},{8,0},{1,9},{9,1},{2,10},{10,2},{3,11},{11,3},{4,12},{12,4},... | collective-permute-start | bytes 3145736 | tf_op jit(solution)/shard_map/ppermute | solution.py:600
  90.4 11.8 %collective-permute-start.14 = (bf16[128,4096]{1,0:T(8,128)(2,1)}, bf16[128,4096]{1,0:T(8,128)(2,1)S(1)}, u32[]{:S(2)}, u32[]{:S(2)}) collective-permute-start(bf16[128,4096]{1,0:T(8,128)(2,1)} %get-tuple-element.107.refs_2_), channel_id=1, source_target_pairs={{0,8},{8,0},{1,9},{9,1},{2,10},{10,2},{3,11},{11,3},{4,12},{12,4},... | collective-permute-start | bytes 3145736 | tf_op jit(solution)/shard_map/ppermute | solution.py:600
  90.5 11.7 %collective-permute-start.15 = (bf16[128,4096]{1,0:T(8,128)(2,1)}, bf16[128,4096]{1,0:T(8,128)(2,1)S(1)}, u32[]{:S(2)}, u32[]{:S(2)}) collective-permute-start(bf16[128,4096]{1,0:T(8,128)(2,1)} %get-tuple-element.108.refs_3_), channel_id=1, source_target_pairs={{0,8},{8,0},{1,9},{9,1},{2,10},{10,2},{3,11},{11,3},{4,12},{12,4},... | collective-permute-start | bytes 3145736 | tf_op jit(solution)/shard_map/ppermute | solution.py:600
  90.9 32.7 %collective-permute-start.10 = (bf16[2,256,1024]{2,1,0:T(8,128)(2,1)}, bf16[2,256,1024]{2,1,0:T(8,128)(2,1)S(1)}, u32[]{:S(2)}, u32[]{:S(2)}) collective-permute-start(bf16[2,256,1024]{2,1,0:T(8,128)(2,1)} %get-tuple-element.102.refs_0_.own), channel_id=1, source_target_pairs={{0,1},{1,2},{2,3},{3,0},{4,5},{5,6},{6,7},{7,4},{8,9},{9,10},{10,1... | collective-permute-start | bytes 3145736 | tf_op jit(solution)/shard_map/ppermute | solution.py:597
  92.8 30.9 %collective-permute-start.11 = (bf16[2,256,1024]{2,1,0:T(8,128)(2,1)}, bf16[2,256,1024]{2,1,0:T(8,128)(2,1)S(1)}, u32[]{:S(2)}, u32[]{:S(2)}) collective-permute-start(bf16[2,256,1024]{2,1,0:T(8,128)(2,1)} %get-tuple-element.103.refs_1_.above), channel_id=1, source_target_pairs={{0,3},{1,0},{2,1},{3,2},{4,7},{5,4},{6,5},{7,6},{8,11},{9,8},{10,9... | collective-permute-start | bytes 3145736 | tf_op jit(solution)/shard_map/ppermute | solution.py:598
  114.3 21.0 %collective-permute-start.16 = (bf16[8,256,128]{2,1,0:T(8,128)(2,1)}, bf16[8,256,128]{2,1,0:T(8,128)(2,1)S(1)}, u32[]{:S(2)}, u32[]{:S(2)}) collective-permute-start(bf16[8,256,128]{2,1,0:T(8,128)(2,1)} %get-tuple-element.112), channel_id=1, source_target_pairs={{0,4},{4,0},{1,5},{5,1},{2,6},{6,2},{3,7},{7,3},{8,12},{12,8},{9,1... | collective-permute-start | bytes 1572872 | tf_op jit(solution)/shard_map/ppermute | solution.py:606
  115.3 43.1 %collective-permute-start.19 = (bf16[8,256,128]{2,1,0:T(8,128)(2,1)}, bf16[8,256,128]{2,1,0:T(8,128)(2,1)S(1)}, u32[]{:S(2)}, u32[]{:S(2)}) collective-permute-start(bf16[8,256,128]{2,1,0:T(8,128)(2,1)} %get-tuple-element.110.refs_4_), channel_id=1, source_target_pairs={{0,4},{4,0},{1,5},{5,1},{2,6},{6,2},{3,7},{7,3},{8,12},{12,8},{9,1... | collective-permute-start | bytes 1572872 | tf_op jit(solution)/shard_map/ppermute | solution.py:606
  136.2 10.1 %copy-start.46 = (bf16[8,256,128]{2,1,0:T(8,128)(2,1)S(1)}, bf16[8,256,128]{2,1,0:T(8,128)(2,1)}, u32[]{:S(2)}) copy-start(bf16[8,256,128]{2,1,0:T(8,128)(2,1)} %get-tuple-element.117) | copy-start | bytes 1572868
  146.3 8.9 %collective-permute-start.20 = (bf16[3,2,256,128]{3,2,1,0:T(8,128)(2,1)}, bf16[3,2,256,128]{3,2,1,0:T(8,128)(2,1)S(1)}, u32[]{:S(2)}, u32[]{:S(2)}) collective-permute-start(bf16[3,2,256,128]{3,2,1,0:T(8,128)(2,1)} %get-tuple-element.119.refs_0_.refs_2_.refs_4_), channel_id=1, source_target_pairs={{0,8},{8,0},{1,9},{9,1},{2,10},{10,2},{3,11},{11,3},{4,12},{12,4},... | collective-permute-start | bytes 1179656 | tf_op jit(solution)/shard_map/ppermute | solution.py:625
  146.3 32.1 %collective-permute-start.18 = (bf16[8,256,128]{2,1,0:T(8,128)(2,1)S(1)}, bf16[8,256,128]{2,1,0:T(8,128)(2,1)S(1)}, u32[]{:S(2)}, u32[]{:S(2)}) collective-permute-start(bf16[8,256,128]{2,1,0:T(8,128)(2,1)S(1)} %copy-done.46), channel_id=1, source_target_pairs={{0,4},{4,0},{1,5},{5,1},{2,6},{6,2},{3,7},{7,3},{8,12},{12,8},{9,1... | collective-permute-start | bytes 1572872 | tf_op jit(solution)/shard_map/ppermute | solution.py:606
  159.2 14.7 %copy-start.18 = (s32[5]{0:T(128)S(1)}, s32[5]{0:T(128)}, u32[]{:S(2)}) copy-start(s32[5]{0:T(128)} %stack.35.meta.refs_6_.refs_3_) | copy-start | bytes 64
  159.2 14.7 %copy-start.23 = (s32[48]{0:T(128)S(1)}, s32[48]{0:T(128)}, u32[]{:S(2)}) copy-start(s32[48]{0:T(128)} %reshape.12.parents) | copy-start | bytes 580
  167.6 4.6 %collective-permute-start.21 = (bf16[2,2,256,128]{3,2,1,0:T(8,128)(2,1)}, bf16[2,2,256,128]{3,2,1,0:T(8,128)(2,1)S(1)}, u32[]{:S(2)}, u32[]{:S(2)}) collective-permute-start(bf16[2,2,256,128]{3,2,1,0:T(8,128)(2,1)} %get-tuple-element.122.refs_0_.refs_2_), channel_id=1, source_target_pairs={{0,8},{8,0},{1,9},{9,1},{2,10},{10,2},{3,11},{11,3},{4,12},{12,4},... | collective-permute-start | bytes 786440 | tf_op jit(solution)/shard_map/ppermute | solution.py:625
  167.8 26.9 %collective-permute-start.17 = (bf16[8,256,128]{2,1,0:T(8,128)(2,1)S(1)}, bf16[8,256,128]{2,1,0:T(8,128)(2,1)S(1)}, u32[]{:S(2)}, u32[]{:S(2)}) collective-permute-start(bf16[8,256,128]{2,1,0:T(8,128)(2,1)S(1)} %copy-done.38), channel_id=1, source_target_pairs={{0,4},{4,0},{1,5},{5,1},{2,6},{6,2},{3,7},{7,3},{8,12},{12,8},{9,1... | collective-permute-start | bytes 1572872 | tf_op jit(solution)/shard_map/ppermute | solution.py:606
  169.0 17.2 %collective-permute-start.23 = (bf16[2,2,256,128]{3,2,1,0:T(8,128)(2,1)S(1)}, bf16[2,2,256,128]{3,2,1,0:T(8,128)(2,1)S(1)}, u32[]{:S(2)}, u32[]{:S(2)}) collective-permute-start(bf16[2,2,256,128]{3,2,1,0:T(8,128)(2,1)S(1)} %get-tuple-element.126), channel_id=1, source_target_pairs={{0,16},{16,32},{32,48},{48,0},{1,17},{17,33},{33,49},{49,1},{2,18}... | collective-permute-start | bytes 786440 | tf_op jit(solution)/shard_map/ppermute | solution.py:632
  170.3 16.0 %collective-permute-start.24 = (bf16[2,2,256,128]{3,2,1,0:T(8,128)(2,1)S(1)}, bf16[2,2,256,128]{3,2,1,0:T(8,128)(2,1)S(1)}, u32[]{:S(2)}, u32[]{:S(2)}) collective-permute-start(bf16[2,2,256,128]{3,2,1,0:T(8,128)(2,1)S(1)} %get-tuple-element.127), channel_id=1, source_target_pairs={{0,48},{16,0},{32,16},{48,32},{1,49},{17,1},{33,17},{49,33},{2,50}... | collective-permute-start | bytes 786440 | tf_op jit(solution)/shard_map/ppermute | solution.py:633
  172.2 16.6 %collective-permute-start.25 = (bf16[2,2,256,128]{3,2,1,0:T(8,128)(2,1)S(1)}, bf16[2,2,256,128]{3,2,1,0:T(8,128)(2,1)S(1)}, u32[]{:S(2)}, u32[]{:S(2)}) collective-permute-start(bf16[2,2,256,128]{3,2,1,0:T(8,128)(2,1)S(1)} %get-tuple-element.128), channel_id=1, source_target_pairs={{0,32},{16,48},{32,0},{48,16},{1,33},{17,49},{33,1},{49,17},{2,34}... | collective-permute-start | bytes 786440 | tf_op jit(solution)/shard_map/ppermute | solution.py:634
  178.5 19.2 %collective-permute-start.29 = (bf16[2,2,256,128]{3,2,1,0:T(8,128)(2,1)S(1)}, bf16[2,2,256,128]{3,2,1,0:T(8,128)(2,1)S(1)}, u32[]{:S(2)}, u32[]{:S(2)}) collective-permute-start(bf16[2,2,256,128]{3,2,1,0:T(8,128)(2,1)S(1)} %get-tuple-element.139), channel_id=1, source_target_pairs={{0,16},{16,32},{32,48},{48,0},{1,17},{17,33},{33,49},{49,1},{2,18}... | collective-permute-start | bytes 786440 | tf_op jit(solution)/shard_map/ppermute | solution.py:632
  179.2 10.2 %copy-start.12 = (bf16[2,2,256,128]{3,2,1,0:T(8,128)(2,1)S(1)}, bf16[2,2,256,128]{3,2,1,0:T(8,128)(2,1)}, u32[]{:S(2)}) copy-start(bf16[2,2,256,128]{3,2,1,0:T(8,128)(2,1)} %copy-done.11) | copy-start | bytes 786436
  179.2 10.2 %copy-start.19 = (s32[5]{0:T(128)S(1)}, s32[5]{0:T(128)}, u32[]{:S(2)}) copy-start(s32[5]{0:T(128)} %stack.35.meta.refs_6_.refs_3_) | copy-start | bytes 64
  179.2 12.5 %copy-start.6 = (bf16[2,2,256,128]{3,2,1,0:T(8,128)(2,1)S(1)}, bf16[2,2,256,128]{3,2,1,0:T(8,128)(2,1)}, u32[]{:S(2)}) copy-start(bf16[2,2,256,128]{3,2,1,0:T(8,128)(2,1)} %get-tuple-element.122.refs_0_.refs_2_) | copy-start | bytes 786436
  186.1 5.6 %collective-permute-start.22 = (bf16[1,2,256,128]{3,2,1,0:T(8,128)(2,1)}, bf16[1,2,256,128]{3,2,1,0:T(8,128)(2,1)S(1)}, u32[]{:S(2)}, u32[]{:S(2)}) collective-permute-start(bf16[1,2,256,128]{3,2,1,0:T(8,128)(2,1)} %get-tuple-element.125.refs_0_), channel_id=1, source_target_pairs={{0,8},{8,0},{1,9},{9,1},{2,10},{10,2},{3,11},{11,3},{4,12},{12,4},... | collective-permute-start | bytes 393224 | tf_op jit(solution)/shard_map/ppermute | solution.py:625
  186.2 18.1 %collective-permute-start.30 = (bf16[2,2,256,128]{3,2,1,0:T(8,128)(2,1)S(1)}, bf16[2,2,256,128]{3,2,1,0:T(8,128)(2,1)S(1)}, u32[]{:S(2)}, u32[]{:S(2)}) collective-permute-start(bf16[2,2,256,128]{3,2,1,0:T(8,128)(2,1)S(1)} %get-tuple-element.140), channel_id=1, source_target_pairs={{0,48},{16,0},{32,16},{48,32},{1,49},{17,1},{33,17},{49,33},{2,50}... | collective-permute-start | bytes 786440 | tf_op jit(solution)/shard_map/ppermute | solution.py:633
  188.8 17.9 %collective-permute-start.31 = (bf16[2,2,256,128]{3,2,1,0:T(8,128)(2,1)S(1)}, bf16[2,2,256,128]{3,2,1,0:T(8,128)(2,1)S(1)}, u32[]{:S(2)}, u32[]{:S(2)}) collective-permute-start(bf16[2,2,256,128]{3,2,1,0:T(8,128)(2,1)S(1)} %get-tuple-element.141), channel_id=1, source_target_pairs={{0,32},{16,48},{32,0},{48,16},{1,33},{17,49},{33,1},{49,17},{2,34}... | collective-permute-start | bytes 786440 | tf_op jit(solution)/shard_map/ppermute | solution.py:634
  194.4 15.9 %collective-permute-start.26 = (bf16[2,2,256,128]{3,2,1,0:T(8,128)(2,1)S(1)}, bf16[2,2,256,128]{3,2,1,0:T(8,128)(2,1)S(1)}, u32[]{:S(2)}, u32[]{:S(2)}) collective-permute-start(bf16[2,2,256,128]{3,2,1,0:T(8,128)(2,1)S(1)} %get-tuple-element.136), channel_id=1, source_target_pairs={{0,16},{16,32},{32,48},{48,0},{1,17},{17,33},{33,49},{49,1},{2,18}... | collective-permute-start | bytes 786440 | tf_op jit(solution)/shard_map/ppermute | solution.py:632
  194.7 17.1 %collective-permute-start.27 = (bf16[2,2,256,128]{3,2,1,0:T(8,128)(2,1)S(1)}, bf16[2,2,256,128]{3,2,1,0:T(8,128)(2,1)S(1)}, u32[]{:S(2)}, u32[]{:S(2)}) collective-permute-start(bf16[2,2,256,128]{3,2,1,0:T(8,128)(2,1)S(1)} %get-tuple-element.137), channel_id=1, source_target_pairs={{0,48},{16,0},{32,16},{48,32},{1,49},{17,1},{33,17},{49,33},{2,50}... | collective-permute-start | bytes 786440 | tf_op jit(solution)/shard_map/ppermute | solution.py:633
  197.6 14.2 %collective-permute-start.28 = (bf16[2,2,256,128]{3,2,1,0:T(8,128)(2,1)S(1)}, bf16[2,2,256,128]{3,2,1,0:T(8,128)(2,1)S(1)}, u32[]{:S(2)}, u32[]{:S(2)}) collective-permute-start(bf16[2,2,256,128]{3,2,1,0:T(8,128)(2,1)S(1)} %get-tuple-element.138), channel_id=1, source_target_pairs={{0,32},{16,48},{32,0},{48,16},{1,33},{17,49},{33,1},{49,17},{2,34}... | collective-permute-start | bytes 786440 | tf_op jit(solution)/shard_map/ppermute | solution.py:634
  199.3 12.5 %copy-start.8 = (bf16[2,2,256,128]{3,2,1,0:T(8,128)(2,1)S(1)}, bf16[2,2,256,128]{3,2,1,0:T(8,128)(2,1)}, u32[]{:S(2)}) copy-start(bf16[2,2,256,128]{3,2,1,0:T(8,128)(2,1)} %copy-done.7) | copy-start | bytes 786436
  204.4 10.4 %collective-permute-start.34 = (bf16[2,256,128]{2,1,0:T(8,128)(2,1)S(1)}, bf16[2,256,128]{2,1,0:T(8,128)(2,1)S(1)}, u32[]{:S(2)}, u32[]{:S(2)}) collective-permute-start(bf16[2,256,128]{2,1,0:T(8,128)(2,1)S(1)} %get-tuple-element.146), channel_id=1, source_target_pairs={{0,64},{64,0},{1,65},{65,1},{2,66},{66,2},{3,67},{67,3},{4,68},{68... | collective-permute-start | bytes 393224 | tf_op jit(solution)/shard_map/ppermute | solution.py:641
  208.3 10.8 %copy-start.13 = (f32[2,256,128]{2,1,0:T(8,128)S(1)}, f32[2,256,128]{2,1,0:T(8,128)}, u32[]{:S(2)}) copy-start(f32[2,256,128]{2,1,0:T(8,128)} %get-tuple-element.135.refs_3_) | copy-start | bytes 786436
  208.3 10.8 %copy-start.14 = (f32[2,256,128]{2,1,0:T(8,128)S(1)}, f32[2,256,128]{2,1,0:T(8,128)}, u32[]{:S(2)}) copy-start(f32[2,256,128]{2,1,0:T(8,128)} %get-tuple-element.134.refs_2_) | copy-start | bytes 786436
  208.3 10.8 %copy-start.15 = (f32[2,256,128]{2,1,0:T(8,128)S(1)}, f32[2,256,128]{2,1,0:T(8,128)}, u32[]{:S(2)}) copy-start(f32[2,256,128]{2,1,0:T(8,128)} %get-tuple-element.133.refs_1_) | copy-start | bytes 786436
  208.3 10.8 %copy-start.16 = (f32[2,256,128]{2,1,0:T(8,128)S(1)}, f32[2,256,128]{2,1,0:T(8,128)}, u32[]{:S(2)}) copy-start(f32[2,256,128]{2,1,0:T(8,128)} %get-tuple-element.132.refs_0_) | copy-start | bytes 786436
  209.0 6.6 %collective-permute-start.33 = (bf16[2,256,128]{2,1,0:T(8,128)(2,1)S(1)}, bf16[2,256,128]{2,1,0:T(8,128)(2,1)S(1)}, u32[]{:S(2)}, u32[]{:S(2)}) collective-permute-start(bf16[2,256,128]{2,1,0:T(8,128)(2,1)S(1)} %get-tuple-element.145), channel_id=1, source_target_pairs={{0,64},{64,0},{1,65},{65,1},{2,66},{66,2},{3,67},{67,3},{4,68},{68... | collective-permute-start | bytes 393224 | tf_op jit(solution)/shard_map/ppermute | solution.py:641
  212.5 6.6 %collective-permute-start.32 = (bf16[2,256,128]{2,1,0:T(8,128)(2,1)S(1)}, bf16[2,256,128]{2,1,0:T(8,128)(2,1)S(1)}, u32[]{:S(2)}, u32[]{:S(2)}) collective-permute-start(bf16[2,256,128]{2,1,0:T(8,128)(2,1)S(1)} %get-tuple-element.144), channel_id=1, source_target_pairs={{0,64},{64,0},{1,65},{65,1},{2,66},{66,2},{3,67},{67,3},{4,68},{68... | collective-permute-start | bytes 393224 | tf_op jit(solution)/shard_map/ppermute | solution.py:641
  (35 other events, 104.9 us)
Sparse Core Ops, SparseCore 0:
  24.5 41.2 all-gather.2

commit v2 on v1

--- a/solution.py
+++ b/solution.py
@@ -23,13 +23,21 @@
 NT = (((1,), (1,)), ((), ()))
 PARAMS = pltpu.CompilerParams(vmem_limit_bytes=56 * 2**20)
 SMALL = pltpu.CompilerParams(vmem_limit_bytes=16 * 2**20)
+LIGHT = pltpu.CompilerParams(vmem_limit_bytes=24 * 2**20)
+LARGE = pltpu.CompilerParams(vmem_limit_bytes=48 * 2**20)
+MIDDLE = pltpu.CompilerParams(vmem_limit_bytes=32 * 2**20)
 ANY = pl.BlockSpec(memory_space=pltpu.HBM)
+FREE = pl.BlockSpec(memory_space=pl.ANY)
 AXES = ("zh", "x", "c")
 ALT = [(0, 3), (1, 2), (2, 1), (3, 0)]
 SWAP = [(0, 1), (1, 0)]
 UP = [(i, (i + 1) % 4) for i in range(4)]
 DOWN = [(i, (i + 3) % 4) for i in range(4)]
 ACROSS = [(i, (i + 2) % 4) for i in range(4)]
+
+
+TOKEN = pl.BlockSpec((8, HD), lambda *_: (0, 0))
+TOKEN_SHAPE = jax.ShapeDtypeStruct((8, HD), jnp.float32)
 
 
 def cost(flops, size, exps=0):
@@ -134,7 +142,8 @@
     ).reshape(2, SEG, ROWS)
     if added:
         total += refs[0][...]
-    refs[-1][...] = total
+    refs[-2][...] = total.astype(refs[-2].dtype)
+    refs[-1][...] = jnp.zeros(TOKEN_SHAPE.shape, jnp.float32)
 
 
 def feature_spec(step):
@@ -144,7 +153,7 @@
     return pl.BlockSpec((ROWS, FEATURES), index)
 
 
-def blocks_product(meta, cots, steps, weight, earlier, token):
+def blocks_product(meta, cots, steps, weight, earlier, dtype, token):
     count = len(cots)
     whole = pl.BlockSpec((2, SEG, FEATURES), lambda n, *_: (0, 0, 0))
     part = pl.BlockSpec((2, SEG, ROWS), lambda n, *_: (0, 0, n))
@@ -157,10 +166,10 @@
             + [feature_spec(step) for step in steps]
             + [part] * len(earlier)
             + [ANY],
-            out_specs=part,
+            out_specs=[part, TOKEN],
         ),
-        out_shape=jax.ShapeDtypeStruct((2, SEG, FEATURES), jnp.float32),
-        compiler_params=PARAMS,
+        out_shape=[jax.ShapeDtypeStruct((2, SEG, FEATURES), dtype), TOKEN_SHAPE],
+        compiler_params=LARGE,
         cost_estimate=cost(count * SEG * 1024 * HALF, 2 * 1024 * HALF),
         name="own_product",
     )(meta, *cots, *[weight] * count, *earlier, token)
@@ -168,7 +177,7 @@
 
 def product_kernel(meta, own, above, below, across, *refs):
     weights, refs = refs[:8], refs[8:]
-    outs, (cots, held, cot_sems, sems) = refs[1:3], refs[3:]
+    outs, token, (cots, held, cot_sems, sems) = refs[1:3], refs[3], refs[4:]
     step = pl.program_id(0)
 
     def place(source, offset, sem, rows):
@@ -208,6 +217,7 @@
             for move in blocks[q]:
                 move.wait()
 
+    token[...] = jnp.zeros(TOKEN_SHAPE.shape, jnp.float32)
     total = lax.dot_general(cots[...], held[step], NT, preferred_element_type=jnp.float32)
     for i in range(2):
         part = total[i * SEG : (i + 1) * SEG]
@@ -216,14 +226,14 @@
 
 
 def product(meta, cots, weights, token):
-    out_shape = [jax.ShapeDtypeStruct((8, SEG, PIECE), jnp.bfloat16)] * 2
-    out_specs = [pl.BlockSpec((2, SEG, PIECE), lambda q, *_: (q, 0, 0))] * 2
+    out_shape = [jax.ShapeDtypeStruct((8, SEG, PIECE), jnp.bfloat16)] * 2 + [TOKEN_SHAPE]
+    out_specs = [pl.BlockSpec((2, SEG, PIECE), lambda q, *_: (q, 0, 0))] * 2 + [TOKEN]
     return pl.pallas_call(
         product_kernel,
         grid_spec=pltpu.PrefetchScalarGridSpec(
             num_scalar_prefetch=1,
             grid=(4,),
-            in_specs=[ANY] * (5 + len(weights)),
+            in_specs=[FREE] * 4 + [ANY] * 4 + [FREE] * 4 + [ANY],
             out_specs=out_specs,
             scratch_shapes=[
                 pltpu.VMEM((2 * SEG, HALF), jnp.bfloat16),
@@ -233,7 +243,7 @@
             ],
         ),
         out_shape=out_shape,
-        compiler_params=PARAMS,
+        compiler_params=LIGHT,
         cost_estimate=cost(4 * SEG * 1024 * HALF, 2 * 1024 * HALF + 8 * SEG * 1024),
         name="partner_product",
     )(meta, *cots, *weights, token)
@@ -284,14 +294,19 @@
     )(meta, parents, mine)
 
 
-def probs_kernel(meta, parents, lengths, query, own_key, mine, other, *refs):
-    outs, picked, sems = refs[1:5], refs[5], refs[6]
+def probs_kernel(levels, meta, parents, lengths, query, own_key, own_value, *refs):
+    count = len(levels)
     me = node_id(meta)
-
-    @pl.when(pl.program_id(0) == 0)
+    if levels != (0,):
+        (mine, other), refs = refs[:2], refs[2:]
+        picked, sems = refs[-2:]
+    refs = refs[1:]
+    outs, averages, inverses = refs[:count], refs[count : 2 * count], refs[2 * count]
+
+    @pl.when((pl.program_id(0) == 0) & (levels != (0,)))
     def _():
         copies = []
-        for i, (level, m) in enumerate(PAIRS):
+        for i, (level, m) in enumerate(PAIRS if levels != (0,) else []):
             c = relative(meta, ancestor(parents, me, level, m))[0]
             for part in range(2):
                 pair = [
@@ -306,7 +321,7 @@
         for copy in copies:
             copy.wait()
 
-    for level in reversed(range(LEVELS)):
+    for k, level in enumerate(levels):
         q = jnp.concatenate(
             [query[level, 0, :, i * HD : (i + 1) * HD] for i in range(BATCH)], axis=0
         )
@@ -326,52 +341,69 @@
         )
         exps = [jnp.exp2((s - top) * EXP2_SCALE) for s in blocks]
         inverse = 1.0 / sum(jnp.sum(e, axis=0, keepdims=True) for e in exps)
+        average = jnp.zeros((HD, BATCH * SEG), jnp.float32)
         for m in range(level + 1):
-            outs[level][0, m * SEG : (m + 1) * SEG] = (exps[m] * inverse).astype(jnp.bfloat16)
-
-
-def probs(meta, parents, lengths, queries, key_rows, mine, other, token):
+            narrow = exps[m].astype(jnp.bfloat16)
+            outs[k][0, m * SEG : (m + 1) * SEG] = narrow
+            value = picked[pair_index(level, m), 1] if m < level else own_value[level, 0]
+            average += jnp.dot(
+                value.astype(jnp.float32).T.astype(jnp.bfloat16),
+                narrow,
+                preferred_element_type=jnp.float32,
+            )
+        averages[k][...] = average * inverse
+        inverses[level : level + 1] = inverse
+
+
+def probs(levels, meta, parents, lengths, queries, key_rows, value_rows, gathered, token):
     width = BATCH * HD
-    counts = [(level + 1) * SEG for level in range(LEVELS)]
-    total = sum(counts)
-    return pl.pallas_call(
-        probs_kernel,
+    counts = [(level + 1) * SEG for level in levels]
+    picked = (len(PAIRS), 2, SEG, HD)
+    out_specs = [
+        pl.BlockSpec((1, count, BATCH * SEG), lambda h, *_: (h, 0, 0)) for count in counts
+    ]
+    out_shape = [
+        jax.ShapeDtypeStruct((GROUP // BATCH, count, BATCH * SEG), jnp.bfloat16)
+        for count in counts
+    ]
+    out_specs += [pl.BlockSpec((HD, BATCH * SEG), lambda h, *_: (0, h))] * len(levels)
+    out_shape += [jax.ShapeDtypeStruct((HD, GROUP * SEG), jnp.float32)] * len(levels)
+    out_specs.append(pl.BlockSpec((8, BATCH * SEG), lambda h, *_: (0, h)))
+    out_shape.append(jax.ShapeDtypeStruct((8, GROUP * SEG), jnp.float32))
+    scratch = []
+    if gathered:
+        out_specs.append(pl.BlockSpec(picked, lambda h, *_: (0, 0, 0, 0)))
+        out_shape.append(jax.ShapeDtypeStruct(picked, jnp.bfloat16))
+        scratch.append(pltpu.SemaphoreType.DMA((len(PAIRS), 2)))
+    own = pl.BlockSpec((LEVELS, 1, SEG, HD), lambda h, *_: (0, 0, 0, 0))
+    return pl.pallas_call(
+        functools.partial(probs_kernel, levels),
         grid_spec=pltpu.PrefetchScalarGridSpec(
             num_scalar_prefetch=3,
             grid=(GROUP // BATCH,),
             in_specs=[
                 pl.BlockSpec((LEVELS, 1, SEG, width), lambda h, *_: (0, 0, 0, h)),
-                pl.BlockSpec((LEVELS, 1, SEG, HD), lambda h, *_: (0, 0, 0, 0)),
-                ANY,
-                ANY,
-                ANY,
+                own,
+                own,
+                *[ANY] * (len(gathered) + 1),
             ],
-            out_specs=[
-                pl.BlockSpec((1, count, BATCH * SEG), lambda h, *_: (h, 0, 0))
-                for count in counts
-            ]
-            + [pl.BlockSpec((len(PAIRS), 2, SEG, HD), lambda h, *_: (0, 0, 0, 0))],
-            scratch_shapes=[pltpu.SemaphoreType.DMA((len(PAIRS), 2))],
+            out_specs=out_specs,
+            scratch_shapes=scratch,
         ),
-        out_shape=[
-            jax.ShapeDtypeStruct((GROUP // BATCH, count, BATCH * SEG), jnp.bfloat16)
-            for count in counts
-        ]
-        + [jax.ShapeDtypeStruct((len(PAIRS), 2, SEG, HD), jnp.bfloat16)],
+        out_shape=out_shape,
         compiler_params=PARAMS,
-        cost_estimate=cost(
-            2 * GROUP * total * SEG * HD, 2 * GROUP * total * SEG, GROUP * total * SEG
-        ),
+        cost_estimate=cost(0, 0),
         name="probs",
-    )(meta, parents, lengths, queries, key_rows, mine, other, token)
+    )(meta, parents, lengths, queries, key_rows, value_rows, *gathered, token)
 
 
 def backward_kernel(
-    level, meta, parents, lengths, probs_ref, query, own, partner, own_key, own_value, *refs
+    level, arrived, meta, parents, lengths, probs_ref, average, inverse, query, own, partner, own_key,
+    own_value, *refs
 ):
     if level:
         picked, refs = refs[0], refs[1:]
-    refs = refs[2:]
+    refs = refs[2 + arrived :]
     if level:
         query_out, own_out, ancestor_out, flipped, key_total, value_total = refs
     else:
@@ -389,25 +421,26 @@
             flipped[:, blocks[m]] = key.astype(jnp.float32).T.astype(jnp.bfloat16)
 
     length = lengths[level * NODES + node_id(meta)]
-    valid = lax.broadcasted_iota(jnp.int32, (SEG, HD), 0) < length
     heads = []
     for i in range(BATCH):
-        head = step * BATCH + i
         piece = lax.rem(step + meta[2], 2) * 4 + i
-        total = own[0, :, i * HD : (i + 1) * HD] + partner[piece].astype(jnp.float32)
-        heads.append(jnp.where(valid, total, 0.0).astype(jnp.bfloat16))
-    dout = jnp.concatenate(heads, axis=0)
+        total = own[0, :, i * HD : (i + 1) * HD].astype(jnp.float32)
+        total += partner[piece].astype(jnp.float32)
+        heads.append(total.astype(jnp.bfloat16).astype(jnp.float32).T)
+    dout = jnp.concatenate(heads, axis=1)
+    position = lax.broadcasted_iota(jnp.int32, dout.shape, 1) & (SEG - 1)
+    dout = jnp.where(position < length, dout, 0.0) * inverse[level : level + 1]
+    dout = dout.astype(jnp.bfloat16)
+    delta = jnp.sum(dout.astype(jnp.float32) * average[...], axis=0, keepdims=True)
     q = jnp.concatenate([query[0, 0, :, i * HD : (i + 1) * HD] for i in range(BATCH)], axis=0)
     value = jnp.concatenate(
         [picked[first + m, 1] for m in range(level)] + [own_value[0, 0]], axis=0
     )
     narrow = probs_ref[0]
-    wide = narrow.astype(jnp.float32)
-    grads = lax.dot_general(value, dout, NT, preferred_element_type=jnp.float32)
-    delta = jnp.sum(wide * grads, axis=0, keepdims=True)
-    scores = (wide * (grads - delta)).astype(jnp.bfloat16)
+    grads = jnp.dot(value, dout, preferred_element_type=jnp.float32)
+    scores = (narrow.astype(jnp.float32) * (grads - delta)).astype(jnp.bfloat16)
     key_total[...] += jnp.dot(scores, q, preferred_element_type=jnp.float32)
-    value_total[...] += jnp.dot(narrow, dout, preferred_element_type=jnp.float32)
+    value_total[...] += lax.dot_general(narrow, dout, NT, preferred_element_type=jnp.float32)
     query_total = jnp.dot(flipped[...], scores, preferred_element_type=jnp.float32) * SCALE
     for i in range(BATCH):
         part = query_total[:, i * SEG : (i + 1) * SEG]
@@ -423,8 +456,8 @@
 
 
 def backward(
-    level, meta, parents, lengths, probabilities, queries, own, partner, key_rows, value_rows,
-    picked, query_grad, token,
+    level, meta, parents, lengths, probabilities, average, inverse, queries, own, partner,
+    key_rows, value_rows, picked, query_grad, token, arrived,
 ):
     count = (level + 1) * SEG
     width = BATCH * HD
@@ -441,12 +474,14 @@
         out_shape.append(jax.ShapeDtypeStruct((level, 2, SEG, HD), jnp.bfloat16))
     last = level == LEVELS - 1
     return pl.pallas_call(
-        functools.partial(backward_kernel, level),
+        functools.partial(backward_kernel, level, len(arrived)),
         grid_spec=pltpu.PrefetchScalarGridSpec(
             num_scalar_prefetch=3,
             grid=(GROUP // BATCH,),
             in_specs=[
                 pl.BlockSpec((1, count, BATCH * SEG), lambda h, *_: (h, 0, 0)),
+                pl.BlockSpec((HD, BATCH * SEG), lambda h, *_: (0, h)),
+                pl.BlockSpec((8, BATCH * SEG), lambda h, *_: (0, h)),
                 pl.BlockSpec((1, 1, SEG, width), lambda h, *_: (level, 0, 0, h)),
                 pl.BlockSpec((1, SEG, width), lambda h, *_: (level % 2, 0, h)),
                 pl.BlockSpec((8, SEG, PIECE), lambda h, *_: (0, 0, 0)),
@@ -454,7 +489,8 @@
                 pl.BlockSpec((1, 1, SEG, HD), lambda h, *_: (level, 0, 0, 0)),
             ]
             + [pl.BlockSpec((len(PAIRS), 2, SEG, HD), lambda h, *_: (0, 0, 0, 0))] * min(level, 1)
-            + [ANY] * 2,
+            + [ANY] * 2
+            + [FREE] * len(arrived),
             out_specs=out_specs,
             scratch_shapes=[
                 pltpu.VMEM((HD, count), jnp.bfloat16),
@@ -463,72 +499,79 @@
             ],
         ),
         out_shape=out_shape,
-        input_output_aliases={} if last else {10 if level else 9: 0},
-        compiler_params=PARAMS,
+        input_output_aliases={} if last else {12 if level else 11: 0},
+        compiler_params=MIDDLE,
         cost_estimate=cost(8 * GROUP * count * SEG * HD, 2 * GROUP * count * SEG),
         name=f"backward_{level}",
     )(
-        meta, parents, lengths, probabilities, queries, own, partner, key_rows, value_rows,
-        *[picked] * min(level, 1), query_grad, token,
-    )
-
-
-def spread_kernel(target, meta, parents, *refs):
-    terms, outs = refs[:-5], refs[-4:]
+        meta, parents, lengths, probabilities, average, inverse, queries, own, partner,
+        key_rows, value_rows, *[picked] * min(level, 1), query_grad, token,
+        *arrived,
+    )
+
+
+def spread_kernel(targets, meta, parents, *refs):
+    terms, outs, token = refs[:-6], refs[-5:-1], refs[-1]
     me = node_id(meta)
     sibling = me + 1 - 2 * meta[2]
-    places = []
-    for i in range(len(terms)):
-        node = sibling if i % 2 else me
-        places.append(ancestor(parents, node, target + 1 + i // 2, target))
-    for step, out in enumerate(outs):
-        x = lax.rem(meta[1] + step, 4)
-        for zh in range(2):
-            wanted = (zh * 4 + x) * 2 + meta[2]
-            total = jnp.zeros((2, SEG, HD), jnp.float32)
-            for term, place in zip(terms, places):
-                total += jnp.where(place == wanted, term[0].astype(jnp.float32), 0.0)
-            out[zh] = total.astype(jnp.bfloat16)
-
-
-def spread(target, meta, parents, terms, token):
-    whole = pl.BlockSpec((2, 2, SEG, HD), lambda n, *_: (0, 0, 0, 0))
-    return pl.pallas_call(
-        functools.partial(spread_kernel, target),
+    lowest = min(targets)
+    token[...] = jnp.zeros(TOKEN_SHAPE.shape, jnp.float32)
+    for j, target in enumerate(targets):
+        found = []
+        for i, term in enumerate(terms):
+            level = lowest + 1 + i // 2
+            if level > target:
+                place = ancestor(parents, sibling if i % 2 else me, level, target)
+                found.append((place, term[target].astype(jnp.float32)))
+        for step, out in enumerate(outs):
+            x = lax.rem(meta[1] + step, 4)
+            for zh in range(2):
+                wanted = (zh * 4 + x) * 2 + meta[2]
+                total = sum(jnp.where(place == wanted, term, 0.0) for place, term in found)
+                out[j, zh] = total.astype(jnp.bfloat16)
+
+
+def spread(targets, meta, parents, terms, token):
+    shape = (len(targets), 2, 2, SEG, HD)
+    return pl.pallas_call(
+        functools.partial(spread_kernel, targets),
         grid_spec=pltpu.PrefetchScalarGridSpec(
             num_scalar_prefetch=2,
             grid=(1,),
-            in_specs=[pl.BlockSpec((1, 2, SEG, HD), lambda n, *_: (target, 0, 0, 0))] * len(terms)
-            + [ANY],
-            out_specs=[whole] * 4,
+            in_specs=[pl.BlockSpec(term.shape, lambda *_: (0, 0, 0, 0)) for term in terms] + [FREE],
+            out_specs=[pl.BlockSpec(shape, lambda *_: (0, 0, 0, 0, 0))] * 4 + [TOKEN],
         ),
-        out_shape=[jax.ShapeDtypeStruct((2, 2, SEG, HD), jnp.bfloat16)] * 4,
+        out_shape=[jax.ShapeDtypeStruct(shape, jnp.bfloat16)] * 4 + [TOKEN_SHAPE],
         compiler_params=SMALL,
         cost_estimate=cost(0, 0),
-        name=f"spread_{target}",
+        name="spread",
     )(meta, parents, *terms, token)
 
 
 def collect_kernel(meta, *refs):
-    parts, (kept, given) = refs[:4], refs[5:]
-    kept[...] = sum(part[meta[0]].astype(jnp.float32) for part in parts)
-    given[...] = sum(part[1 - meta[0]].astype(jnp.float32) for part in parts).astype(jnp.bfloat16)
+    parts, (kept, given, token) = refs[:4], refs[5:]
+    token[...] = jnp.zeros(TOKEN_SHAPE.shape, jnp.float32)
+    for j in range(kept.shape[0]):
+        kept[j] = sum(part[j, meta[0]].astype(jnp.float32) for part in parts)
+        sent = sum(part[j, 1 - meta[0]].astype(jnp.float32) for part in parts)
+        given[j] = sent.astype(jnp.bfloat16)
 
 
 def collect(meta, parts, token):
-    whole = pl.BlockSpec((2, 2, SEG, HD), lambda n, *_: (0, 0, 0, 0))
-    half = pl.BlockSpec((2, SEG, HD), lambda n, *_: (0, 0, 0))
+    shape = parts[0].shape
+    half = (shape[0], *shape[2:])
     return pl.pallas_call(
         collect_kernel,
         grid_spec=pltpu.PrefetchScalarGridSpec(
             num_scalar_prefetch=1,
             grid=(1,),
-            in_specs=[whole] * 4 + [ANY],
-            out_specs=[half] * 2,
+            in_specs=[pl.BlockSpec(shape, lambda *_: (0, 0, 0, 0, 0))] * 4 + [FREE],
+            out_specs=[pl.BlockSpec(half, lambda *_: (0, 0, 0, 0))] * 2 + [TOKEN],
         ),
         out_shape=[
-            jax.ShapeDtypeStruct((2, SEG, HD), jnp.float32),
-            jax.ShapeDtypeStruct((2, SEG, HD), jnp.bfloat16),
+            jax.ShapeDtypeStruct(half, jnp.float32),
+            jax.ShapeDtypeStruct(half, jnp.bfloat16),
+            TOKEN_SHAPE,
         ],
         compiler_params=SMALL,
         cost_estimate=cost(0, 0),
@@ -537,27 +580,31 @@
 
 
 def finish_kernel(*refs):
-    owns, parts, outs = refs[:LEVELS], refs[LEVELS:-2], refs[-2:]
+    owns, terms, outs = refs[:LEVELS], refs[LEVELS:8], refs[8:]
     for t in range(LEVELS):
         total = owns[t][...]
-        for part in parts[2 * t : 2 * t + 2]:
-            total += part[...].astype(jnp.float32)
+        if t < LEVELS - 1:
+            for term in terms[2:] if t == 0 else terms[:2]:
+                total += term[0 if t == 0 else 2 - t].astype(jnp.float32)
         for i in range(2):
             outs[i][t, 0] = total[i].astype(jnp.bfloat16)
 
 
-def finish(owns, parts, shape):
-    both = pl.BlockSpec((2, SEG, HD), lambda n: (0, 0, 0))
+def finish(owns, terms, shape):
+    arrays = [*owns, *terms]
     return pl.pallas_call(
         finish_kernel,
         grid=(1,),
-        in_specs=[both] * (LEVELS + len(parts)),
-        out_specs=[pl.BlockSpec((LEVELS, 1, SEG, HD), lambda n: (0, 0, 0, 0))] * 2,
+        in_specs=[
+            pl.BlockSpec(array.shape, functools.partial(lambda rank, *_: (0,) * rank, array.ndim))
+            for array in arrays
+        ],
+        out_specs=[pl.BlockSpec((LEVELS, 1, SEG, HD), lambda *_: (0, 0, 0, 0))] * 2,
         out_shape=[jax.ShapeDtypeStruct(shape, jnp.bfloat16)] * 2,
         compiler_params=SMALL,
-        cost_estimate=cost(16 * SEG * HD, 64 * SEG * HD),
+        cost_estimate=cost(0, 0),
         name="finish",
-    )(*owns, *parts)
+    )(*arrays)
 
 
 def local(queries, key_rows, value_rows, cotangent, out_weight, parents, seg_len):
@@ -580,22 +627,36 @@
     above = lax.ppermute(upper, "y", DOWN)
     below = lax.ppermute(upper, "y", UP)
     w0, w1 = hop(pieces[0], 0), hop(pieces[1], 1)
-    above, below, w0, w1, lower, p2, p3 = tie(
-        above, below, w0, w1, lower, pieces[2], pieces[3]
+    first_high, token = blocks_product(meta, [upper], (0,), out_weight, [], jnp.float32, meta)
+    first_low, token = blocks_product(meta, [lower], (0,), out_weight, [], jnp.float32, token)
+    root, root_average, root_inverse = probs(
+        (0,), *table, queries, key_rows, value_rows, [], token
+    )
+    above, below, w0, w1, lower, p2, p3, first_high, first_low, root = tie(
+        above, below, w0, w1, lower, pieces[2], pieces[3], first_high, first_low, root
     )
     across = lax.ppermute(below, "y", UP)
     above_low = lax.ppermute(lower, "y", DOWN)
     w2, w3 = hop(p2, 2), hop(p3, 3)
-    early = blocks_product(meta, [upper, above, below], (0, 1, 3), out_weight, [], meta)
+    early, token = blocks_product(
+        meta, [above, below], (1, 3), out_weight, [first_high], jnp.float32, meta
+    )
     mine, early = tie(mine, early)
     mine, other = pick(meta, parents, mine)
     other = lax.ppermute(other, "c", SWAP)
-    *probabilities, picked = probs(*table, queries, key_rows, mine, other, early)
+    results = probs(
+        (3, 2, 1), *table, queries, key_rows, value_rows, [mine, other], token
+    )
+    probabilities = [root, *results[2::-1]]
+    averages = [root_average, *results[5:2:-1]]
+    inverse, picked = results[6:]
+    inverses = [root_inverse, inverse, inverse, inverse]
     across, above_low, w0, w1, w2, w3, lower, early, picked = tie(
         across, above_low, w0, w1, w2, w3, lower, early, picked
     )
     below_low = lax.ppermute(lower, "y", UP)
     across_low = lax.ppermute(above_low, "y", DOWN)
+    cots_low = (lower, above_low, below_low, across_low)
     weights = [w0, w1, w2, w3]
     weights += [lax.ppermute(piece, "c", SWAP) for piece in weights]
     partners = [None] * LEVELS
@@ -604,57 +665,54 @@
         parts = product(meta, cots, weights, token)
         for j in (1, 0):
             partners[2 * i + j] = lax.ppermute(parts[j], "zl", SWAP)
-        return parts[0]
-
-    own_high = blocks_product(meta, [across], (2,), out_weight, [early], meta)
-    token = partner_pair(1, (upper, above, below, across), own_high)
-    early_low = blocks_product(meta, [lower, above_low], (0, 1), out_weight, [], token)
-    token = partner_pair(0, (lower, above_low, below_low, across_low), early_low)
+        return parts[2]
+
+    own_high, token = blocks_product(
+        meta, [across], (2,), out_weight, [early], jnp.bfloat16, meta
+    )
+    token = partner_pair(1, (upper, above, below, across), token)
+    token = partner_pair(0, cots_low, token)
     own_grads = [None] * LEVELS
     terms = [None] * 6
-    moved = [None] * (LEVELS - 1)
-    parts = [None] * 6
 
     def back(level, own, query_grad, token):
         query_grad, own_grads[level], *rest = backward(
-            level, *table, probabilities[level], queries, own, partners[level],
-            key_rows, value_rows, picked, query_grad, token,
+            level, *table, probabilities[level], averages[level], inverses[level], queries, own,
+            partners[level], key_rows, value_rows, picked, query_grad, token,
+            [],
         )
         if level:
             terms[2 * level - 2] = rest[0]
             terms[2 * level - 1] = lax.ppermute(rest[0], "c", SWAP)
         return query_grad
 
-    def spread_out(target, token):
-        here, up, across, down = spread(target, meta, parents, terms[2 * target :], token)
-        moved[target] = [
+    query_grad = back(3, own_high, token, token)
+    query_grad = back(2, own_high, query_grad, token)
+
+    def send(targets, token):
+        here, up, across, down, token = spread(
+            targets, meta, parents, terms[2 * min(targets) :], token
+        )
+        moved = [
             here,
             lax.ppermute(up, "x", UP),
             lax.ppermute(down, "x", DOWN),
             lax.ppermute(across, "x", ACROSS),
         ]
-        return here
-
-    def bring(target, token):
-        kept, given = collect(meta, moved[target], token)
-        parts[2 * target] = kept
-        parts[2 * target + 1] = lax.ppermute(given, "zh", SWAP)
-        return kept
-
-    query_grad = back(3, own_high, token, token)
-    own_low = blocks_product(
-        meta, [below_low, across_low], (3, 2), out_weight, [early_low], query_grad
-    )
-    token = spread_out(2, own_low)
-    query_grad = back(2, own_high, query_grad, token)
-    token = spread_out(1, query_grad)
+        return moved, token
+
+    high, token = send((2, 1), own_grads[2])
+    own_low, token = blocks_product(
+        meta, cots_low[1:], (1, 3, 2), out_weight, [first_low], jnp.bfloat16, token
+    )
     query_grad = back(1, own_low, query_grad, token)
-    token = bring(2, query_grad)
-    token = spread_out(0, token)
+    low, token = send((0,), own_grads[1])
     query_grad = back(0, own_low, query_grad, token)
-    token = bring(1, query_grad)
-    bring(0, token)
-    key_grad, value_grad = finish(own_grads, parts, key_rows.shape)
+    high, high_given, token = collect(meta, high, own_grads[0])
+    high_given = lax.ppermute(high_given, "zh", SWAP)
+    low, low_given, token = collect(meta, low, token)
+    low_given = lax.ppermute(low_given, "zh", SWAP)
+    key_grad, value_grad = finish(own_grads, [high, high_given, low, low_given], key_rows.shape)
     return (query_grad, key_grad, value_grad)
 
 

time: 229 us -> 200 us (0.87)
  Pallas kernels: 111 us -> 95 us
  local copies, waits for them, and re-layouts: 21.9 us -> 16.5 us
  starting transfers between devices: 44.4 us -> 40.3 us
  waiting for transfers between devices: 33.1 us -> 30.7 us
    ppermute x2, waiting for transfers between devices: 17.5 us -> 0.01 us  [hop(): return lax.ppermute(piece, 'zl', SWAP)]
    pallas_call x9, Pallas kernels: 49.5 us -> 41.3 us  [the longest x4 18.9 us: backward(): pl.pallas_call(functools.partial(backward_kernel, level, len(arrived)), g...]
    unnamed x94, local copies, waits for them, and re-layouts: 19 us -> 13.6 us
    ppermute x1, waiting for transfers between devices: 0.01 us -> 5.15 us  [local(): below_low = lax.ppermute(lower, 'y', UP)]
    ppermute x4, waiting for transfers between devices: 0.01 us -> 4.22 us  [partner_pair(): partners[2 * i + j] = lax.ppermute(parts[j], 'zl', SWAP)]
    pallas_call x2, Pallas kernels: 19.6 us -> 15.4 us  [product(): pl.pallas_call(product_kernel, grid_spec=pltpu.PrefetchScalarGridSpec(num...]
    ppermute x12 -> x8, starting transfers between devices: 19.6 us -> 15.9 us  [the longest x2 4.49 us: send(): lax.ppermute(down, 'x', DOWN)]
    ppermute x12 -> x8, waiting for transfers between devices: 5.75 us -> 9.28 us  [the longest x2 4.77 us: send(): lax.ppermute(across, 'x', ACROSS)]
  transfers between devices with their start and end apart: 36 -> 32, of which waited for: 10 -> 15; matrix products, arithmetic and copies ran while one was open for 1% -> 1% of each run, Pallas kernels for 48% -> 47%
where the time goes in v2:
time: 200 us; the launch traced here: 199 us
  Pallas kernels  95 us (48%)
  starting transfers between devices  40.3 us (20%)
  waiting for transfers between devices  30.7 us (15%)
  local copies, waits for them, and re-layouts  16.5 us (8%)
  between operations  14.6 us (7%)
  other arithmetic  2.16 us (1%)
    pallas_call x5, Pallas kernels, blocks_product(): pl.pallas_call(functools.partial(blocks_kernel, count, len(earlier)), gri...  27 us
    pallas_call x4, Pallas kernels, backward(): pl.pallas_call(functools.partial(backward_kernel, level, len(arrived)), g...  18.9 us
    pallas_call x2, Pallas kernels, probs(): pl.pallas_call(functools.partial(probs_kernel, levels), grid_spec=pltpu.P...  18 us
    pallas_call x2, Pallas kernels, product(): pl.pallas_call(product_kernel, grid_spec=pltpu.PrefetchScalarGridSpec(num...  15.4 us
    unnamed x94, local copies, waits for them, and re-layouts  13.6 us
    pallas_call x1, Pallas kernels, prepare(): pl.pallas_call(prepare_kernel, grid_spec=pltpu.PrefetchScalarGridSpec(num...  6.13 us
    ppermute x1, waiting for transfers between devices, local(): below_low = lax.ppermute(lower, 'y', UP)  5.15 us
    ppermute x2, waiting for transfers between devices, send(): lax.ppermute(across, 'x', ACROSS)  4.77 us
  transfers between devices with their start and end apart: 32, of which 15 were waited for; matrix products, arithmetic and copies ran while one was open for 1% of the time, Pallas kernels for 47%

profile of v2, /device:TPU:0, one launch (start us, length us, event | category | flops | bytes accessed | tf_op | source)
XLA Modules:
  0.0 199.2 jit_solution(18436925989041244984)
XLA Ops:
  8.3 4.0 %collective-permute-start = (bf16[2,3,256,128]{3,2,1,0:T(8,128)(2,1)S(1)}, bf16[2,3,256,128]{3,2,1,0:T(8,128)(2,1)S(1)}, u32[]{:S(2)}, u32[]{:S(2)}) collective-permute-start(bf16[2,3,256,128]{3,2,1,0:T(8,128)(2,1)S(1)} %pad_maximum_fusion.1.refs_0_), channel_id=1, source_target_pairs={{0,64},{64,0},{1,65},{65,1},{2,66},{66,2},{3,67},{67,3},{4,68},{68... | collective-permute-start | bytes 1179656 | tf_op jit(solution)/shard_map/ppermute | solution.py:617
  13.0 6.1 %prepare.1 = (bf16[128,4096]{1,0:T(8,128)(2,1)}, bf16[128,4096]{1,0:T(8,128)(2,1)}, bf16[128,4096]{1,0:T(8,128)(2,1)}, bf16[128,4096]{1,0:T(8,128)(2,1)}, bf16[2...) custom-call(s32[5]{0:T(128)} %stack.35.meta.refs_2_.refs_5_.refs_3_, bf16[1024,8192]{1,0:T(8,128)(2,1)} %refs_5_.1, ...), custom_call_target="tpu_custom_call" | custom-call | flops 1 | bytes 1 | tf_op jit(solution)/shard_map/prepare/pallas_call | solution.py:95
  19.1 2.3 %collective-permute-done.refs_1_ = bf16[2,3,256,128]{3,2,1,0:T(8,128)(2,1)S(1)} collective-permute-done((bf16[2,3,256,128]{3,2,1,0:T(8,128)(2,1)S(1)}, bf16[2,3,256,128]{3,2,1,0:T(8,128)(2,1)S(1)}, u32[]{:S(2)}, u32[]{:S(2)}) %collective-permute-start) | collective-permute-done | bytes 393248 | tf_op jit(solution)/shard_map/ppermute | solution.py:617
  22.3 2.1 %pad_maximum_fusion = bf16[2,2,3,256,128]{4,3,2,1,0:T(8,128)(2,1)} fusion(bf16[1,2,3,256,128]{4,3,2,1,0:T(8,128)(2,1)} %bitcast.18, bf16[1,2,3,256,128]{4,3,2,1,0:T(8,128)(2,1)} %bitcast.17), kind=kLoop, calls=%fused_computation | loop fusion | flops 393216 | bytes 1572864 | tf_op jit(solution)/shard_map/stack | solution.py:620
  24.4 1.4 collective-permute-start.3
  25.8 2.5 %collective-permute-start.4 = (bf16[128,4096]{1,0:T(8,128)(2,1)}, bf16[128,4096]{1,0:T(8,128)(2,1)S(1)}, u32[]{:S(2)}, u32[]{:S(2)}) collective-permute-start(bf16[128,4096]{1,0:T(8,128)(2,1)} %get-tuple-element.101), channel_id=1, source_target_pairs={{0,68},{4,64},{64,4},{68,0},{1,69},{5,65},{65,5},{69,1},{2,70},{6,... | collective-permute-start | bytes 3145736 | tf_op jit(solution)/shard_map/ppermute | solution.py:624
  28.3 1.6 collective-permute-start.2
  29.9 1.7 collective-permute-start.1
  32.7 1.2 copy-done.21
  34.0 4.3 %own_product.5 = (f32[2,256,1024]{2,1,0:T(8,128)S(1)}, f32[8,128]{1,0:T(8,128)S(1)}) custom-call(s32[5]{0:T(128)S(1)} %copy-done.34, bf16[2,256,1024]{2,1,0:T(8,128)(2,1)S(1)} %copy-done.21, bf16[1024,8192]{1,0:T(8,128)(2,1)} %refs_5_.1, s32[5]{0:T(128)S(1)} %copy-done.34), custom_call_target="tpu_custom_call" | custom-call | flops 1 | bytes 1 | tf_op jit(solution)/shard_map/own_product/pallas_call | solution.py:160
  38.2 1.3 copy-done.24
  39.5 4.2 %own_product.6 = (f32[2,256,1024]{2,1,0:T(8,128)S(1)}, f32[8,128]{1,0:T(8,128)S(1)}) custom-call(s32[5]{0:T(128)S(1)} %copy-done.34, bf16[2,256,1024]{2,1,0:T(8,128)(2,1)S(1)} %copy-done.3, bf16[1024,8192]{1,0:T(8,128)(2,1)} %refs_5_.1, f32[8,128]{1,0:T(8,128)S(1)} %get-tuple-element.106.refs_2_), custom_call_target="tpu_custom_call" | custom-call | flops 1 | bytes 1 | tf_op jit(solution)/shard_map/own_product/pallas_call | solution.py:160
  43.8 1.4 copy-done.23
  45.7 4.2 %probs.2 = (bf16[2,256,1024]{2,1,0:T(8,128)(2,1)}, f32[128,2048]{1,0:T(8,128)}, f32[8,2048]{1,0:T(8,128)}) custom-call(s32[5]{0:T(128)} %stack.35.meta.refs_2_.refs_5_.refs_3_, s32[48]{0:T(128)} %reshape.12.parents, s32[64]{0:T(128)} %reshape.13.lengths, bf16[4,1,256,1024]{3,2,1,0:T(8,128)(2,1)} %query.11, bf16[4,1,256,128]{3,2,1,0:T(8,128)(2,1)} %own_key.11, ...), custom_call_target="tpu_custom_call" | custom-call | flops 1 | bytes 1 | tf_op jit(solution)/shard_map/probs/pallas_call | solution.py:379
  50.9 2.3 %collective-permute-done.2.refs_1_ = bf16[2,256,1024]{2,1,0:T(8,128)(2,1)S(1)} collective-permute-done((bf16[2,256,1024]{2,1,0:T(8,128)(2,1)}, bf16[2,256,1024]{2,1,0:T(8,128)(2,1)S(1)}, u32[]{:S(2)}, u32[]{:S(2)}) %collective-permute-start.2) | collective-permute-done | bytes 1048608 | tf_op jit(solution)/shard_map/ppermute | solution.py:628
  56.1 2.2 %collective-permute-start.6 = (bf16[2,256,1024]{2,1,0:T(8,128)(2,1)}, bf16[2,256,1024]{2,1,0:T(8,128)(2,1)S(1)}, u32[]{:S(2)}, u32[]{:S(2)}) collective-permute-start(bf16[2,256,1024]{2,1,0:T(8,128)(2,1)} %get-tuple-element.114.refs_6_), channel_id=1, source_target_pairs={{0,3},{1,0},{2,1},{3,2},{4,7},{5,4},{6,5},{7,6},{8,11},{9,8},{10,9... | collective-permute-start | bytes 3145736 | tf_op jit(solution)/shard_map/ppermute | solution.py:639
  58.3 1.3 copy-done.19
  59.6 6.3 %own_product.7 = (f32[2,256,1024]{2,1,0:T(8,128)S(1)}, f32[8,128]{1,0:T(8,128)S(1)}) custom-call(s32[5]{0:T(128)S(1)} %copy-done.35, bf16[2,256,1024]{2,1,0:T(8,128)(2,1)} %get-tuple-element.121.refs_0_.above, bf16[2,256,1024]{2,1,0:T(8,128)(2,1)S(1)} %copy-done.19, bf16[1024,8192]{1,0:T(8,128)(2,1)} %refs_5_.1, bf16[1024,8192]{1,0:T(8,128)(2,1)} %refs_5_.1, ...), custom_call_target="tpu_custom_call" | custom-call | flops 1 | bytes 1 | tf_op jit(solution)/shard_map/own_product/pallas_call | solution.py:160
  65.9 1.3 copy-done.1
  67.9 3.1 %pick.1 = (bf16[6,2,256,128]{3,2,1,0:T(8,128)(2,1)}, bf16[6,2,256,128]{3,2,1,0:T(8,128)(2,1)}) custom-call(s32[5]{0:T(128)} %stack.35.meta.refs_2_.refs_5_.refs_3_, s32[48]{0:T(128)} %reshape.12.parents, bf16[4,2,2,3,256,128]{5,4,3,2,1,0:T(8,128)(2,1)} %get-tuple-element.125.mine), custom_call_target="tpu_custom_call" | custom-call | flops 1 | bytes 1 | tf_op jit(solution)/shard_map/pick/pallas_call | solution.py:281
  71.1 2.5 %collective-permute-done.9.refs_1_ = bf16[6,2,256,128]{3,2,1,0:T(8,128)(2,1)S(1)} collective-permute-done((bf16[6,2,256,128]{3,2,1,0:T(8,128)(2,1)}, bf16[6,2,256,128]{3,2,1,0:T(8,128)(2,1)S(1)}, u32[]{:S(2)}, u32[]{:S(2)}) %collective-permute-start.9) | collective-permute-done | bytes 786464 | tf_op jit(solution)/shard_map/ppermute | solution.py:646
  74.5 13.8 %probs.3 = (bf16[2,1024,1024]{2,1,0:T(8,128)(2,1)}, bf16[2,768,1024]{2,1,0:T(8,128)(2,1)}, bf16[2,512,1024]{2,1,0:T(8,128)(2,1)}, f32[128,2048]{1,0:T(8,128)}, f...) custom-call(s32[5]{0:T(128)} %stack.35.meta.refs_2_.refs_5_.refs_3_, ...), custom_call_target="tpu_custom_call" | custom-call | flops 1 | bytes 1 | tf_op jit(solution)/shard_map/probs/pallas_call | solution.py:379
  92.9 3.2 %collective-permute-start.11 = (bf16[2,256,1024]{2,1,0:T(8,128)(2,1)}, bf16[2,256,1024]{2,1,0:T(8,128)(2,1)S(1)}, u32[]{:S(2)}, u32[]{:S(2)}) collective-permute-start(bf16[2,256,1024]{2,1,0:T(8,128)(2,1)} %get-tuple-element.130.above.refs_0_), channel_id=1, source_target_pairs={{0,3},{1,0},{2,1},{3,2},{4,7},{5,4},{6,5},{7,6},{8,11},{9,8},{10,9... | collective-permute-start | bytes 3145736 | tf_op jit(solution)/shard_map/ppermute | solution.py:658
  96.2 1.6 copy-done.2
  97.8 4.9 %own_product.8 = (bf16[2,256,1024]{2,1,0:T(8,128)(2,1)S(1)}, f32[8,128]{1,0:T(8,128)S(1)}) custom-call(s32[5]{0:T(128)S(1)} %copy-done.36, bf16[2,256,1024]{2,1,0:T(8,128)(2,1)} %get-tuple-element.136.refs_0_.across, bf16[1024,8192]{1,0:T(8,128)(2,1)} %refs_5_.1, f32[2,256,1024]{2,1,0:T(8,128)S(1)} %copy-done.2, s32[5]{0:T(128)S(1)} %copy-done.36), custom_call_target="tpu_custom_call" | custom-call | flops 1 | bytes 1 | tf_op jit(solution)/shard_map/own_product/pallas_call | solution.py:160
  102.8 7.9 %partner_product.2 = (bf16[8,256,128]{2,1,0:T(8,128)(2,1)S(1)}, bf16[8,256,128]{2,1,0:T(8,128)(2,1)S(1)}, f32[8,128]{1,0:T(8,128)S(1)}) custom-call(s32[5]{0:T(128)S(1)} %copy-done.36, bf16[2,256,1024]{2,1,0:T(8,128)(2,1)S(1)} %copy-done.22, bf16[2,256,1024]{2,1,0:T(8,128)(2,1)} %get-tuple-element.121.refs_0_.above, bf16[2,256,1024]{2,1,0:T(8,128)(2,1)S(1)} %copy-done.20, ...), custom_call_target="tpu_custom_call" | custom-call | flops 1 | bytes 1 | tf_op jit(solution)/shard_map/partner_product/pallas_call | solution.py:231
  112.8 5.1 %collective-permute-done.10.below.refs_1_ = bf16[2,256,1024]{2,1,0:T(8,128)(2,1)S(1)} collective-permute-done((bf16[2,256,1024]{2,1,0:T(8,128)(2,1)}, bf16[2,256,1024]{2,1,0:T(8,128)(2,1)S(1)}, u32[]{:S(2)}, u32[]{:S(2)}) %collective-permute-start.10) | collective-permute-done | bytes 1048608 | tf_op jit(solution)/shard_map/ppermute | solution.py:657
  118.0 1.2 collective-permute-done.11.across.refs_2_
  119.3 7.5 %partner_product.3 = (bf16[8,256,128]{2,1,0:T(8,128)(2,1)}, bf16[8,256,128]{2,1,0:T(8,128)(2,1)}, f32[8,128]{1,0:T(8,128)S(1)}) custom-call(s32[5]{0:T(128)S(1)} %copy-done.36, bf16[2,256,1024]{2,1,0:T(8,128)(2,1)S(1)} %copy-done.4, bf16[2,256,1024]{2,1,0:T(8,128)(2,1)S(1)} %copy-done.17, bf16[2,256,1024]{2,1,0:T(8,128)(2,1)S(1)} %collective-permute-done.10.below.refs_1_, ...), custom_call_target="tpu_custom_call" | custom-call | flops 1 | bytes 1 | tf_op jit(solution)/shard_map/partner_product/pallas_call | solution.py:231
  126.9 6.2 %backward_3.1 = (bf16[4,1,256,1024]{3,2,1,0:T(8,128)(2,1)}, f32[2,256,128]{2,1,0:T(8,128)S(1)}, bf16[3,2,256,128]{3,2,1,0:T(8,128)(2,1)S(1)}) custom-call(s32[5]{0:T(128)S(1)} %copy-done.36, s32[48]{0:T(128)S(1)} %copy-done.38, s32[64]{0:T(128)S(1)} %copy-done.39, bf16[2,1024,1024]{2,1,0:T(8,128)(2,1)S(1)} %copy-done.25, f32[128,2048]{1,0:T(8,128)S(1)} %copy-done.30, ...), custom_call_target="tpu_custom_call" | custom-call | flops 1 | bytes 1 | tf_op jit(solution)/shard_map/backward_3/pallas_call | solution.py:476
  133.1 2.6 %collective-permute-done.16.partner = bf16[8,256,128]{2,1,0:T(8,128)(2,1)S(1)} collective-permute-done((bf16[8,256,128]{2,1,0:T(8,128)(2,1)S(1)}, bf16[8,256,128]{2,1,0:T(8,128)(2,1)S(1)}, u32[]{:S(2)}, u32[]{:S(2)}) %collective-permute-start.16) | collective-permute-done | bytes 524320 | tf_op jit(solution)/shard_map/ppermute | solution.py:667
  135.7 5.2 %backward_2.1 = (bf16[4,1,256,1024]{3,2,1,0:T(8,128)(2,1)}, f32[2,256,128]{2,1,0:T(8,128)S(1)}, bf16[2,2,256,128]{3,2,1,0:T(8,128)(2,1)S(1)}) custom-call(s32[5]{0:T(128)S(1)} %copy-done.36, s32[48]{0:T(128)S(1)} %copy-done.38, s32[64]{0:T(128)S(1)} %copy-done.39, bf16[2,768,1024]{2,1,0:T(8,128)(2,1)S(1)} %copy-done.27, ...), custom_call_target="tpu_custom_call", output_to_operand_aliasing={{0}: (12, {})} | custom-call | flops 1 | bytes 1 | tf_op jit(solution)/shard_map/backward_2/pallas_call | solution.py:476
  143.0 2.2 %spread.2 = (bf16[2,2,2,256,128]{4,3,2,1,0:T(8,128)(2,1)S(1)}, bf16[2,2,2,256,128]{4,3,2,1,0:T(8,128)(2,1)}, bf16[2,2,2,256,128]{4,3,2,1,0:T(8,128)(2,1)}, bf16[...) custom-call(s32[5]{0:T(128)S(1)} %copy-done.36, s32[48]{0:T(128)S(1)} %copy-done.38, ...), custom_call_target="tpu_custom_call" | custom-call | flops 1 | bytes 1 | tf_op jit(solution)/shard_map/spread/pallas_call | solution.py:536
  145.2 1.5 collective-permute-start.23
  146.6 1.8 collective-permute-start.24
  148.4 1.8 collective-permute-start.25
  150.2 7.3 %own_product.9 = (bf16[2,256,1024]{2,1,0:T(8,128)(2,1)S(1)}, f32[8,128]{1,0:T(8,128)S(1)}) custom-call(s32[5]{0:T(128)S(1)} %copy-done.36, bf16[2,256,1024]{2,1,0:T(8,128)(2,1)S(1)} %copy-done.17, bf16[2,256,1024]{2,1,0:T(8,128)(2,1)S(1)} %collective-permute-done.10.below.refs_1_, bf16[2,256,1024]{2,1,0:T(8,128)(2,1)S(1)} %collective-permute-done.11.across.refs_2_, ...), custom_call_target="tpu_custom_call" | custom-call | flops 1 | bytes 1 | tf_op jit(solution)/shard_map/own_product/pallas_call | solution.py:160
  157.6 4.2 %backward_1.1 = (bf16[4,1,256,1024]{3,2,1,0:T(8,128)(2,1)}, f32[2,256,128]{2,1,0:T(8,128)S(1)}, bf16[1,2,256,128]{3,2,1,0:T(8,128)(2,1)S(1)}) custom-call(s32[5]{0:T(128)S(1)} %copy-done.36, s32[48]{0:T(128)S(1)} %copy-done.38, s32[64]{0:T(128)S(1)} %copy-done.39, bf16[2,512,1024]{2,1,0:T(8,128)(2,1)S(1)} %copy-done.28, ...), custom_call_target="tpu_custom_call", output_to_operand_aliasing={{0}: (12, {})} | custom-call | flops 1 | bytes 1 | tf_op jit(solution)/shard_map/backward_1/pallas_call | solution.py:476
  161.8 1.3 collective-permute-done.22.refs_1_
  163.1 1.4 spread.3
  165.1 1.6 collective-permute-done.20.partner
  166.8 2.7 %collective-permute-start.28 = (bf16[1,2,2,256,128]{4,3,2,1,0:T(8,128)(2,1)S(1)}, bf16[1,2,2,256,128]{4,3,2,1,0:T(8,128)(2,1)S(1)}, u32[]{:S(2)}, u32[]{:S(2)}) collective-permute-start(bf16[1,2,2,256,128]{4,3,2,1,0:T(8,128)(2,1)S(1)} %get-tuple-element.178), channel_id=1, source_target_pairs={{0,48},{16,0},{32,16},{48,32},{1,49},{17,1},{33,17},{49,33},{2,50}... | collective-permute-start | bytes 786440 | tf_op jit(solution)/shard_map/ppermute | solution.py:699
  170.3 3.2 %backward_0.1 = (bf16[4,1,256,1024]{3,2,1,0:T(8,128)(2,1)}, f32[2,256,128]{2,1,0:T(8,128)S(1)}) custom-call(s32[5]{0:T(128)S(1)} %copy-done.36, s32[48]{0:T(128)S(1)} %copy-done.38, s32[64]{0:T(128)S(1)} %copy-done.39, bf16[2,256,1024]{2,1,0:T(8,128)(2,1)S(1)} %copy-done.26, f32[128,2048]{1,0:T(8,128)S(1)} %copy-done.31, ...), custom_call_target="tpu_custom_call", output_to_operand_aliasing={{0}: (11, {})} | custom-call | flops 1 | bytes 1 | tf_op jit(solution)/shard_map/backward_0/pallas_call | solution.py:476
  174.4 4.5 %collective-permute-start.26 = (bf16[2,2,256,128]{3,2,1,0:T(8,128)(2,1)S(1)}, bf16[2,2,256,128]{3,2,1,0:T(8,128)(2,1)S(1)}, u32[]{:S(2)}, u32[]{:S(2)}) collective-permute-start(bf16[2,2,256,128]{3,2,1,0:T(8,128)(2,1)S(1)} %get-tuple-element.175), channel_id=1, source_target_pairs={{0,64},{64,0},{1,65},{65,1},{2,66},{66,2},{3,67},{67,3},{4,68},{68... | collective-permute-start | bytes 786440 | tf_op jit(solution)/shard_map/ppermute | solution.py:712
  179.1 4.7 %collective-permute-done.29.refs_3_ = bf16[1,2,2,256,128]{4,3,2,1,0:T(8,128)(2,1)S(1)} collective-permute-done((bf16[1,2,2,256,128]{4,3,2,1,0:T(8,128)(2,1)S(1)}, bf16[1,2,2,256,128]{4,3,2,1,0:T(8,128)(2,1)S(1)}, u32[]{:S(2)}, u32[]{:S(2)}) %collective-permute-start.29) | collective-permute-done | bytes 262176 | tf_op jit(solution)/shard_map/ppermute | solution.py:700
  183.8 1.2 collect.3
  185.0 2.2 %collective-permute-start.30 = (bf16[1,2,256,128]{3,2,1,0:T(8,128)(2,1)S(1)}, bf16[1,2,256,128]{3,2,1,0:T(8,128)(2,1)S(1)}, u32[]{:S(2)}, u32[]{:S(2)}) collective-permute-start(bf16[1,2,256,128]{3,2,1,0:T(8,128)(2,1)S(1)} %get-tuple-element.182), channel_id=1, source_target_pairs={{0,64},{64,0},{1,65},{65,1},{2,66},{66,2},{3,67},{67,3},{4,68},{68... | collective-permute-start | bytes 393224 | tf_op jit(solution)/shard_map/ppermute | solution.py:714
  187.3 4.2 %collective-permute-done.30.refs_7_ = bf16[1,2,256,128]{3,2,1,0:T(8,128)(2,1)S(1)} collective-permute-done((bf16[1,2,256,128]{3,2,1,0:T(8,128)(2,1)S(1)}, bf16[1,2,256,128]{3,2,1,0:T(8,128)(2,1)S(1)}, u32[]{:S(2)}, u32[]{:S(2)}) %collective-permute-start.30) | collective-permute-done | bytes 131104 | tf_op jit(solution)/shard_map/ppermute | solution.py:714
  (141 shorter events, 22.2 us)
Async XLA Ops:
  7.2 60.7 %all-gather.3.cloned.1.call-start = ((), (), s32[]{:S(2)}) async-start(), calls=%async_computation | async-start | bytes 3932160 | tf_op jit(solution)/shard_map/all_gather | solution.py:620
  8.3 10.8 %copy-start.42 = (bf16[2,3,256,128]{3,2,1,0:T(8,128)(2,1)}, bf16[2,3,256,128]{3,2,1,0:T(8,128)(2,1)S(1)}, u32[]{:S(2)}) copy-start(bf16[2,3,256,128]{3,2,1,0:T(8,128)(2,1)S(1)} %pad_maximum_fusion.1.refs_0_) | copy-start | bytes 1179652
  8.3 13.2 %collective-permute-start = (bf16[2,3,256,128]{3,2,1,0:T(8,128)(2,1)S(1)}, bf16[2,3,256,128]{3,2,1,0:T(8,128)(2,1)S(1)}, u32[]{:S(2)}, u32[]{:S(2)}) collective-permute-start(bf16[2,3,256,128]{3,2,1,0:T(8,128)(2,1)S(1)} %pad_maximum_fusion.1.refs_0_), channel_id=1, source_target_pairs={{0,64},{64,0},{1,65},{65,1},{2,66},{66,2},{3,67},{67,3},{4,68},{68... | collective-permute-start | bytes 1179656 | tf_op jit(solution)/shard_map/ppermute | solution.py:617
  22.2 9.3 %copy-start.45 = (s32[3,16]{1,0:T(4,128)S(1)}, s32[3,16]{1,0:T(4,128)}, u32[]{:S(2)}) copy-start(s32[3,16]{1,0:T(4,128)} %param.12) | copy-start | bytes 580
  22.2 9.9 %copy-start.46 = (s32[4,16]{1,0:T(4,128)S(1)}, s32[4,16]{1,0:T(4,128)}, u32[]{:S(2)}) copy-start(s32[4,16]{1,0:T(4,128)} %param.13) | copy-start | bytes 772
  22.3 10.5 %copy-start.34 = (s32[5]{0:T(128)S(1)}, s32[5]{0:T(128)}, u32[]{:S(2)}) copy-start(s32[5]{0:T(128)} %stack.35.meta.refs_2_.refs_5_.refs_3_) | copy-start | bytes 64
  24.4 25.5 %collective-permute-start.3 = (bf16[128,4096]{1,0:T(8,128)(2,1)}, bf16[128,4096]{1,0:T(8,128)(2,1)S(1)}, u32[]{:S(2)}, u32[]{:S(2)}) collective-permute-start(bf16[128,4096]{1,0:T(8,128)(2,1)} %get-tuple-element.100), channel_id=1, source_target_pairs={{0,4},{4,0},{1,5},{5,1},{2,6},{6,2},{3,7},{7,3},{8,12},{12,8},{9,1... | collective-permute-start | bytes 3145736 | tf_op jit(solution)/shard_map/ppermute | solution.py:625
  25.8 25.2 %collective-permute-start.4 = (bf16[128,4096]{1,0:T(8,128)(2,1)}, bf16[128,4096]{1,0:T(8,128)(2,1)S(1)}, u32[]{:S(2)}, u32[]{:S(2)}) collective-permute-start(bf16[128,4096]{1,0:T(8,128)(2,1)} %get-tuple-element.101), channel_id=1, source_target_pairs={{0,68},{4,64},{64,4},{68,0},{1,69},{5,65},{65,5},{69,1},{2,70},{6,... | collective-permute-start | bytes 3145736 | tf_op jit(solution)/shard_map/ppermute | solution.py:624
  28.3 24.9 %collective-permute-start.2 = (bf16[2,256,1024]{2,1,0:T(8,128)(2,1)}, bf16[2,256,1024]{2,1,0:T(8,128)(2,1)S(1)}, u32[]{:S(2)}, u32[]{:S(2)}) collective-permute-start(bf16[2,256,1024]{2,1,0:T(8,128)(2,1)} %get-tuple-element.99.refs_0_.own), channel_id=1, source_target_pairs={{0,1},{1,2},{2,3},{3,0},{4,5},{5,6},{6,7},{7,4},{8,9},{9,10},{10,1... | collective-permute-start | bytes 3145736 | tf_op jit(solution)/shard_map/ppermute | solution.py:628
  29.9 23.5 %collective-permute-start.1 = (bf16[2,256,1024]{2,1,0:T(8,128)(2,1)}, bf16[2,256,1024]{2,1,0:T(8,128)(2,1)}, u32[]{:S(2)}, u32[]{:S(2)}) collective-permute-start(bf16[2,256,1024]{2,1,0:T(8,128)(2,1)} %get-tuple-element.99.refs_0_.own), channel_id=1, source_target_pairs={{0,3},{1,0},{2,1},{3,2},{4,7},{5,4},{6,5},{7,6},{8,11},{9,8},{10,9... | collective-permute-start | bytes 3145736 | tf_op jit(solution)/shard_map/ppermute | solution.py:627
  54.2 34.0 %collective-permute-start.7 = (bf16[128,4096]{1,0:T(8,128)(2,1)}, bf16[128,4096]{1,0:T(8,128)(2,1)S(1)}, u32[]{:S(2)}, u32[]{:S(2)}) collective-permute-start(bf16[128,4096]{1,0:T(8,128)(2,1)} %get-tuple-element.117), channel_id=1, source_target_pairs={{0,4},{4,0},{1,5},{5,1},{2,6},{6,2},{3,7},{7,3},{8,12},{12,8},{9,1... | collective-permute-start | bytes 3145736 | tf_op jit(solution)/shard_map/ppermute | solution.py:625
  55.3 33.0 %collective-permute-start.8 = (bf16[128,4096]{1,0:T(8,128)(2,1)}, bf16[128,4096]{1,0:T(8,128)(2,1)S(1)}, u32[]{:S(2)}, u32[]{:S(2)}) collective-permute-start(bf16[128,4096]{1,0:T(8,128)(2,1)} %get-tuple-element.118), channel_id=1, source_target_pairs={{0,68},{4,64},{64,4},{68,0},{1,69},{5,65},{65,5},{69,1},{2,70},{6,... | collective-permute-start | bytes 3145736 | tf_op jit(solution)/shard_map/ppermute | solution.py:624
  56.1 32.2 %collective-permute-start.6 = (bf16[2,256,1024]{2,1,0:T(8,128)(2,1)}, bf16[2,256,1024]{2,1,0:T(8,128)(2,1)S(1)}, u32[]{:S(2)}, u32[]{:S(2)}) collective-permute-start(bf16[2,256,1024]{2,1,0:T(8,128)(2,1)} %get-tuple-element.114.refs_6_), channel_id=1, source_target_pairs={{0,3},{1,0},{2,1},{3,2},{4,7},{5,4},{6,5},{7,6},{8,11},{9,8},{10,9... | collective-permute-start | bytes 3145736 | tf_op jit(solution)/shard_map/ppermute | solution.py:639
  58.3 30.0 %collective-permute-start.5 = (bf16[2,256,1024]{2,1,0:T(8,128)(2,1)}, bf16[2,256,1024]{2,1,0:T(8,128)(2,1)}, u32[]{:S(2)}, u32[]{:S(2)}) collective-permute-start(bf16[2,256,1024]{2,1,0:T(8,128)(2,1)} %get-tuple-element.113.refs_1_.below), channel_id=1, source_target_pairs={{0,1},{1,2},{2,3},{3,0},{4,5},{5,6},{6,7},{7,4},{8,9},{9,10},{10,1... | collective-permute-start | bytes 3145736 | tf_op jit(solution)/shard_map/ppermute | solution.py:638
  71.0 2.6 %collective-permute-start.9 = (bf16[6,2,256,128]{3,2,1,0:T(8,128)(2,1)}, bf16[6,2,256,128]{3,2,1,0:T(8,128)(2,1)S(1)}, u32[]{:S(2)}, u32[]{:S(2)}) collective-permute-start(bf16[6,2,256,128]{3,2,1,0:T(8,128)(2,1)} %get-tuple-element.127), channel_id=1, source_target_pairs={{0,8},{8,0},{1,9},{9,1},{2,10},{10,2},{3,11},{11,3},{4,12},{12,4},... | collective-permute-start | bytes 2359304 | tf_op jit(solution)/shard_map/ppermute | solution.py:646
  90.0 2.9 %collective-permute-start.12 = (bf16[128,4096]{1,0:T(8,128)(2,1)}, bf16[128,4096]{1,0:T(8,128)(2,1)S(1)}, u32[]{:S(2)}, u32[]{:S(2)}) collective-permute-start(bf16[128,4096]{1,0:T(8,128)(2,1)} %get-tuple-element.139.refs_0_), channel_id=1, source_target_pairs={{0,8},{8,0},{1,9},{9,1},{2,10},{10,2},{3,11},{11,3},{4,12},{12,4},... | collective-permute-start | bytes 3145736 | tf_op jit(solution)/shard_map/ppermute | solution.py:661
  90.2 12.5 %collective-permute-start.13 = (bf16[128,4096]{1,0:T(8,128)(2,1)}, bf16[128,4096]{1,0:T(8,128)(2,1)S(1)}, u32[]{:S(2)}, u32[]{:S(2)}) collective-permute-start(bf16[128,4096]{1,0:T(8,128)(2,1)} %get-tuple-element.140.refs_1_), channel_id=1, source_target_pairs={{0,8},{8,0},{1,9},{9,1},{2,10},{10,2},{3,11},{11,3},{4,12},{12,4},... | collective-permute-start | bytes 3145736 | tf_op jit(solution)/shard_map/ppermute | solution.py:661
  90.6 12.1 %collective-permute-start.14 = (bf16[128,4096]{1,0:T(8,128)(2,1)}, bf16[128,4096]{1,0:T(8,128)(2,1)S(1)}, u32[]{:S(2)}, u32[]{:S(2)}) collective-permute-start(bf16[128,4096]{1,0:T(8,128)(2,1)} %get-tuple-element.141.refs_2_), channel_id=1, source_target_pairs={{0,8},{8,0},{1,9},{9,1},{2,10},{10,2},{3,11},{11,3},{4,12},{12,4},... | collective-permute-start | bytes 3145736 | tf_op jit(solution)/shard_map/ppermute | solution.py:661
  90.7 12.0 %collective-permute-start.15 = (bf16[128,4096]{1,0:T(8,128)(2,1)}, bf16[128,4096]{1,0:T(8,128)(2,1)}, u32[]{:S(2)}, u32[]{:S(2)}) collective-permute-start(bf16[128,4096]{1,0:T(8,128)(2,1)} %get-tuple-element.142.refs_3_), channel_id=1, source_target_pairs={{0,8},{8,0},{1,9},{9,1},{2,10},{10,2},{3,11},{11,3},{4,12},{12,4},... | collective-permute-start | bytes 3145736 | tf_op jit(solution)/shard_map/ppermute | solution.py:661
  91.1 26.9 %collective-permute-start.10 = (bf16[2,256,1024]{2,1,0:T(8,128)(2,1)}, bf16[2,256,1024]{2,1,0:T(8,128)(2,1)S(1)}, u32[]{:S(2)}, u32[]{:S(2)}) collective-permute-start(bf16[2,256,1024]{2,1,0:T(8,128)(2,1)} %get-tuple-element.131.own), channel_id=1, source_target_pairs={{0,1},{1,2},{2,3},{3,0},{4,5},{5,6},{6,7},{7,4},{8,9},{9,10},{10,1... | collective-permute-start | bytes 3145736 | tf_op jit(solution)/shard_map/ppermute | solution.py:657
  92.9 26.3 %collective-permute-start.11 = (bf16[2,256,1024]{2,1,0:T(8,128)(2,1)}, bf16[2,256,1024]{2,1,0:T(8,128)(2,1)S(1)}, u32[]{:S(2)}, u32[]{:S(2)}) collective-permute-start(bf16[2,256,1024]{2,1,0:T(8,128)(2,1)} %get-tuple-element.130.above.refs_0_), channel_id=1, source_target_pairs={{0,3},{1,0},{2,1},{3,2},{4,7},{5,4},{6,5},{7,6},{8,11},{9,8},{10,9... | collective-permute-start | bytes 3145736 | tf_op jit(solution)/shard_map/ppermute | solution.py:658
  102.8 16.4 %copy-start.4 = (bf16[2,256,1024]{2,1,0:T(8,128)(2,1)S(1)}, bf16[2,256,1024]{2,1,0:T(8,128)(2,1)}, u32[]{:S(2)}) copy-start(bf16[2,256,1024]{2,1,0:T(8,128)(2,1)} %get-tuple-element.131.own) | copy-start | bytes 3145732
  102.8 16.4 %copy-start.17 = (bf16[2,256,1024]{2,1,0:T(8,128)(2,1)S(1)}, bf16[2,256,1024]{2,1,0:T(8,128)(2,1)}, u32[]{:S(2)}) copy-start(bf16[2,256,1024]{2,1,0:T(8,128)(2,1)} %get-tuple-element.130.above.refs_0_) | copy-start | bytes 3145732
  110.7 16.1 %collective-permute-start.17 = (bf16[8,256,128]{2,1,0:T(8,128)(2,1)S(1)}, bf16[8,256,128]{2,1,0:T(8,128)(2,1)S(1)}, u32[]{:S(2)}, u32[]{:S(2)}) collective-permute-start(bf16[8,256,128]{2,1,0:T(8,128)(2,1)S(1)} %get-tuple-element.148), channel_id=1, source_target_pairs={{0,4},{4,0},{1,5},{5,1},{2,6},{6,2},{3,7},{7,3},{8,12},{12,8},{9,1... | collective-permute-start | bytes 1572872 | tf_op jit(solution)/shard_map/ppermute | solution.py:667
  111.7 24.0 %collective-permute-start.16 = (bf16[8,256,128]{2,1,0:T(8,128)(2,1)S(1)}, bf16[8,256,128]{2,1,0:T(8,128)(2,1)S(1)}, u32[]{:S(2)}, u32[]{:S(2)}) collective-permute-start(bf16[8,256,128]{2,1,0:T(8,128)(2,1)S(1)} %get-tuple-element.144), channel_id=1, source_target_pairs={{0,4},{4,0},{1,5},{5,1},{2,6},{6,2},{3,7},{7,3},{8,12},{12,8},{9,1... | collective-permute-start | bytes 1572872 | tf_op jit(solution)/shard_map/ppermute | solution.py:667
  119.2 7.6 %copy-start.10 = (bf16[4,1,256,128]{3,2,1,0:T(8,128)(2,1)S(1)}, bf16[4,1,256,128]{3,2,1,0:T(8,128)(2,1)}, u32[]{:S(2)}) copy-start(bf16[4,1,256,128]{3,2,1,0:T(8,128)(2,1)} %own_value.11) | copy-start | bytes 786436
  119.2 7.6 %copy-start.11 = (bf16[4,1,256,128]{3,2,1,0:T(8,128)(2,1)S(1)}, bf16[4,1,256,128]{3,2,1,0:T(8,128)(2,1)}, u32[]{:S(2)}) copy-start(bf16[4,1,256,128]{3,2,1,0:T(8,128)(2,1)} %own_key.11) | copy-start | bytes 786436
  119.2 7.6 %copy-start.25 = (bf16[2,1024,1024]{2,1,0:T(8,128)(2,1)S(1)}, bf16[2,1024,1024]{2,1,0:T(8,128)(2,1)}, u32[]{:S(2)}) copy-start(bf16[2,1024,1024]{2,1,0:T(8,128)(2,1)} %get-tuple-element.146.probs_ref) | copy-start | bytes 12582916
  119.2 7.6 %copy-start.30 = (f32[128,2048]{1,0:T(8,128)S(1)}, f32[128,2048]{1,0:T(8,128)}, u32[]{:S(2)}) copy-start(f32[128,2048]{1,0:T(8,128)} %get-tuple-element.147.average) | copy-start | bytes 3145732
  119.2 7.6 %copy-start.33 = (f32[8,2048]{1,0:T(8,128)S(1)}, f32[8,2048]{1,0:T(8,128)}, u32[]{:S(2)}) copy-start(f32[8,2048]{1,0:T(8,128)} %get-tuple-element.135.inverse) | copy-start | bytes 196612
  126.9 8.8 %copy-start.27 = (bf16[2,768,1024]{2,1,0:T(8,128)(2,1)S(1)}, bf16[2,768,1024]{2,1,0:T(8,128)(2,1)}, u32[]{:S(2)}) copy-start(bf16[2,768,1024]{2,1,0:T(8,128)(2,1)} %get-tuple-element.133.probs_ref) | copy-start | bytes 9437188
  126.9 8.8 %copy-start.32 = (f32[128,2048]{1,0:T(8,128)S(1)}, f32[128,2048]{1,0:T(8,128)}, u32[]{:S(2)}) copy-start(f32[128,2048]{1,0:T(8,128)} %get-tuple-element.134.average) | copy-start | bytes 3145732
  133.1 9.9 %collective-permute-start.19 = (bf16[3,2,256,128]{3,2,1,0:T(8,128)(2,1)S(1)}, bf16[3,2,256,128]{3,2,1,0:T(8,128)(2,1)S(1)}, u32[]{:S(2)}, u32[]{:S(2)}) collective-permute-start(bf16[3,2,256,128]{3,2,1,0:T(8,128)(2,1)S(1)} %get-tuple-element.153.refs_2_.refs_4_), channel_id=1, source_target_pairs={{0,8},{8,0},{1,9},{9,1},{2,10},{10,2},{3,11},{11,3},{4,12},{12,4},... | collective-permute-start | bytes 1179656 | tf_op jit(solution)/shard_map/ppermute | solution.py:686
  141.0 2.0 %collective-permute-start.18 = (bf16[2,2,256,128]{3,2,1,0:T(8,128)(2,1)S(1)}, bf16[2,2,256,128]{3,2,1,0:T(8,128)(2,1)S(1)}, u32[]{:S(2)}, u32[]{:S(2)}) collective-permute-start(bf16[2,2,256,128]{3,2,1,0:T(8,128)(2,1)S(1)} %get-tuple-element.152.refs_0_.refs_2_), channel_id=1, source_target_pairs={{0,8},{8,0},{1,9},{9,1},{2,10},{10,2},{3,11},{11,3},{4,12},{12,4},... | collective-permute-start | bytes 786440 | tf_op jit(solution)/shard_map/ppermute | solution.py:686
  141.0 16.5 %collective-permute-start.21 = (bf16[8,256,128]{2,1,0:T(8,128)(2,1)}, bf16[8,256,128]{2,1,0:T(8,128)(2,1)S(1)}, u32[]{:S(2)}, u32[]{:S(2)}) collective-permute-start(bf16[8,256,128]{2,1,0:T(8,128)(2,1)} %get-tuple-element.160), channel_id=1, source_target_pairs={{0,4},{4,0},{1,5},{5,1},{2,6},{6,2},{3,7},{7,3},{8,12},{12,8},{9,1... | collective-permute-start | bytes 1572872 | tf_op jit(solution)/shard_map/ppermute | solution.py:667
  141.9 24.9 %collective-permute-start.20 = (bf16[8,256,128]{2,1,0:T(8,128)(2,1)}, bf16[8,256,128]{2,1,0:T(8,128)(2,1)S(1)}, u32[]{:S(2)}, u32[]{:S(2)}) collective-permute-start(bf16[8,256,128]{2,1,0:T(8,128)(2,1)} %get-tuple-element.157), channel_id=1, source_target_pairs={{0,4},{4,0},{1,5},{5,1},{2,6},{6,2},{3,7},{7,3},{8,12},{12,8},{9,1... | collective-permute-start | bytes 1572872 | tf_op jit(solution)/shard_map/ppermute | solution.py:667
  145.2 24.3 %collective-permute-start.23 = (bf16[2,2,2,256,128]{4,3,2,1,0:T(8,128)(2,1)}, bf16[2,2,2,256,128]{4,3,2,1,0:T(8,128)(2,1)S(1)}, u32[]{:S(2)}, u32[]{:S(2)}) collective-permute-start(bf16[2,2,2,256,128]{4,3,2,1,0:T(8,128)(2,1)} %get-tuple-element.171), channel_id=1, source_target_pairs={{0,16},{16,32},{32,48},{48,0},{1,17},{17,33},{33,49},{49,1},{2,18}... | collective-permute-start | bytes 1572872 | tf_op jit(solution)/shard_map/ppermute | solution.py:698
  146.6 26.9 %collective-permute-start.24 = (bf16[2,2,2,256,128]{4,3,2,1,0:T(8,128)(2,1)}, bf16[2,2,2,256,128]{4,3,2,1,0:T(8,128)(2,1)S(1)}, u32[]{:S(2)}, u32[]{:S(2)}) collective-permute-start(bf16[2,2,2,256,128]{4,3,2,1,0:T(8,128)(2,1)} %get-tuple-element.172), channel_id=1, source_target_pairs={{0,48},{16,0},{32,16},{48,32},{1,49},{17,1},{33,17},{49,33},{2,50}... | collective-permute-start | bytes 1572872 | tf_op jit(solution)/shard_map/ppermute | solution.py:699
  148.4 25.2 %collective-permute-start.25 = (bf16[2,2,2,256,128]{4,3,2,1,0:T(8,128)(2,1)}, bf16[2,2,2,256,128]{4,3,2,1,0:T(8,128)(2,1)S(1)}, u32[]{:S(2)}, u32[]{:S(2)}) collective-permute-start(bf16[2,2,2,256,128]{4,3,2,1,0:T(8,128)(2,1)} %get-tuple-element.173), channel_id=1, source_target_pairs={{0,32},{16,48},{32,0},{48,16},{1,33},{17,49},{33,1},{49,17},{2,34}... | collective-permute-start | bytes 1572872 | tf_op jit(solution)/shard_map/ppermute | solution.py:700
  157.5 12.8 %copy-start.31 = (f32[128,2048]{1,0:T(8,128)S(1)}, f32[128,2048]{1,0:T(8,128)}, u32[]{:S(2)}) copy-start(f32[128,2048]{1,0:T(8,128)} %get-tuple-element.111.average) | copy-start | bytes 3145732
  157.6 12.7 %copy-start.37 = (f32[8,2048]{1,0:T(8,128)S(1)}, f32[8,2048]{1,0:T(8,128)}, u32[]{:S(2)}) copy-start(f32[8,2048]{1,0:T(8,128)} %get-tuple-element.112.inverse) | copy-start | bytes 196612
  161.8 8.5 %copy-start.26 = (bf16[2,256,1024]{2,1,0:T(8,128)(2,1)S(1)}, bf16[2,256,1024]{2,1,0:T(8,128)(2,1)}, u32[]{:S(2)}) copy-start(bf16[2,256,1024]{2,1,0:T(8,128)(2,1)} %get-tuple-element.110.probs_ref) | copy-start | bytes 3145732
  161.8 1.3 collective-permute-start.22
  164.5 14.6 %collective-permute-start.27 = (bf16[1,2,2,256,128]{4,3,2,1,0:T(8,128)(2,1)S(1)}, bf16[1,2,2,256,128]{4,3,2,1,0:T(8,128)(2,1)S(1)}, u32[]{:S(2)}, u32[]{:S(2)}) collective-permute-start(bf16[1,2,2,256,128]{4,3,2,1,0:T(8,128)(2,1)S(1)} %get-tuple-element.177), channel_id=1, source_target_pairs={{0,16},{16,32},{32,48},{48,0},{1,17},{17,33},{33,49},{49,1},{2,18}... | collective-permute-start | bytes 786440 | tf_op jit(solution)/shard_map/ppermute | solution.py:698
  166.8 12.4 %collective-permute-start.28 = (bf16[1,2,2,256,128]{4,3,2,1,0:T(8,128)(2,1)S(1)}, bf16[1,2,2,256,128]{4,3,2,1,0:T(8,128)(2,1)S(1)}, u32[]{:S(2)}, u32[]{:S(2)}) collective-permute-start(bf16[1,2,2,256,128]{4,3,2,1,0:T(8,128)(2,1)S(1)} %get-tuple-element.178), channel_id=1, source_target_pairs={{0,48},{16,0},{32,16},{48,32},{1,49},{17,1},{33,17},{49,33},{2,50}... | collective-permute-start | bytes 786440 | tf_op jit(solution)/shard_map/ppermute | solution.py:699
  169.5 14.3 %collective-permute-start.29 = (bf16[1,2,2,256,128]{4,3,2,1,0:T(8,128)(2,1)S(1)}, bf16[1,2,2,256,128]{4,3,2,1,0:T(8,128)(2,1)S(1)}, u32[]{:S(2)}, u32[]{:S(2)}) collective-permute-start(bf16[1,2,2,256,128]{4,3,2,1,0:T(8,128)(2,1)S(1)} %get-tuple-element.179), channel_id=1, source_target_pairs={{0,32},{16,48},{32,0},{48,16},{1,33},{17,49},{33,1},{49,17},{2,34}... | collective-permute-start | bytes 786440 | tf_op jit(solution)/shard_map/ppermute | solution.py:700
  174.4 17.1 %collective-permute-start.26 = (bf16[2,2,256,128]{3,2,1,0:T(8,128)(2,1)S(1)}, bf16[2,2,256,128]{3,2,1,0:T(8,128)(2,1)S(1)}, u32[]{:S(2)}, u32[]{:S(2)}) collective-permute-start(bf16[2,2,256,128]{3,2,1,0:T(8,128)(2,1)S(1)} %get-tuple-element.175), channel_id=1, source_target_pairs={{0,64},{64,0},{1,65},{65,1},{2,66},{66,2},{3,67},{67,3},{4,68},{68... | collective-permute-start | bytes 786440 | tf_op jit(solution)/shard_map/ppermute | solution.py:712
  185.0 6.5 %collective-permute-start.30 = (bf16[1,2,256,128]{3,2,1,0:T(8,128)(2,1)S(1)}, bf16[1,2,256,128]{3,2,1,0:T(8,128)(2,1)S(1)}, u32[]{:S(2)}, u32[]{:S(2)}) collective-permute-start(bf16[1,2,256,128]{3,2,1,0:T(8,128)(2,1)S(1)} %get-tuple-element.182), channel_id=1, source_target_pairs={{0,64},{64,0},{1,65},{65,1},{2,66},{66,2},{3,67},{67,3},{4,68},{68... | collective-permute-start | bytes 393224 | tf_op jit(solution)/shard_map/ppermute | solution.py:714
  (31 other events, 112.8 us)
Sparse Core Ops, SparseCore 0:
  24.5 41.2 all-gather.2

commit v3 on v2

--- a/solution.py
+++ b/solution.py
@@ -169,7 +169,7 @@
             out_specs=[part, TOKEN],
         ),
         out_shape=[jax.ShapeDtypeStruct((2, SEG, FEATURES), dtype), TOKEN_SHAPE],
-        compiler_params=LARGE,
+        compiler_params=PARAMS if dtype == jnp.float32 else LARGE,
         cost_estimate=cost(count * SEG * 1024 * HALF, 2 * 1024 * HALF),
         name="own_product",
     )(meta, *cots, *[weight] * count, *earlier, token)

time: 200 us -> 198 us (0.990)
  local copies, waits for them, and re-layouts: 16.5 us -> 8.89 us
  Pallas kernels: 95 us -> 99.6 us
  waiting for transfers between devices: 30.7 us -> 33.7 us
    unnamed x94 -> x74, local copies, waits for them, and re-layouts: 13.6 us -> 5.9 us
    pallas_call x5, Pallas kernels: 27 us -> 31.4 us  [blocks_product(): pl.pallas_call(functools.partial(blocks_kernel, count, len(earlier)), gri...]
    ppermute x1, starting transfers between devices: 4.45 us -> 2.23 us  [local(): high_given = lax.ppermute(high_given, 'zh', SWAP)]
    ppermute x2, waiting for transfers between devices: 0.28 us -> 2.5 us  [send(): lax.ppermute(up, 'x', UP)]
  transfers between devices with their start and end apart: 32 -> 32, of which waited for: 15 -> 16; matrix products, arithmetic and copies ran while one was open for 1% -> 1% of each run, Pallas kernels for 47% -> 50%
where the time goes in v3:
time: 198 us
  Pallas kernels  99.6 us (50%)
  starting transfers between devices  38.7 us (20%)
  waiting for transfers between devices  33.7 us (17%)
  between operations  14.5 us (7%)
  local copies, waits for them, and re-layouts  8.89 us (4%)
  other arithmetic  2.14 us (1%)
    pallas_call x5, Pallas kernels, blocks_product(): pl.pallas_call(functools.partial(blocks_kernel, count, len(earlier)), gri...  31.4 us
    pallas_call x4, Pallas kernels, backward(): pl.pallas_call(functools.partial(backward_kernel, level, len(arrived)), g...  18.9 us
    pallas_call x2, Pallas kernels, probs(): pl.pallas_call(functools.partial(probs_kernel, levels), grid_spec=pltpu.P...  18 us
    pallas_call x2, Pallas kernels, product(): pl.pallas_call(product_kernel, grid_spec=pltpu.PrefetchScalarGridSpec(num...  15.4 us
    pallas_call x1, Pallas kernels, prepare(): pl.pallas_call(prepare_kernel, grid_spec=pltpu.PrefetchScalarGridSpec(num...  6.13 us
    unnamed x74, local copies, waits for them, and re-layouts  5.9 us
    ppermute x1, waiting for transfers between devices, local(): below_low = lax.ppermute(lower, 'y', UP)  5.13 us
    ppermute x2, waiting for transfers between devices, send(): lax.ppermute(across, 'x', ACROSS)  4.85 us
  transfers between devices with their start and end apart: 32, of which 16 were waited for; matrix products, arithmetic and copies ran while one was open for 1% of the time, Pallas kernels for 50%

profile of v3, /device:TPU:0, one launch (start us, length us, event | category | flops | bytes accessed | tf_op | source)
XLA Modules:
  0.0 197.6 jit_solution(17761859670163364601)
XLA Ops:
  7.2 1.1 slice_bitcast_fusion
  8.3 4.0 %collective-permute-start = (bf16[2,3,256,128]{3,2,1,0:T(8,128)(2,1)S(1)}, bf16[2,3,256,128]{3,2,1,0:T(8,128)(2,1)S(1)}, u32[]{:S(2)}, u32[]{:S(2)}) collective-permute-start(bf16[2,3,256,128]{3,2,1,0:T(8,128)(2,1)S(1)} %pad_maximum_fusion.1.refs_0_), channel_id=1, source_target_pairs={{0,64},{64,0},{1,65},{65,1},{2,66},{66,2},{3,67},{67,3},{4,68},{68... | collective-permute-start | bytes 1179656 | tf_op jit(solution)/shard_map/ppermute | solution.py:617
  13.0 6.1 %prepare.1 = (bf16[128,4096]{1,0:T(8,128)(2,1)}, bf16[128,4096]{1,0:T(8,128)(2,1)}, bf16[128,4096]{1,0:T(8,128)(2,1)}, bf16[128,4096]{1,0:T(8,128)(2,1)}, bf16[2...) custom-call(s32[5]{0:T(128)} %stack.35.meta.refs_2_.refs_5_.refs_3_, bf16[1024,8192]{1,0:T(8,128)(2,1)} %refs_5_.1, ...), custom_call_target="tpu_custom_call" | custom-call | flops 1 | bytes 1 | tf_op jit(solution)/shard_map/prepare/pallas_call | solution.py:95
  19.1 2.4 %collective-permute-done.refs_1_ = bf16[2,3,256,128]{3,2,1,0:T(8,128)(2,1)S(1)} collective-permute-done((bf16[2,3,256,128]{3,2,1,0:T(8,128)(2,1)S(1)}, bf16[2,3,256,128]{3,2,1,0:T(8,128)(2,1)S(1)}, u32[]{:S(2)}, u32[]{:S(2)}) %collective-permute-start) | collective-permute-done | bytes 393248 | tf_op jit(solution)/shard_map/ppermute | solution.py:617
  22.2 2.1 %pad_maximum_fusion = bf16[2,2,3,256,128]{4,3,2,1,0:T(8,128)(2,1)} fusion(bf16[1,2,3,256,128]{4,3,2,1,0:T(8,128)(2,1)} %bitcast.18, bf16[1,2,3,256,128]{4,3,2,1,0:T(8,128)(2,1)} %bitcast.17), kind=kLoop, calls=%fused_computation | loop fusion | flops 393216 | bytes 1572864 | tf_op jit(solution)/shard_map/stack | solution.py:620
  24.4 1.4 collective-permute-start.3
  25.7 2.5 %collective-permute-start.4 = (bf16[128,4096]{1,0:T(8,128)(2,1)}, bf16[128,4096]{1,0:T(8,128)(2,1)S(1)}, u32[]{:S(2)}, u32[]{:S(2)}) collective-permute-start(bf16[128,4096]{1,0:T(8,128)(2,1)} %get-tuple-element.101), channel_id=1, source_target_pairs={{0,68},{4,64},{64,4},{68,0},{1,69},{5,65},{65,5},{69,1},{2,70},{6,... | collective-permute-start | bytes 3145736 | tf_op jit(solution)/shard_map/ppermute | solution.py:624
  28.2 1.6 collective-permute-start.2
  29.8 1.7 collective-permute-start.1
  32.8 5.8 %own_product.5 = (f32[2,256,1024]{2,1,0:T(8,128)}, f32[8,128]{1,0:T(8,128)}) custom-call(s32[5]{0:T(128)} %stack.35.meta.refs_2_.refs_5_.refs_3_, bf16[2,256,1024]{2,1,0:T(8,128)(2,1)} %get-tuple-element.99.refs_0_.own, bf16[1024,8192]{1,0:T(8,128)(2,1)} %refs_5_.1, s32[5]{0:T(128)} %stack.35.meta.refs_2_.refs_5_.refs_3_), custom_call_target="tpu_custom_call" | custom-call | flops 1 | bytes 1 | tf_op jit(solution)/shard_map/own_product/pallas_call | solution.py:160
  38.6 5.7 %own_product.6 = (f32[2,256,1024]{2,1,0:T(8,128)}, f32[8,128]{1,0:T(8,128)}) custom-call(s32[5]{0:T(128)} %stack.35.meta.refs_2_.refs_5_.refs_3_, bf16[2,256,1024]{2,1,0:T(8,128)(2,1)} %get-tuple-element.102.refs_0_.refs_4_, bf16[1024,8192]{1,0:T(8,128)(2,1)} %refs_5_.1, f32[8,128]{1,0:T(8,128)} %get-tuple-element.106.refs_2_), custom_call_target="tpu_custom_call" | custom-call | flops 1 | bytes 1 | tf_op jit(solution)/shard_map/own_product/pallas_call | solution.py:160
  44.3 4.2 %probs.2 = (bf16[2,256,1024]{2,1,0:T(8,128)(2,1)}, f32[128,2048]{1,0:T(8,128)}, f32[8,2048]{1,0:T(8,128)}) custom-call(s32[5]{0:T(128)} %stack.35.meta.refs_2_.refs_5_.refs_3_, s32[48]{0:T(128)} %reshape.12.parents, s32[64]{0:T(128)} %reshape.13.lengths, bf16[4,1,256,1024]{3,2,1,0:T(8,128)(2,1)} %query.11, bf16[4,1,256,128]{3,2,1,0:T(8,128)(2,1)} %own_key.11, ...), custom_call_target="tpu_custom_call" | custom-call | flops 1 | bytes 1 | tf_op jit(solution)/shard_map/probs/pallas_call | solution.py:379
  49.0 1.9 collective-permute-done.4.refs_3_
  50.9 2.3 %collective-permute-done.2.refs_1_ = bf16[2,256,1024]{2,1,0:T(8,128)(2,1)S(1)} collective-permute-done((bf16[2,256,1024]{2,1,0:T(8,128)(2,1)}, bf16[2,256,1024]{2,1,0:T(8,128)(2,1)S(1)}, u32[]{:S(2)}, u32[]{:S(2)}) %collective-permute-start.2) | collective-permute-done | bytes 1048608 | tf_op jit(solution)/shard_map/ppermute | solution.py:628
  56.2 2.1 %collective-permute-start.6 = (bf16[2,256,1024]{2,1,0:T(8,128)(2,1)}, bf16[2,256,1024]{2,1,0:T(8,128)(2,1)S(1)}, u32[]{:S(2)}, u32[]{:S(2)}) collective-permute-start(bf16[2,256,1024]{2,1,0:T(8,128)(2,1)} %get-tuple-element.114.refs_6_), channel_id=1, source_target_pairs={{0,3},{1,0},{2,1},{3,2},{4,7},{5,4},{6,5},{7,6},{8,11},{9,8},{10,9... | collective-permute-start | bytes 3145736 | tf_op jit(solution)/shard_map/ppermute | solution.py:639
  58.3 7.7 %own_product.7 = (f32[2,256,1024]{2,1,0:T(8,128)}, f32[8,128]{1,0:T(8,128)}) custom-call(s32[5]{0:T(128)} %stack.35.meta.refs_2_.refs_5_.refs_3_, bf16[2,256,1024]{2,1,0:T(8,128)(2,1)} %get-tuple-element.121.refs_0_.above, bf16[2,256,1024]{2,1,0:T(8,128)(2,1)} %get-tuple-element.113.refs_1_.below, bf16[1024,8192]{1,0:T(8,128)(2,1)} %refs_5_.1, ...), custom_call_target="tpu_custom_call" | custom-call | flops 1 | bytes 1 | tf_op jit(solution)/shard_map/own_product/pallas_call | solution.py:160
  66.0 3.3 %pick.1 = (bf16[6,2,256,128]{3,2,1,0:T(8,128)(2,1)}, bf16[6,2,256,128]{3,2,1,0:T(8,128)(2,1)}) custom-call(s32[5]{0:T(128)} %stack.35.meta.refs_2_.refs_5_.refs_3_, s32[48]{0:T(128)} %reshape.12.parents, bf16[4,2,2,3,256,128]{5,4,3,2,1,0:T(8,128)(2,1)} %get-tuple-element.125.mine), custom_call_target="tpu_custom_call" | custom-call | flops 1 | bytes 1 | tf_op jit(solution)/shard_map/pick/pallas_call | solution.py:281
  69.4 2.5 %collective-permute-done.9.refs_1_ = bf16[6,2,256,128]{3,2,1,0:T(8,128)(2,1)S(1)} collective-permute-done((bf16[6,2,256,128]{3,2,1,0:T(8,128)(2,1)}, bf16[6,2,256,128]{3,2,1,0:T(8,128)(2,1)S(1)}, u32[]{:S(2)}, u32[]{:S(2)}) %collective-permute-start.9) | collective-permute-done | bytes 786464 | tf_op jit(solution)/shard_map/ppermute | solution.py:646
  72.8 13.8 %probs.3 = (bf16[2,1024,1024]{2,1,0:T(8,128)(2,1)}, bf16[2,768,1024]{2,1,0:T(8,128)(2,1)}, bf16[2,512,1024]{2,1,0:T(8,128)(2,1)}, f32[128,2048]{1,0:T(8,128)}, f...) custom-call(s32[5]{0:T(128)} %stack.35.meta.refs_2_.refs_5_.refs_3_, ...), custom_call_target="tpu_custom_call" | custom-call | flops 1 | bytes 1 | tf_op jit(solution)/shard_map/probs/pallas_call | solution.py:379
  89.3 1.3 collective-permute-start.10
  91.1 3.2 %collective-permute-start.11 = (bf16[2,256,1024]{2,1,0:T(8,128)(2,1)}, bf16[2,256,1024]{2,1,0:T(8,128)(2,1)S(1)}, u32[]{:S(2)}, u32[]{:S(2)}) collective-permute-start(bf16[2,256,1024]{2,1,0:T(8,128)(2,1)} %get-tuple-element.130.above.refs_0_), channel_id=1, source_target_pairs={{0,3},{1,0},{2,1},{3,2},{4,7},{5,4},{6,5},{7,6},{8,11},{9,8},{10,9... | collective-permute-start | bytes 3145736 | tf_op jit(solution)/shard_map/ppermute | solution.py:658
  94.4 1.6 copy-done.1
  96.0 4.9 %own_product.8 = (bf16[2,256,1024]{2,1,0:T(8,128)(2,1)S(1)}, f32[8,128]{1,0:T(8,128)S(1)}) custom-call(s32[5]{0:T(128)S(1)} %copy-done.28, bf16[2,256,1024]{2,1,0:T(8,128)(2,1)} %get-tuple-element.136.refs_0_.across, bf16[1024,8192]{1,0:T(8,128)(2,1)} %refs_5_.1, f32[2,256,1024]{2,1,0:T(8,128)S(1)} %copy-done.1, s32[5]{0:T(128)S(1)} %copy-done.28), custom_call_target="tpu_custom_call" | custom-call | flops 1 | bytes 1 | tf_op jit(solution)/shard_map/own_product/pallas_call | solution.py:160
  101.0 7.9 %partner_product.2 = (bf16[8,256,128]{2,1,0:T(8,128)(2,1)S(1)}, bf16[8,256,128]{2,1,0:T(8,128)(2,1)S(1)}, f32[8,128]{1,0:T(8,128)S(1)}) custom-call(s32[5]{0:T(128)S(1)} %copy-done.28, bf16[2,256,1024]{2,1,0:T(8,128)(2,1)S(1)} %copy-done.18, bf16[2,256,1024]{2,1,0:T(8,128)(2,1)} %get-tuple-element.121.refs_0_.above, bf16[2,256,1024]{2,1,0:T(8,128)(2,1)S(1)} %copy-done.17, ...), custom_call_target="tpu_custom_call" | custom-call | flops 1 | bytes 1 | tf_op jit(solution)/shard_map/partner_product/pallas_call | solution.py:231
  108.9 1.1 collective-permute-start.17
  111.0 5.1 %collective-permute-done.10.below.refs_1_ = bf16[2,256,1024]{2,1,0:T(8,128)(2,1)S(1)} collective-permute-done((bf16[2,256,1024]{2,1,0:T(8,128)(2,1)}, bf16[2,256,1024]{2,1,0:T(8,128)(2,1)S(1)}, u32[]{:S(2)}, u32[]{:S(2)}) %collective-permute-start.10) | collective-permute-done | bytes 1048608 | tf_op jit(solution)/shard_map/ppermute | solution.py:657
  116.2 1.2 collective-permute-done.11.across.refs_2_
  117.5 7.5 %partner_product.3 = (bf16[8,256,128]{2,1,0:T(8,128)(2,1)}, bf16[8,256,128]{2,1,0:T(8,128)(2,1)}, f32[8,128]{1,0:T(8,128)S(1)}) custom-call(s32[5]{0:T(128)S(1)} %copy-done.28, bf16[2,256,1024]{2,1,0:T(8,128)(2,1)S(1)} %copy-done.2, bf16[2,256,1024]{2,1,0:T(8,128)(2,1)S(1)} %copy-done.15, bf16[2,256,1024]{2,1,0:T(8,128)(2,1)S(1)} %collective-permute-done.10.below.refs_1_, ...), custom_call_target="tpu_custom_call" | custom-call | flops 1 | bytes 1 | tf_op jit(solution)/shard_map/partner_product/pallas_call | solution.py:231
  125.1 6.2 %backward_3.1 = (bf16[4,1,256,1024]{3,2,1,0:T(8,128)(2,1)}, f32[2,256,128]{2,1,0:T(8,128)S(1)}, bf16[3,2,256,128]{3,2,1,0:T(8,128)(2,1)S(1)}) custom-call(s32[5]{0:T(128)S(1)} %copy-done.28, s32[48]{0:T(128)S(1)} %copy-done.30, s32[64]{0:T(128)S(1)} %copy-done.31, bf16[2,1024,1024]{2,1,0:T(8,128)(2,1)S(1)} %copy-done.19, f32[128,2048]{1,0:T(8,128)S(1)} %copy-done.24, ...), custom_call_target="tpu_custom_call" | custom-call | flops 1 | bytes 1 | tf_op jit(solution)/shard_map/backward_3/pallas_call | solution.py:476
  131.3 2.6 %collective-permute-done.16.partner = bf16[8,256,128]{2,1,0:T(8,128)(2,1)S(1)} collective-permute-done((bf16[8,256,128]{2,1,0:T(8,128)(2,1)S(1)}, bf16[8,256,128]{2,1,0:T(8,128)(2,1)S(1)}, u32[]{:S(2)}, u32[]{:S(2)}) %collective-permute-start.16) | collective-permute-done | bytes 524320 | tf_op jit(solution)/shard_map/ppermute | solution.py:667
  133.9 5.2 %backward_2.1 = (bf16[4,1,256,1024]{3,2,1,0:T(8,128)(2,1)}, f32[2,256,128]{2,1,0:T(8,128)S(1)}, bf16[2,2,256,128]{3,2,1,0:T(8,128)(2,1)S(1)}) custom-call(s32[5]{0:T(128)S(1)} %copy-done.28, s32[48]{0:T(128)S(1)} %copy-done.30, s32[64]{0:T(128)S(1)} %copy-done.31, bf16[2,768,1024]{2,1,0:T(8,128)(2,1)S(1)} %copy-done.21, ...), custom_call_target="tpu_custom_call", output_to_operand_aliasing={{0}: (12, {})} | custom-call | flops 1 | bytes 1 | tf_op jit(solution)/shard_map/backward_2/pallas_call | solution.py:476
  141.2 2.2 %spread.2 = (bf16[2,2,2,256,128]{4,3,2,1,0:T(8,128)(2,1)S(1)}, bf16[2,2,2,256,128]{4,3,2,1,0:T(8,128)(2,1)}, bf16[2,2,2,256,128]{4,3,2,1,0:T(8,128)(2,1)}, bf16[...) custom-call(s32[5]{0:T(128)S(1)} %copy-done.28, s32[48]{0:T(128)S(1)} %copy-done.30, ...), custom_call_target="tpu_custom_call" | custom-call | flops 1 | bytes 1 | tf_op jit(solution)/shard_map/spread/pallas_call | solution.py:536
  143.4 1.5 collective-permute-start.23
  144.9 1.7 collective-permute-start.24
  146.6 1.8 collective-permute-start.25
  148.4 7.3 %own_product.9 = (bf16[2,256,1024]{2,1,0:T(8,128)(2,1)S(1)}, f32[8,128]{1,0:T(8,128)S(1)}) custom-call(s32[5]{0:T(128)S(1)} %copy-done.28, bf16[2,256,1024]{2,1,0:T(8,128)(2,1)S(1)} %copy-done.15, bf16[2,256,1024]{2,1,0:T(8,128)(2,1)S(1)} %collective-permute-done.10.below.refs_1_, bf16[2,256,1024]{2,1,0:T(8,128)(2,1)S(1)} %collective-permute-done.11.across.refs_2_, ...), custom_call_target="tpu_custom_call" | custom-call | flops 1 | bytes 1 | tf_op jit(solution)/shard_map/own_product/pallas_call | solution.py:160
  155.8 4.2 %backward_1.1 = (bf16[4,1,256,1024]{3,2,1,0:T(8,128)(2,1)}, f32[2,256,128]{2,1,0:T(8,128)S(1)}, bf16[1,2,256,128]{3,2,1,0:T(8,128)(2,1)S(1)}) custom-call(s32[5]{0:T(128)S(1)} %copy-done.28, s32[48]{0:T(128)S(1)} %copy-done.30, s32[64]{0:T(128)S(1)} %copy-done.31, bf16[2,512,1024]{2,1,0:T(8,128)(2,1)S(1)} %copy-done.22, ...), custom_call_target="tpu_custom_call", output_to_operand_aliasing={{0}: (12, {})} | custom-call | flops 1 | bytes 1 | tf_op jit(solution)/shard_map/backward_1/pallas_call | solution.py:476
  160.0 1.3 collective-permute-done.22.refs_1_
  161.3 1.4 spread.3
  163.5 1.5 collective-permute-done.20.partner
  165.0 2.8 %collective-permute-start.28 = (bf16[1,2,2,256,128]{4,3,2,1,0:T(8,128)(2,1)S(1)}, bf16[1,2,2,256,128]{4,3,2,1,0:T(8,128)(2,1)S(1)}, u32[]{:S(2)}, u32[]{:S(2)}) collective-permute-start(bf16[1,2,2,256,128]{4,3,2,1,0:T(8,128)(2,1)S(1)} %get-tuple-element.178), channel_id=1, source_target_pairs={{0,48},{16,0},{32,16},{48,32},{1,49},{17,1},{33,17},{49,33},{2,50}... | collective-permute-start | bytes 786440 | tf_op jit(solution)/shard_map/ppermute | solution.py:699
  168.6 3.2 %backward_0.1 = (bf16[4,1,256,1024]{3,2,1,0:T(8,128)(2,1)}, f32[2,256,128]{2,1,0:T(8,128)S(1)}) custom-call(s32[5]{0:T(128)S(1)} %copy-done.28, s32[48]{0:T(128)S(1)} %copy-done.30, s32[64]{0:T(128)S(1)} %copy-done.31, bf16[2,256,1024]{2,1,0:T(8,128)(2,1)S(1)} %copy-done.20, f32[128,2048]{1,0:T(8,128)S(1)} %copy-done.25, ...), custom_call_target="tpu_custom_call", output_to_operand_aliasing={{0}: (11, {})} | custom-call | flops 1 | bytes 1 | tf_op jit(solution)/shard_map/backward_0/pallas_call | solution.py:476
  172.7 2.2 %collective-permute-start.26 = (bf16[2,2,256,128]{3,2,1,0:T(8,128)(2,1)S(1)}, bf16[2,2,256,128]{3,2,1,0:T(8,128)(2,1)S(1)}, u32[]{:S(2)}, u32[]{:S(2)}) collective-permute-start(bf16[2,2,256,128]{3,2,1,0:T(8,128)(2,1)S(1)} %get-tuple-element.175), channel_id=1, source_target_pairs={{0,64},{64,0},{1,65},{65,1},{2,66},{66,2},{3,67},{67,3},{4,68},{68... | collective-permute-start | bytes 786440 | tf_op jit(solution)/shard_map/ppermute | solution.py:712
  175.0 2.5 %collective-permute-done.27.refs_1_ = bf16[1,2,2,256,128]{4,3,2,1,0:T(8,128)(2,1)S(1)} collective-permute-done((bf16[1,2,2,256,128]{4,3,2,1,0:T(8,128)(2,1)S(1)}, bf16[1,2,2,256,128]{4,3,2,1,0:T(8,128)(2,1)S(1)}, u32[]{:S(2)}, u32[]{:S(2)}) %collective-permute-start.27) | collective-permute-done | bytes 262176 | tf_op jit(solution)/shard_map/ppermute | solution.py:698
  177.5 4.7 %collective-permute-done.29.refs_3_ = bf16[1,2,2,256,128]{4,3,2,1,0:T(8,128)(2,1)S(1)} collective-permute-done((bf16[1,2,2,256,128]{4,3,2,1,0:T(8,128)(2,1)S(1)}, bf16[1,2,2,256,128]{4,3,2,1,0:T(8,128)(2,1)S(1)}, u32[]{:S(2)}, u32[]{:S(2)}) %collective-permute-start.29) | collective-permute-done | bytes 262176 | tf_op jit(solution)/shard_map/ppermute | solution.py:700
  182.2 1.2 collect.3
  183.3 2.1 %collective-permute-start.30 = (bf16[1,2,256,128]{3,2,1,0:T(8,128)(2,1)S(1)}, bf16[1,2,256,128]{3,2,1,0:T(8,128)(2,1)S(1)}, u32[]{:S(2)}, u32[]{:S(2)}) collective-permute-start(bf16[1,2,256,128]{3,2,1,0:T(8,128)(2,1)S(1)} %get-tuple-element.182), channel_id=1, source_target_pairs={{0,64},{64,0},{1,65},{65,1},{2,66},{66,2},{3,67},{67,3},{4,68},{68... | collective-permute-start | bytes 393224 | tf_op jit(solution)/shard_map/ppermute | solution.py:714
  185.5 4.3 %collective-permute-done.30.refs_7_ = bf16[1,2,256,128]{3,2,1,0:T(8,128)(2,1)S(1)} collective-permute-done((bf16[1,2,256,128]{3,2,1,0:T(8,128)(2,1)S(1)}, bf16[1,2,256,128]{3,2,1,0:T(8,128)(2,1)S(1)}, u32[]{:S(2)}, u32[]{:S(2)}) %collective-permute-start.30) | collective-permute-done | bytes 131104 | tf_op jit(solution)/shard_map/ppermute | solution.py:714
  (121 shorter events, 16.9 us)
Async XLA Ops:
  7.2 58.8 %all-gather.3.cloned.1.call-start = ((), (), s32[]{:S(2)}) async-start(), calls=%async_computation | async-start | bytes 3932160 | tf_op jit(solution)/shard_map/all_gather | solution.py:620
  8.3 10.8 %copy-start.32 = (bf16[2,3,256,128]{3,2,1,0:T(8,128)(2,1)}, bf16[2,3,256,128]{3,2,1,0:T(8,128)(2,1)S(1)}, u32[]{:S(2)}) copy-start(bf16[2,3,256,128]{3,2,1,0:T(8,128)(2,1)S(1)} %pad_maximum_fusion.1.refs_0_) | copy-start | bytes 1179652
  8.3 13.2 %collective-permute-start = (bf16[2,3,256,128]{3,2,1,0:T(8,128)(2,1)S(1)}, bf16[2,3,256,128]{3,2,1,0:T(8,128)(2,1)S(1)}, u32[]{:S(2)}, u32[]{:S(2)}) collective-permute-start(bf16[2,3,256,128]{3,2,1,0:T(8,128)(2,1)S(1)} %pad_maximum_fusion.1.refs_0_), channel_id=1, source_target_pairs={{0,64},{64,0},{1,65},{65,1},{2,66},{66,2},{3,67},{67,3},{4,68},{68... | collective-permute-start | bytes 1179656 | tf_op jit(solution)/shard_map/ppermute | solution.py:617
  22.2 9.3 %copy-start.35 = (s32[3,16]{1,0:T(4,128)S(1)}, s32[3,16]{1,0:T(4,128)}, u32[]{:S(2)}) copy-start(s32[3,16]{1,0:T(4,128)} %param.12) | copy-start | bytes 580
  22.2 9.9 %copy-start.36 = (s32[4,16]{1,0:T(4,128)S(1)}, s32[4,16]{1,0:T(4,128)}, u32[]{:S(2)}) copy-start(s32[4,16]{1,0:T(4,128)} %param.13) | copy-start | bytes 772
  24.4 24.6 %collective-permute-start.3 = (bf16[128,4096]{1,0:T(8,128)(2,1)}, bf16[128,4096]{1,0:T(8,128)(2,1)S(1)}, u32[]{:S(2)}, u32[]{:S(2)}) collective-permute-start(bf16[128,4096]{1,0:T(8,128)(2,1)} %get-tuple-element.100), channel_id=1, source_target_pairs={{0,4},{4,0},{1,5},{5,1},{2,6},{6,2},{3,7},{7,3},{8,12},{12,8},{9,1... | collective-permute-start | bytes 3145736 | tf_op jit(solution)/shard_map/ppermute | solution.py:625
  25.7 25.2 %collective-permute-start.4 = (bf16[128,4096]{1,0:T(8,128)(2,1)}, bf16[128,4096]{1,0:T(8,128)(2,1)S(1)}, u32[]{:S(2)}, u32[]{:S(2)}) collective-permute-start(bf16[128,4096]{1,0:T(8,128)(2,1)} %get-tuple-element.101), channel_id=1, source_target_pairs={{0,68},{4,64},{64,4},{68,0},{1,69},{5,65},{65,5},{69,1},{2,70},{6,... | collective-permute-start | bytes 3145736 | tf_op jit(solution)/shard_map/ppermute | solution.py:624
  28.2 24.9 %collective-permute-start.2 = (bf16[2,256,1024]{2,1,0:T(8,128)(2,1)}, bf16[2,256,1024]{2,1,0:T(8,128)(2,1)S(1)}, u32[]{:S(2)}, u32[]{:S(2)}) collective-permute-start(bf16[2,256,1024]{2,1,0:T(8,128)(2,1)} %get-tuple-element.99.refs_0_.own), channel_id=1, source_target_pairs={{0,1},{1,2},{2,3},{3,0},{4,5},{5,6},{6,7},{7,4},{8,9},{9,10},{10,1... | collective-permute-start | bytes 3145736 | tf_op jit(solution)/shard_map/ppermute | solution.py:628
  29.8 23.5 %collective-permute-start.1 = (bf16[2,256,1024]{2,1,0:T(8,128)(2,1)}, bf16[2,256,1024]{2,1,0:T(8,128)(2,1)}, u32[]{:S(2)}, u32[]{:S(2)}) collective-permute-start(bf16[2,256,1024]{2,1,0:T(8,128)(2,1)} %get-tuple-element.99.refs_0_.own), channel_id=1, source_target_pairs={{0,3},{1,0},{2,1},{3,2},{4,7},{5,4},{6,5},{7,6},{8,11},{9,8},{10,9... | collective-permute-start | bytes 3145736 | tf_op jit(solution)/shard_map/ppermute | solution.py:627
  54.3 32.3 %collective-permute-start.7 = (bf16[128,4096]{1,0:T(8,128)(2,1)}, bf16[128,4096]{1,0:T(8,128)(2,1)S(1)}, u32[]{:S(2)}, u32[]{:S(2)}) collective-permute-start(bf16[128,4096]{1,0:T(8,128)(2,1)} %get-tuple-element.117), channel_id=1, source_target_pairs={{0,4},{4,0},{1,5},{5,1},{2,6},{6,2},{3,7},{7,3},{8,12},{12,8},{9,1... | collective-permute-start | bytes 3145736 | tf_op jit(solution)/shard_map/ppermute | solution.py:625
  55.3 31.3 %collective-permute-start.8 = (bf16[128,4096]{1,0:T(8,128)(2,1)}, bf16[128,4096]{1,0:T(8,128)(2,1)S(1)}, u32[]{:S(2)}, u32[]{:S(2)}) collective-permute-start(bf16[128,4096]{1,0:T(8,128)(2,1)} %get-tuple-element.118), channel_id=1, source_target_pairs={{0,68},{4,64},{64,4},{68,0},{1,69},{5,65},{65,5},{69,1},{2,70},{6,... | collective-permute-start | bytes 3145736 | tf_op jit(solution)/shard_map/ppermute | solution.py:624
  56.2 30.5 %collective-permute-start.6 = (bf16[2,256,1024]{2,1,0:T(8,128)(2,1)}, bf16[2,256,1024]{2,1,0:T(8,128)(2,1)S(1)}, u32[]{:S(2)}, u32[]{:S(2)}) collective-permute-start(bf16[2,256,1024]{2,1,0:T(8,128)(2,1)} %get-tuple-element.114.refs_6_), channel_id=1, source_target_pairs={{0,3},{1,0},{2,1},{3,2},{4,7},{5,4},{6,5},{7,6},{8,11},{9,8},{10,9... | collective-permute-start | bytes 3145736 | tf_op jit(solution)/shard_map/ppermute | solution.py:639
  58.3 28.4 %collective-permute-start.5 = (bf16[2,256,1024]{2,1,0:T(8,128)(2,1)}, bf16[2,256,1024]{2,1,0:T(8,128)(2,1)}, u32[]{:S(2)}, u32[]{:S(2)}) collective-permute-start(bf16[2,256,1024]{2,1,0:T(8,128)(2,1)} %get-tuple-element.113.refs_1_.below), channel_id=1, source_target_pairs={{0,1},{1,2},{2,3},{3,0},{4,5},{5,6},{6,7},{7,4},{8,9},{9,10},{10,1... | collective-permute-start | bytes 3145736 | tf_op jit(solution)/shard_map/ppermute | solution.py:638
  69.3 2.6 %collective-permute-start.9 = (bf16[6,2,256,128]{3,2,1,0:T(8,128)(2,1)}, bf16[6,2,256,128]{3,2,1,0:T(8,128)(2,1)S(1)}, u32[]{:S(2)}, u32[]{:S(2)}) collective-permute-start(bf16[6,2,256,128]{3,2,1,0:T(8,128)(2,1)} %get-tuple-element.127), channel_id=1, source_target_pairs={{0,8},{8,0},{1,9},{9,1},{2,10},{10,2},{3,11},{11,3},{4,12},{12,4},... | collective-permute-start | bytes 2359304 | tf_op jit(solution)/shard_map/ppermute | solution.py:646
  88.3 2.9 %collective-permute-start.12 = (bf16[128,4096]{1,0:T(8,128)(2,1)}, bf16[128,4096]{1,0:T(8,128)(2,1)S(1)}, u32[]{:S(2)}, u32[]{:S(2)}) collective-permute-start(bf16[128,4096]{1,0:T(8,128)(2,1)} %get-tuple-element.139.refs_0_), channel_id=1, source_target_pairs={{0,8},{8,0},{1,9},{9,1},{2,10},{10,2},{3,11},{11,3},{4,12},{12,4},... | collective-permute-start | bytes 3145736 | tf_op jit(solution)/shard_map/ppermute | solution.py:661
  88.4 12.5 %collective-permute-start.13 = (bf16[128,4096]{1,0:T(8,128)(2,1)}, bf16[128,4096]{1,0:T(8,128)(2,1)S(1)}, u32[]{:S(2)}, u32[]{:S(2)}) collective-permute-start(bf16[128,4096]{1,0:T(8,128)(2,1)} %get-tuple-element.140.refs_1_), channel_id=1, source_target_pairs={{0,8},{8,0},{1,9},{9,1},{2,10},{10,2},{3,11},{11,3},{4,12},{12,4},... | collective-permute-start | bytes 3145736 | tf_op jit(solution)/shard_map/ppermute | solution.py:661
  88.8 12.2 %collective-permute-start.14 = (bf16[128,4096]{1,0:T(8,128)(2,1)}, bf16[128,4096]{1,0:T(8,128)(2,1)S(1)}, u32[]{:S(2)}, u32[]{:S(2)}) collective-permute-start(bf16[128,4096]{1,0:T(8,128)(2,1)} %get-tuple-element.141.refs_2_), channel_id=1, source_target_pairs={{0,8},{8,0},{1,9},{9,1},{2,10},{10,2},{3,11},{11,3},{4,12},{12,4},... | collective-permute-start | bytes 3145736 | tf_op jit(solution)/shard_map/ppermute | solution.py:661
  88.9 12.0 %collective-permute-start.15 = (bf16[128,4096]{1,0:T(8,128)(2,1)}, bf16[128,4096]{1,0:T(8,128)(2,1)}, u32[]{:S(2)}, u32[]{:S(2)}) collective-permute-start(bf16[128,4096]{1,0:T(8,128)(2,1)} %get-tuple-element.142.refs_3_), channel_id=1, source_target_pairs={{0,8},{8,0},{1,9},{9,1},{2,10},{10,2},{3,11},{11,3},{4,12},{12,4},... | collective-permute-start | bytes 3145736 | tf_op jit(solution)/shard_map/ppermute | solution.py:661
  89.3 26.9 %collective-permute-start.10 = (bf16[2,256,1024]{2,1,0:T(8,128)(2,1)}, bf16[2,256,1024]{2,1,0:T(8,128)(2,1)S(1)}, u32[]{:S(2)}, u32[]{:S(2)}) collective-permute-start(bf16[2,256,1024]{2,1,0:T(8,128)(2,1)} %get-tuple-element.131.own), channel_id=1, source_target_pairs={{0,1},{1,2},{2,3},{3,0},{4,5},{5,6},{6,7},{7,4},{8,9},{9,10},{10,1... | collective-permute-start | bytes 3145736 | tf_op jit(solution)/shard_map/ppermute | solution.py:657
  91.1 26.3 %collective-permute-start.11 = (bf16[2,256,1024]{2,1,0:T(8,128)(2,1)}, bf16[2,256,1024]{2,1,0:T(8,128)(2,1)S(1)}, u32[]{:S(2)}, u32[]{:S(2)}) collective-permute-start(bf16[2,256,1024]{2,1,0:T(8,128)(2,1)} %get-tuple-element.130.above.refs_0_), channel_id=1, source_target_pairs={{0,3},{1,0},{2,1},{3,2},{4,7},{5,4},{6,5},{7,6},{8,11},{9,8},{10,9... | collective-permute-start | bytes 3145736 | tf_op jit(solution)/shard_map/ppermute | solution.py:658
  101.0 16.4 %copy-start.2 = (bf16[2,256,1024]{2,1,0:T(8,128)(2,1)S(1)}, bf16[2,256,1024]{2,1,0:T(8,128)(2,1)}, u32[]{:S(2)}) copy-start(bf16[2,256,1024]{2,1,0:T(8,128)(2,1)} %get-tuple-element.131.own) | copy-start | bytes 3145732
  101.0 16.4 %copy-start.15 = (bf16[2,256,1024]{2,1,0:T(8,128)(2,1)S(1)}, bf16[2,256,1024]{2,1,0:T(8,128)(2,1)}, u32[]{:S(2)}) copy-start(bf16[2,256,1024]{2,1,0:T(8,128)(2,1)} %get-tuple-element.130.above.refs_0_) | copy-start | bytes 3145732
  108.9 16.0 %collective-permute-start.17 = (bf16[8,256,128]{2,1,0:T(8,128)(2,1)S(1)}, bf16[8,256,128]{2,1,0:T(8,128)(2,1)S(1)}, u32[]{:S(2)}, u32[]{:S(2)}) collective-permute-start(bf16[8,256,128]{2,1,0:T(8,128)(2,1)S(1)} %get-tuple-element.148), channel_id=1, source_target_pairs={{0,4},{4,0},{1,5},{5,1},{2,6},{6,2},{3,7},{7,3},{8,12},{12,8},{9,1... | collective-permute-start | bytes 1572872 | tf_op jit(solution)/shard_map/ppermute | solution.py:667
  110.0 23.9 %collective-permute-start.16 = (bf16[8,256,128]{2,1,0:T(8,128)(2,1)S(1)}, bf16[8,256,128]{2,1,0:T(8,128)(2,1)S(1)}, u32[]{:S(2)}, u32[]{:S(2)}) collective-permute-start(bf16[8,256,128]{2,1,0:T(8,128)(2,1)S(1)} %get-tuple-element.144), channel_id=1, source_target_pairs={{0,4},{4,0},{1,5},{5,1},{2,6},{6,2},{3,7},{7,3},{8,12},{12,8},{9,1... | collective-permute-start | bytes 1572872 | tf_op jit(solution)/shard_map/ppermute | solution.py:667
  117.4 7.6 %copy-start.7 = (bf16[6,2,256,128]{3,2,1,0:T(8,128)(2,1)S(1)}, bf16[6,2,256,128]{3,2,1,0:T(8,128)(2,1)}, u32[]{:S(2)}) copy-start(bf16[6,2,256,128]{3,2,1,0:T(8,128)(2,1)} %get-tuple-element.145.refs_0_) | copy-start | bytes 2359300
  117.4 7.6 %copy-start.8 = (bf16[4,1,256,128]{3,2,1,0:T(8,128)(2,1)S(1)}, bf16[4,1,256,128]{3,2,1,0:T(8,128)(2,1)}, u32[]{:S(2)}) copy-start(bf16[4,1,256,128]{3,2,1,0:T(8,128)(2,1)} %own_value.11) | copy-start | bytes 786436
  117.4 7.6 %copy-start.9 = (bf16[4,1,256,128]{3,2,1,0:T(8,128)(2,1)S(1)}, bf16[4,1,256,128]{3,2,1,0:T(8,128)(2,1)}, u32[]{:S(2)}) copy-start(bf16[4,1,256,128]{3,2,1,0:T(8,128)(2,1)} %own_key.11) | copy-start | bytes 786436
  117.4 7.6 %copy-start.19 = (bf16[2,1024,1024]{2,1,0:T(8,128)(2,1)S(1)}, bf16[2,1024,1024]{2,1,0:T(8,128)(2,1)}, u32[]{:S(2)}) copy-start(bf16[2,1024,1024]{2,1,0:T(8,128)(2,1)} %get-tuple-element.146.probs_ref) | copy-start | bytes 12582916
  117.4 7.6 %copy-start.24 = (f32[128,2048]{1,0:T(8,128)S(1)}, f32[128,2048]{1,0:T(8,128)}, u32[]{:S(2)}) copy-start(f32[128,2048]{1,0:T(8,128)} %get-tuple-element.147.average) | copy-start | bytes 3145732
  117.5 7.6 %copy-start.27 = (f32[8,2048]{1,0:T(8,128)S(1)}, f32[8,2048]{1,0:T(8,128)}, u32[]{:S(2)}) copy-start(f32[8,2048]{1,0:T(8,128)} %get-tuple-element.135.inverse) | copy-start | bytes 196612
  125.1 8.9 %copy-start.21 = (bf16[2,768,1024]{2,1,0:T(8,128)(2,1)S(1)}, bf16[2,768,1024]{2,1,0:T(8,128)(2,1)}, u32[]{:S(2)}) copy-start(bf16[2,768,1024]{2,1,0:T(8,128)(2,1)} %get-tuple-element.133.probs_ref) | copy-start | bytes 9437188
  125.1 8.9 %copy-start.26 = (f32[128,2048]{1,0:T(8,128)S(1)}, f32[128,2048]{1,0:T(8,128)}, u32[]{:S(2)}) copy-start(f32[128,2048]{1,0:T(8,128)} %get-tuple-element.134.average) | copy-start | bytes 3145732
  131.3 9.9 %collective-permute-start.19 = (bf16[3,2,256,128]{3,2,1,0:T(8,128)(2,1)S(1)}, bf16[3,2,256,128]{3,2,1,0:T(8,128)(2,1)S(1)}, u32[]{:S(2)}, u32[]{:S(2)}) collective-permute-start(bf16[3,2,256,128]{3,2,1,0:T(8,128)(2,1)S(1)} %get-tuple-element.153.refs_2_.refs_4_), channel_id=1, source_target_pairs={{0,8},{8,0},{1,9},{9,1},{2,10},{10,2},{3,11},{11,3},{4,12},{12,4},... | collective-permute-start | bytes 1179656 | tf_op jit(solution)/shard_map/ppermute | solution.py:686
  139.2 2.0 %collective-permute-start.18 = (bf16[2,2,256,128]{3,2,1,0:T(8,128)(2,1)S(1)}, bf16[2,2,256,128]{3,2,1,0:T(8,128)(2,1)S(1)}, u32[]{:S(2)}, u32[]{:S(2)}) collective-permute-start(bf16[2,2,256,128]{3,2,1,0:T(8,128)(2,1)S(1)} %get-tuple-element.152.refs_0_.refs_2_), channel_id=1, source_target_pairs={{0,8},{8,0},{1,9},{9,1},{2,10},{10,2},{3,11},{11,3},{4,12},{12,4},... | collective-permute-start | bytes 786440 | tf_op jit(solution)/shard_map/ppermute | solution.py:686
  139.2 16.6 %collective-permute-start.21 = (bf16[8,256,128]{2,1,0:T(8,128)(2,1)}, bf16[8,256,128]{2,1,0:T(8,128)(2,1)S(1)}, u32[]{:S(2)}, u32[]{:S(2)}) collective-permute-start(bf16[8,256,128]{2,1,0:T(8,128)(2,1)} %get-tuple-element.160), channel_id=1, source_target_pairs={{0,4},{4,0},{1,5},{5,1},{2,6},{6,2},{3,7},{7,3},{8,12},{12,8},{9,1... | collective-permute-start | bytes 1572872 | tf_op jit(solution)/shard_map/ppermute | solution.py:667
  140.2 24.8 %collective-permute-start.20 = (bf16[8,256,128]{2,1,0:T(8,128)(2,1)}, bf16[8,256,128]{2,1,0:T(8,128)(2,1)S(1)}, u32[]{:S(2)}, u32[]{:S(2)}) collective-permute-start(bf16[8,256,128]{2,1,0:T(8,128)(2,1)} %get-tuple-element.157), channel_id=1, source_target_pairs={{0,4},{4,0},{1,5},{5,1},{2,6},{6,2},{3,7},{7,3},{8,12},{12,8},{9,1... | collective-permute-start | bytes 1572872 | tf_op jit(solution)/shard_map/ppermute | solution.py:667
  143.4 24.4 %collective-permute-start.23 = (bf16[2,2,2,256,128]{4,3,2,1,0:T(8,128)(2,1)}, bf16[2,2,2,256,128]{4,3,2,1,0:T(8,128)(2,1)S(1)}, u32[]{:S(2)}, u32[]{:S(2)}) collective-permute-start(bf16[2,2,2,256,128]{4,3,2,1,0:T(8,128)(2,1)} %get-tuple-element.171), channel_id=1, source_target_pairs={{0,16},{16,32},{32,48},{48,0},{1,17},{17,33},{33,49},{49,1},{2,18}... | collective-permute-start | bytes 1572872 | tf_op jit(solution)/shard_map/ppermute | solution.py:698
  144.9 26.9 %collective-permute-start.24 = (bf16[2,2,2,256,128]{4,3,2,1,0:T(8,128)(2,1)}, bf16[2,2,2,256,128]{4,3,2,1,0:T(8,128)(2,1)S(1)}, u32[]{:S(2)}, u32[]{:S(2)}) collective-permute-start(bf16[2,2,2,256,128]{4,3,2,1,0:T(8,128)(2,1)} %get-tuple-element.172), channel_id=1, source_target_pairs={{0,48},{16,0},{32,16},{48,32},{1,49},{17,1},{33,17},{49,33},{2,50}... | collective-permute-start | bytes 1572872 | tf_op jit(solution)/shard_map/ppermute | solution.py:699
  146.6 25.3 %collective-permute-start.25 = (bf16[2,2,2,256,128]{4,3,2,1,0:T(8,128)(2,1)}, bf16[2,2,2,256,128]{4,3,2,1,0:T(8,128)(2,1)S(1)}, u32[]{:S(2)}, u32[]{:S(2)}) collective-permute-start(bf16[2,2,2,256,128]{4,3,2,1,0:T(8,128)(2,1)} %get-tuple-element.173), channel_id=1, source_target_pairs={{0,32},{16,48},{32,0},{48,16},{1,33},{17,49},{33,1},{49,17},{2,34}... | collective-permute-start | bytes 1572872 | tf_op jit(solution)/shard_map/ppermute | solution.py:700
  155.8 12.8 %copy-start.25 = (f32[128,2048]{1,0:T(8,128)S(1)}, f32[128,2048]{1,0:T(8,128)}, u32[]{:S(2)}) copy-start(f32[128,2048]{1,0:T(8,128)} %get-tuple-element.111.average) | copy-start | bytes 3145732
  155.8 12.8 %copy-start.29 = (f32[8,2048]{1,0:T(8,128)S(1)}, f32[8,2048]{1,0:T(8,128)}, u32[]{:S(2)}) copy-start(f32[8,2048]{1,0:T(8,128)} %get-tuple-element.112.inverse) | copy-start | bytes 196612
  160.0 8.6 %copy-start.20 = (bf16[2,256,1024]{2,1,0:T(8,128)(2,1)S(1)}, bf16[2,256,1024]{2,1,0:T(8,128)(2,1)}, u32[]{:S(2)}) copy-start(bf16[2,256,1024]{2,1,0:T(8,128)(2,1)} %get-tuple-element.110.probs_ref) | copy-start | bytes 3145732
  160.0 1.3 collective-permute-start.22
  162.7 14.7 %collective-permute-start.27 = (bf16[1,2,2,256,128]{4,3,2,1,0:T(8,128)(2,1)S(1)}, bf16[1,2,2,256,128]{4,3,2,1,0:T(8,128)(2,1)S(1)}, u32[]{:S(2)}, u32[]{:S(2)}) collective-permute-start(bf16[1,2,2,256,128]{4,3,2,1,0:T(8,128)(2,1)S(1)} %get-tuple-element.177), channel_id=1, source_target_pairs={{0,16},{16,32},{32,48},{48,0},{1,17},{17,33},{33,49},{49,1},{2,18}... | collective-permute-start | bytes 786440 | tf_op jit(solution)/shard_map/ppermute | solution.py:698
  165.0 12.5 %collective-permute-start.28 = (bf16[1,2,2,256,128]{4,3,2,1,0:T(8,128)(2,1)S(1)}, bf16[1,2,2,256,128]{4,3,2,1,0:T(8,128)(2,1)S(1)}, u32[]{:S(2)}, u32[]{:S(2)}) collective-permute-start(bf16[1,2,2,256,128]{4,3,2,1,0:T(8,128)(2,1)S(1)} %get-tuple-element.178), channel_id=1, source_target_pairs={{0,48},{16,0},{32,16},{48,32},{1,49},{17,1},{33,17},{49,33},{2,50}... | collective-permute-start | bytes 786440 | tf_op jit(solution)/shard_map/ppermute | solution.py:699
  167.8 14.3 %collective-permute-start.29 = (bf16[1,2,2,256,128]{4,3,2,1,0:T(8,128)(2,1)S(1)}, bf16[1,2,2,256,128]{4,3,2,1,0:T(8,128)(2,1)S(1)}, u32[]{:S(2)}, u32[]{:S(2)}) collective-permute-start(bf16[1,2,2,256,128]{4,3,2,1,0:T(8,128)(2,1)S(1)} %get-tuple-element.179), channel_id=1, source_target_pairs={{0,32},{16,48},{32,0},{48,16},{1,33},{17,49},{33,1},{49,17},{2,34}... | collective-permute-start | bytes 786440 | tf_op jit(solution)/shard_map/ppermute | solution.py:700
  172.7 17.1 %collective-permute-start.26 = (bf16[2,2,256,128]{3,2,1,0:T(8,128)(2,1)S(1)}, bf16[2,2,256,128]{3,2,1,0:T(8,128)(2,1)S(1)}, u32[]{:S(2)}, u32[]{:S(2)}) collective-permute-start(bf16[2,2,256,128]{3,2,1,0:T(8,128)(2,1)S(1)} %get-tuple-element.175), channel_id=1, source_target_pairs={{0,64},{64,0},{1,65},{65,1},{2,66},{66,2},{3,67},{67,3},{4,68},{68... | collective-permute-start | bytes 786440 | tf_op jit(solution)/shard_map/ppermute | solution.py:712
  183.3 6.5 %collective-permute-start.30 = (bf16[1,2,256,128]{3,2,1,0:T(8,128)(2,1)S(1)}, bf16[1,2,256,128]{3,2,1,0:T(8,128)(2,1)S(1)}, u32[]{:S(2)}, u32[]{:S(2)}) collective-permute-start(bf16[1,2,256,128]{3,2,1,0:T(8,128)(2,1)S(1)} %get-tuple-element.182), channel_id=1, source_target_pairs={{0,64},{64,0},{1,65},{65,1},{2,66},{66,2},{3,67},{67,3},{4,68},{68... | collective-permute-start | bytes 393224 | tf_op jit(solution)/shard_map/ppermute | solution.py:714
  (21 other events, 88.5 us)
Sparse Core Ops, SparseCore 0:
  24.5 41.2 all-gather.2
